TPU v7x, 32 devices: a whole 2x2x4 slice. The times are simulated.
32 devices in a mesh: dp: 4 (over x, core), seq: 8 (over z, y).
Axes of the slice: x: 2, y: 2, z: 4, core: 2. Of those that a mesh axis runs over, the one named last changes fastest.
Arguments:
- tokens: bfloat16 [4, 1024, 1536], P('dp', 'seq'), may hold values from -6 to 6
- upstream: bfloat16 [4, 1024, 1536], P('dp', 'seq'), may hold values from -6 to 6
- conv_value: float32 [3, 1536], replicated, may hold values from -3.5 to 3.5
- conv_gate: float32 [3, 1536], replicated, may hold values from -3.5 to 3.5
- mix_one: bfloat16 [2, 8, 128, 128], P(None, 'seq'), may hold values from -0.375 to 0.375
- mix_two: bfloat16 [2, 128, 8, 8], P(None, 'seq'), may hold values from -1.5 to 1.5
- mix_three: bfloat16 [2, 128, 8, 8], P(None, 'seq'), may hold values from -1.5 to 1.5
- mix_four: bfloat16 [2, 8, 128, 128], P(None, 'seq'), may hold values from -0.375 to 0.375
- filter_log: bfloat16 [128, 8, 1536], P('seq'), may hold values from -2.5 to 2.5
Outputs:
- grad_x: bfloat16 [4, 1024, 1536], P('dp', 'seq')
- grad_conv_value: float32 [3, 1536], replicated
- grad_conv_gate: float32 [3, 1536], replicated
- grad_mix_one: bfloat16 [2, 8, 128, 128], P(None, 'seq')
- grad_mix_two: bfloat16 [2, 128, 8, 8], P(None, 'seq')
- grad_mix_three: bfloat16 [2, 128, 8, 8], P(None, 'seq')
- grad_mix_four: bfloat16 [2, 8, 128, 128], P(None, 'seq')
- grad_filter: bfloat16 [128, 8, 1536], P('seq')
All inputs are finite; a program needn't handle non-finite values.
Results may differ from a plain program's by a relative error of at most 0.018.
Values may be sent and summed in bfloat16 or wider, within the bound.
No kernel may reach another device: no remote copies, remote signals or barrier semaphores. Data moves between devices by JAX's collectives and lax.ppermute only.
A program may use at most 64 MiB of HBM per device.

v0:
```python
import jax
import jax.numpy as jnp
from jax import lax
from jax.sharding import PartitionSpec as P

C = 1536
BLK = 128


def with_halo(cells, sides, width):
    for axis, dim in sides:
        count = lax.axis_size(axis)
        ends = count - 1
        head = lax.slice_in_dim(cells, 0, width, axis=dim)
        tail = lax.slice_in_dim(cells, cells.shape[dim] - width, cells.shape[dim], axis=dim)
        cells = jnp.concatenate(
            [
                lax.ppermute(tail, axis, [(i, (i + 1) % count) for i in range(ends)]),
                cells,
                lax.ppermute(head, axis, [((i + 1) % count, i) for i in range(ends)]),
            ],
            axis=dim,
        )
    return cells


def complex_stack(factor, conjugate):
    real_part = factor[0]
    imag_part = factor[1]
    if conjugate:
        return jnp.stack([jnp.stack([real_part, imag_part]), jnp.stack([-imag_part, real_part])])
    return jnp.stack([jnp.stack([real_part, -imag_part]), jnp.stack([imag_part, real_part])])


def shortconv(padded, weights):
    length = padded.shape[0] - 2
    return (
        weights[0] * padded[0:length]
        + weights[1] * padded[1 : length + 1]
        + weights[2] * padded[2 : length + 2]
    )


def edge_apply(edged, weights):
    return weights[0] * edged[2:] + weights[1] * edged[1:-1] + weights[2] * edged[:-2]


def conv_grad(grad, padded):
    length = grad.shape[0]
    return jnp.stack(
        [jnp.sum(grad * padded[offset : offset + length], axis=0) for offset in range(3)]
    )


def shards(
    tokens, upstream, conv_value, conv_gate, mix_one, mix_two, mix_three, mix_four, filter_log
):
    local_tokens = tokens[0]
    length = local_tokens.shape[0]
    blocks_here = length // BLK
    stacked_two = complex_stack(mix_two, False)
    stacked_two_conj = complex_stack(mix_two, True)
    stacked_three = complex_stack(mix_three, False)
    stacked_three_conj = complex_stack(mix_three, True)
    signed_four = jnp.stack([mix_four[0], -mix_four[1]])
    padded = with_halo(local_tokens, (("seq", 0),), 1).astype(jnp.float32)
    values = shortconv(padded, conv_value).astype(jnp.bfloat16)
    gating = shortconv(padded, conv_gate).astype(jnp.bfloat16)
    value_blocks = values.reshape(blocks_here, BLK, C)
    first = jnp.einsum(
        "pikj,ijc->pikc", mix_one, value_blocks, preferred_element_type=jnp.float32
    ).astype(jnp.bfloat16)
    first_freq = lax.all_to_all(first, "seq", split_axis=2, concat_axis=1, tiled=True)
    second = jnp.einsum(
        "pqkmi,qikc->pkmc", stacked_two, first_freq, preferred_element_type=jnp.float32
    )
    filt = jnp.exp(filter_log.astype(jnp.float32))
    weighted = (filt * second).astype(jnp.bfloat16)
    third = jnp.einsum(
        "pqknm,qkmc->pknc", stacked_three, weighted, preferred_element_type=jnp.float32
    ).astype(jnp.bfloat16)
    third_time = lax.all_to_all(third, "seq", split_axis=2, concat_axis=1, tiled=True)
    mixed_out = jnp.einsum(
        "pnqk,pknc->nqc", signed_four, third_time, preferred_element_type=jnp.float32
    ).reshape(length, C)
    upstream_f = upstream[0].astype(jnp.float32)
    mix_grad = (upstream_f * gating.astype(jnp.float32)).astype(jnp.bfloat16)
    gate_grad = upstream_f * mixed_out
    mix_blocks = mix_grad.reshape(blocks_here, BLK, C)
    third_grad = jnp.einsum(
        "pnqk,nqc->pknc", signed_four, mix_blocks, preferred_element_type=jnp.float32
    ).astype(jnp.bfloat16)
    products = jnp.einsum(
        "nqc,pknc->pnqk", mix_blocks, third_time, preferred_element_type=jnp.float32
    )
    grad_four = jnp.stack([products[0], -products[1]])
    third_grad_freq = lax.all_to_all(third_grad, "seq", split_axis=1, concat_axis=2, tiled=True)
    weighted_grad = jnp.einsum(
        "pqknm,qknc->pkmc", stacked_three_conj, third_grad_freq, preferred_element_type=jnp.float32
    )
    products = jnp.einsum(
        "qknc,pkmc->qpknm", third_grad_freq, weighted, preferred_element_type=jnp.float32
    )
    grad_three = jnp.stack([products[0, 0] + products[1, 1], products[1, 0] - products[0, 1]])
    filter_term = weighted_grad[0] * second[0] + weighted_grad[1] * second[1]
    filter_part = lax.psum_scatter(filter_term, "dp", scatter_dimension=2, tiled=True)
    share_width = filter_part.shape[2]
    filt_share = lax.dynamic_slice_in_dim(filt, lax.axis_index("dp") * share_width, share_width, 2)
    finished = (filt_share * filter_part).astype(jnp.bfloat16)
    grad_filter = lax.all_gather(finished, "dp", axis=2, tiled=True)
    second_grad = (filt * weighted_grad).astype(jnp.bfloat16)
    first_grad = jnp.einsum(
        "pqkmi,qkmc->pikc", stacked_two_conj, second_grad, preferred_element_type=jnp.float32
    ).astype(jnp.bfloat16)
    products = jnp.einsum(
        "qkmc,pikc->qpkmi", second_grad, first_freq, preferred_element_type=jnp.float32
    )
    grad_two = jnp.stack([products[0, 0] + products[1, 1], products[1, 0] - products[0, 1]])
    first_grad_time = lax.all_to_all(first_grad, "seq", split_axis=1, concat_axis=2, tiled=True)
    value_grad = jnp.einsum(
        "pikj,pikc->ijc", mix_one, first_grad_time, preferred_element_type=jnp.float32
    ).reshape(length, C)
    grad_one = jnp.einsum(
        "pikc,ijc->pikj", first_grad_time, value_blocks, preferred_element_type=jnp.float32
    )
    edged = with_halo(jnp.stack([value_grad, gate_grad]), (("seq", 1),), 1)
    token_grad = (edge_apply(edged[0], conv_value) + edge_apply(edged[1], conv_gate)).astype(
        jnp.bfloat16
    )
    conv_value_grad, conv_gate_grad = lax.psum(
        (conv_grad(value_grad, padded), conv_grad(gate_grad, padded)), ("dp", "seq")
    )
    grad_one, grad_two, grad_three, grad_four = lax.psum(
        (grad_one, grad_two, grad_three, grad_four), "dp"
    )
    return (
        token_grad[None],
        conv_value_grad,
        conv_gate_grad,
        grad_one.astype(jnp.bfloat16),
        grad_two.astype(jnp.bfloat16),
        grad_three.astype(jnp.bfloat16),
        grad_four.astype(jnp.bfloat16),
        grad_filter,
    )


def solution(mesh):
    return jax.shard_map(
        shards,
        mesh=mesh,
        in_specs=(
            P("dp", "seq", None),
            P("dp", "seq", None),
            P(),
            P(),
            P(None, "seq", None, None),
            P(None, "seq", None, None),
            P(None, "seq", None, None),
            P(None, "seq", None, None),
            P("seq", None, None),
        ),
        out_specs=(
            P("dp", "seq", None),
            P(),
            P(),
            P(None, "seq", None, None),
            P(None, "seq", None, None),
            P(None, "seq", None, None),
            P(None, "seq", None, None),
            P("seq", None, None),
        ),
        check_vma=False,
    )
```

profile of v0, /device:TPU:0, one launch (start us, length us, event | category | flops | bytes accessed | tf_op | source)
XLA Modules:
  0.0 203.9 jit_solution(13383383508430073012)
XLA Ops:
  7.2 0.0 copy-start
  7.2 0.8 slice_bitcast_fusion.5
  8.0 4.9 %collective-permute-start = (bf16[1,1536]{1,0:T(2,128)(2,1)S(1)}, bf16[1,1536]{1,0:T(2,128)(2,1)S(1)}, u32[]{:S(2)}, u32[]{:S(2)}) collective-permute-start(bf16[1,1536]{1,0:T(2,128)(2,1)S(1)} %get-tuple-element.57), channel_id=1, source_target_pairs={{0,1},{1,2},{2,3},{3,4},{4,5},{5,6},{6,7},{8,9},{9,10},{10,11},{11... | collective-permute-start | bytes 9224 | tf_op jit(solution)/shard_map/ppermute | solution.py:18
  12.9 1.3 collective-permute-start.1
  14.2 0.8 fusion.63
  15.0 1.0 slice_reduce_fusion.4
  16.0 2.4 %collective-permute-done.1 = bf16[1,1536]{1,0:T(2,128)(2,1)S(1)} collective-permute-done((bf16[1,1536]{1,0:T(2,128)(2,1)S(1)}, bf16[1,1536]{1,0:T(2,128)(2,1)S(1)}, u32[]{:S(2)}, u32[]{:S(2)}) %collective-permute-start.1) | collective-permute-done | bytes 3104 | tf_op jit(solution)/shard_map/ppermute | solution.py:20
  18.4 1.1 maximum_convert_fusion
  19.5 0.4 fusion.8
  20.1 0.0 copy-start.4
  20.1 0.0 copy-start.6
  20.1 0.4 fusion.2
  20.5 1.8 copy.72
  22.4 5.7 %all-to-all-start = ((bf16[2,128,1,1536]{3,0,2,1:T(2,128)(2,1)}), bf16[2,128,1,1536]{3,0,2,1:T(2,128)(2,1)S(1)}, u32[]{:S(2)}, u32[]{:S(2)}) async-start(bf16[2,128,1,1536]{3,0,2,1:T(2,128)(2,1)} %copy.72), calls=%async_computation | async-start | bytes 1572864 | tf_op jit(solution)/shard_map/all_to_all | solution.py:97
  28.1 0.1 copy.78
  28.2 0.1 copy.75
  28.4 0.4 fusion.3
  28.8 1.9 copy.85
  30.7 16.2 %all-to-all-done = bf16[2,128,1,1536]{3,0,2,1:T(2,128)(2,1)S(1)} async-done(((bf16[2,128,1,1536]{3,0,2,1:T(2,128)(2,1)}), bf16[2,128,1,1536]{3,0,2,1:T(2,128)(2,1)S(1)}, u32[]{:S(2)}, u32[]{:S(2)}) %all-to-all-start) | async-done | bytes 786464 | tf_op jit(solution)/shard_map/all_to_all | solution.py:97
  46.9 4.2 %all-to-all-start.2 = ((bf16[2,1,128,1536]{3,0,1,2:T(2,128)(2,1)}), bf16[2,1,128,1536]{3,0,1,2:T(2,128)(2,1)}, u32[]{:S(2)}, u32[]{:S(2)}) async-start(bf16[2,1,128,1536]{3,0,1,2:T(2,128)(2,1)} %copy.85), calls=%async_computation.2 | async-start | bytes 1572864 | tf_op jit(solution)/shard_map/all_to_all | solution.py:73
  51.2 0.7 fusion.42
  51.9 0.1 convert_exponential_fusion
  52.0 1.7 convolution_bitcast_fusion.3
  53.7 0.4 fusion.5
  54.1 1.5 copy.81
  55.6 14.7 %all-to-all-done.2 = bf16[2,1,128,1536]{3,0,1,2:T(2,128)(2,1)} async-done(((bf16[2,1,128,1536]{3,0,1,2:T(2,128)(2,1)}), bf16[2,1,128,1536]{3,0,1,2:T(2,128)(2,1)}, u32[]{:S(2)}, u32[]{:S(2)}) %all-to-all-start.2) | async-done | bytes 786464 | tf_op jit(solution)/shard_map/all_to_all | solution.py:73
  70.3 4.2 %all-to-all-start.1 = ((bf16[2,8,16,1536]{3,0,2,1:T(2,128)(2,1)}), bf16[2,8,16,1536]{3,0,2,1:T(2,128)(2,1)}, u32[]{:S(2)}, u32[]{:S(2)}) async-start(bf16[2,8,16,1536]{3,0,2,1:T(2,128)(2,1)} %copy.81), calls=%async_computation.1 | async-start | bytes 1572864 | tf_op jit(solution)/shard_map/all_to_all | solution.py:119
  74.5 1.2 copy.86
  75.7 0.7 convolution_bitcast_fusion.1
  76.4 0.4 fusion.4
  76.9 1.5 copy.90
  78.4 1.9 convolution_bitcast_fusion.4
  80.3 0.7 fusion.46
  80.9 0.6 fusion.48
  81.5 1.9 convolution_bitcast_fusion.5
  83.4 0.7 fusion.49
  84.1 10.1 %all-to-all-done.1 = bf16[2,8,16,1536]{3,0,2,1:T(2,128)(2,1)} async-done(((bf16[2,8,16,1536]{3,0,2,1:T(2,128)(2,1)}), bf16[2,8,16,1536]{3,0,2,1:T(2,128)(2,1)}, u32[]{:S(2)}, u32[]{:S(2)}) %all-to-all-start.1) | async-done | bytes 786464 | tf_op jit(solution)/shard_map/all_to_all | solution.py:119
  94.2 4.2 %all-to-all-start.3 = ((bf16[2,16,8,1536]{3,0,1,2:T(2,128)(2,1)}), bf16[2,16,8,1536]{3,0,1,2:T(2,128)(2,1)}, u32[]{:S(2)}, u32[]{:S(2)}) async-start(bf16[2,16,8,1536]{3,0,1,2:T(2,128)(2,1)} %copy.90), calls=%async_computation.3 | async-start | bytes 1572864 | tf_op jit(solution)/shard_map/all_to_all | solution.py:82
  98.4 0.0 reduce-scatter.2.cloned.1.call-start
  98.4 1.5 pad_maximum_fusion.7
  100.0 0.9 pad_maximum_fusion.6
  100.9 2.5 %fusion.11 = f32[16,8,1536]{2,1,0:T(8,128)} fusion(f32[2,16,8,1536]{3,2,0,1:T(8,128)} %copy-done.1, f32[2,16,8,1536]{3,2,0,1:T(8,128)S(1)} %convolution_bitcast_fusion.3), kind=kLoop, calls=%fused_computation.26 | loop fusion | flops 589824 | bytes 3932160 | tf_op jit(solution)/shard_map/add | solution.py:105
  103.3 0.0 reduce-scatter.2.cloned.1.call-update
  103.4 1.3 copy.82
  104.7 0.4 convolution_bitcast_fusion.7
  105.1 0.3 fusion.53
  105.4 12.8 %all-to-all-done.3 = bf16[2,16,8,1536]{3,0,1,2:T(2,128)(2,1)} async-done(((bf16[2,16,8,1536]{3,0,1,2:T(2,128)(2,1)}), bf16[2,16,8,1536]{3,0,1,2:T(2,128)(2,1)}, u32[]{:S(2)}, u32[]{:S(2)}) %all-to-all-start.3) | async-done | bytes 786464 | tf_op jit(solution)/shard_map/all_to_all | solution.py:82
  118.2 1.3 copy.91
  119.5 0.4 convolution_bitcast_fusion.6
  119.9 0.3 convert_multiply_fusion
  120.2 0.7 pad_maximum_fusion.8
  120.9 0.5 multiply_reduce_fusion.2
  121.6 1.4 collective-permute-start.2
  123.0 4.5 %collective-permute-start.3 = (f32[2,1,1536]{2,1,0:T(1,128)S(1)}, f32[2,1,1536]{2,1,0:T(1,128)S(1)}, u32[]{:S(2)}, u32[]{:S(2)}) collective-permute-start(f32[2,1,1536]{2,1,0:T(1,128)S(1)} %get-tuple-element.54), channel_id=1, source_target_pairs={{0,1},{1,2},{2,3},{3,4},{4,5},{5,6},{6,7},{8,9},{9,10},{10,11},{11... | collective-permute-start | bytes 36872 | tf_op jit(solution)/shard_map/ppermute | solution.py:18
  127.7 16.6 %all-reduce.3 = (bf16[2,1,128,128]{2,3,0,1:T(8,128)(2,1)S(1)}, bf16[2,16,8,8]{2,3,1,0:T(8,128)(2,1)S(1)}, bf16[2,16,8,8]{2,3,1,0:T(8,128)(2,1)S(1)}, bf16[2,1,128,128]{2,3,0,1:T(8,128)(2,1)S(1)}) all-reduce(f32[2,1,128,128]{2,3,0,1:T(8,128)S(1)} %convolution_bitcast_fusion.7, ...), channel_id=1, replica_groups=mesh['dp'=4,'seq'=8] {'dp'}, use_global_device_ids=true, to_apply=%region_8.0 | all-reduce | flops 69632 | bytes 417792 | tf_op jit(solution)/shard_map/psum | solution.py:133
  144.3 0.7 copy.97
  145.0 0.7 copy.98
  145.7 0.7 copy.99
  146.5 0.7 copy.100
  147.2 39.5 %all-reduce = (f32[3,1536]{1,0:T(4,128)}, f32[3,1536]{1,0:T(4,128)}) all-reduce(f32[3,1536]{1,0:T(4,128)S(1)} %pad_maximum_fusion.13, f32[3,1536]{1,0:T(4,128)S(1)} %pad_maximum_fusion.14), channel_id=1, replica_groups=mesh['dp'=4,'seq'=8] {'dp','seq'}, use_global_device_ids=true, to_apply=%region_3.0 | all-reduce | flops 9216 | bytes 73728 | tf_op jit(solution)/shard_map/psum | solution.py:130
  186.8 1.3 fusion.15
  188.1 0.9 multiply_convert_fusion.2
  189.0 7.2 %all_gather.3 = bf16[16,8,1536]{2,1,0:T(8,128)(2,1)S(1)} all-gather(bf16[16,8,384]{2,1,0:T(8,128)(2,1)S(1)} %multiply_convert_fusion.2), channel_id=1, replica_groups=mesh['dp'=4,'seq'=8] {'dp'}, dimensions={2}, use_global_device_ids=true | all-gather | bytes 491520 | tf_op jit(solution)/shard_map/all_gather | solution.py:110
  196.3 0.7 copy.155
  (77 shorter events, 0.3 us)
Async XLA Ops:
  7.2 21.2 %copy-start = (bf16[2,1,128,128]{3,2,1,0:T(8,128)(2,1)S(1)}, bf16[2,1,128,128]{3,2,1,0:T(8,128)(2,1)}, u32[]{:S(2)}) copy-start(bf16[2,1,128,128]{3,2,1,0:T(8,128)(2,1)} %param.13) | copy-start | bytes 196612
  7.2 12.4 %copy-start.8 = (bf16[1,128,1536]{2,1,0:T(8,128)(2,1)S(1)}, bf16[1,128,1536]{2,1,0:T(8,128)(2,1)}, u32[]{:S(2)}) copy-start(bf16[1,128,1536]{2,1,0:T(8,128)(2,1)} %param.10) | copy-start | bytes 1179652
  8.0 8.0 %collective-permute-start = (bf16[1,1536]{1,0:T(2,128)(2,1)S(1)}, bf16[1,1536]{1,0:T(2,128)(2,1)S(1)}, u32[]{:S(2)}, u32[]{:S(2)}) collective-permute-start(bf16[1,1536]{1,0:T(2,128)(2,1)S(1)} %get-tuple-element.57), channel_id=1, source_target_pairs={{0,1},{1,2},{2,3},{3,4},{4,5},{5,6},{6,7},{8,9},{9,10},{10,11},{11... | collective-permute-start | bytes 9224 | tf_op jit(solution)/shard_map/ppermute | solution.py:18
  12.9 5.5 %collective-permute-start.1 = (bf16[1,1536]{1,0:T(2,128)(2,1)S(1)}, bf16[1,1536]{1,0:T(2,128)(2,1)S(1)}, u32[]{:S(2)}, u32[]{:S(2)}) collective-permute-start(bf16[1,1536]{1,0:T(2,128)(2,1)S(1)} %get-tuple-element.58), channel_id=1, source_target_pairs={{1,0},{2,1},{3,2},{4,3},{5,4},{6,5},{7,6},{9,8},{10,9},{11,10},{12... | collective-permute-start | bytes 9224 | tf_op jit(solution)/shard_map/ppermute | solution.py:20
  15.0 5.1 %copy-start.13 = (bf16[1,1,128,128]{3,2,0,1:T(8,128)(2,1)}, bf16[1,1,128,128]{3,2,0,1:T(8,128)(2,1)S(1)}, u32[]{:S(2)}) copy-start(bf16[1,1,128,128]{3,2,0,1:T(8,128)(2,1)S(1)} %get-tuple-element.66) | copy-start | bytes 98308
  16.0 4.0 %copy-start.17 = (f32[1536]{0:T(1024)}, f32[1536]{0:T(1024)S(1)}, u32[]{:S(2)}) copy-start(f32[1536]{0:T(1024)S(1)} %get-tuple-element.41) | copy-start | bytes 18436
  16.0 4.0 %copy-start.19 = (f32[1536]{0:T(1024)}, f32[1536]{0:T(1024)S(1)}, u32[]{:S(2)}) copy-start(f32[1536]{0:T(1024)S(1)} %get-tuple-element.42) | copy-start | bytes 18436
  16.0 4.0 %copy-start.21 = (f32[1536]{0:T(1024)}, f32[1536]{0:T(1024)S(1)}, u32[]{:S(2)}) copy-start(f32[1536]{0:T(1024)S(1)} %get-tuple-element.43) | copy-start | bytes 18436
  16.0 4.0 %copy-start.23 = (f32[1536]{0:T(1024)}, f32[1536]{0:T(1024)S(1)}, u32[]{:S(2)}) copy-start(f32[1536]{0:T(1024)S(1)} %get-tuple-element.77) | copy-start | bytes 18436
  16.0 4.0 %copy-start.25 = (f32[1536]{0:T(1024)}, f32[1536]{0:T(1024)S(1)}, u32[]{:S(2)}) copy-start(f32[1536]{0:T(1024)S(1)} %get-tuple-element.78) | copy-start | bytes 18436
  16.0 4.0 %copy-start.27 = (f32[1536]{0:T(1024)}, f32[1536]{0:T(1024)S(1)}, u32[]{:S(2)}) copy-start(f32[1536]{0:T(1024)S(1)} %get-tuple-element.79) | copy-start | bytes 18436
  20.1 2.3 %copy-start.4 = (bf16[128,1536]{1,0:T(8,128)(2,1)}, bf16[128,1536]{1,0:T(8,128)(2,1)S(1)}, u32[]{:S(2)}) copy-start(bf16[128,1536]{1,0:T(8,128)(2,1)S(1)} %get-tuple-element.55) | copy-start | bytes 1179652
  20.1 8.3 %copy-start.6 = (bf16[128,1536,1]{1,0,2:T(8,128)(2,1)}, bf16[128,1536,1]{1,0,2:T(8,128)(2,1)S(1)}, u32[]{:S(2)}) copy-start(bf16[128,1536,1]{1,0,2:T(8,128)(2,1)S(1)} %get-tuple-element.56) | copy-start | bytes 1179652
  20.5 7.6 %copy-start.29 = (bf16[2,16,8,8]{1,3,2,0:T(8,128)(2,1)S(1)}, bf16[2,16,8,8]{1,3,2,0:T(8,128)(2,1)}, u32[]{:S(2)}) copy-start(bf16[2,16,8,8]{1,3,2,0:T(8,128)(2,1)} %param.14) | copy-start | bytes 12292
  20.5 7.7 %copy-start.30 = (bf16[2,16,8,8]{1,3,2,0:T(8,128)(2,1)S(1)}, bf16[2,16,8,8]{1,3,2,0:T(8,128)(2,1)}, u32[]{:S(2)}) copy-start(bf16[2,16,8,8]{1,3,2,0:T(8,128)(2,1)} %param.15) | copy-start | bytes 12292
  22.4 24.5 %all-to-all-start = ((bf16[2,128,1,1536]{3,0,2,1:T(2,128)(2,1)}), bf16[2,128,1,1536]{3,0,2,1:T(2,128)(2,1)S(1)}, u32[]{:S(2)}, u32[]{:S(2)}) async-start(bf16[2,128,1,1536]{3,0,2,1:T(2,128)(2,1)} %copy.72), calls=%async_computation | async-start | bytes 1572864 | tf_op jit(solution)/shard_map/all_to_all | solution.py:97
  30.7 21.2 %copy-start.12 = (bf16[16,8,1536]{2,1,0:T(8,128)(2,1)S(1)}, bf16[16,8,1536]{2,1,0:T(8,128)(2,1)}, u32[]{:S(2)}) copy-start(bf16[16,8,1536]{2,1,0:T(8,128)(2,1)} %param.17) | copy-start | bytes 1179652
  46.9 5.1 %copy-start.2 = (bf16[2,128,1,1536]{3,0,2,1:T(2,128)(2,1)}, bf16[2,128,1,1536]{3,0,2,1:T(2,128)(2,1)S(1)}, u32[]{:S(2)}) copy-start(bf16[2,128,1,1536]{3,0,2,1:T(2,128)(2,1)S(1)} %all-to-all-done) | copy-start | bytes 2359300
  46.9 23.4 %all-to-all-start.2 = ((bf16[2,1,128,1536]{3,0,1,2:T(2,128)(2,1)}), bf16[2,1,128,1536]{3,0,1,2:T(2,128)(2,1)}, u32[]{:S(2)}, u32[]{:S(2)}) async-start(bf16[2,1,128,1536]{3,0,1,2:T(2,128)(2,1)} %copy.85), calls=%async_computation.2 | async-start | bytes 1572864 | tf_op jit(solution)/shard_map/all_to_all | solution.py:73
  55.6 20.1 %copy-start.15 = (bf16[1,2,16,8,8]{3,4,1,2,0:T(8,128)(2,1)S(1)}, bf16[1,2,16,8,8]{3,4,1,2,0:T(8,128)(2,1)}, u32[]{:S(2)}) copy-start(bf16[1,2,16,8,8]{3,4,1,2,0:T(8,128)(2,1)} %get-tuple-element.64) | copy-start | bytes 12292
  55.6 20.1 %copy-start.16 = (bf16[1,2,16,8,8]{3,4,1,2,0:T(8,128)(2,1)S(1)}, bf16[1,2,16,8,8]{3,4,1,2,0:T(8,128)(2,1)}, u32[]{:S(2)}) copy-start(bf16[1,2,16,8,8]{3,4,1,2,0:T(8,128)(2,1)} %get-tuple-element.74) | copy-start | bytes 12292
  70.3 23.9 %all-to-all-start.1 = ((bf16[2,8,16,1536]{3,0,2,1:T(2,128)(2,1)}), bf16[2,8,16,1536]{3,0,2,1:T(2,128)(2,1)}, u32[]{:S(2)}, u32[]{:S(2)}) async-start(bf16[2,8,16,1536]{3,0,2,1:T(2,128)(2,1)} %copy.81), calls=%async_computation.1 | async-start | bytes 1572864 | tf_op jit(solution)/shard_map/all_to_all | solution.py:119
  76.4 2.0 copy-start.1
  76.9 1.5 copy-start.3
  94.2 24.1 %all-to-all-start.3 = ((bf16[2,16,8,1536]{3,0,1,2:T(2,128)(2,1)}), bf16[2,16,8,1536]{3,0,1,2:T(2,128)(2,1)}, u32[]{:S(2)}, u32[]{:S(2)}) async-start(bf16[2,16,8,1536]{3,0,1,2:T(2,128)(2,1)} %copy.90), calls=%async_computation.3 | async-start | bytes 1572864 | tf_op jit(solution)/shard_map/all_to_all | solution.py:82
  98.4 89.7 %reduce-scatter.2.cloned.1.call-start = ((), (), s32[]{:S(2)}) async-start(), calls=%async_computation.5 | async-start | bytes 983040 | tf_op jit(solution)/shard_map/reduce_scatter | solution.py:106
  103.3 1.3 copy-start.7
  105.1 14.5 %copy-start.5 = (bf16[128,1536]{1,0:T(8,128)(2,1)S(1)}, bf16[128,1536]{1,0:T(8,128)(2,1)}, u32[]{:S(2)}) copy-start(bf16[128,1536]{1,0:T(8,128)(2,1)} %copy-done.4) | copy-start | bytes 1179652
  118.2 1.7 copy-start.9
  118.2 1.7 copy-start.14
  121.4 6.2 %copy-start.10 = (f32[2,16,8,8]{2,3,1,0:T(8,128)S(1)}, f32[2,16,8,8]{2,3,1,0:T(8,128)}, u32[]{:S(2)}) copy-start(f32[2,16,8,8]{2,3,1,0:T(8,128)} %pad_maximum_fusion.7) | copy-start | bytes 24580
  121.4 6.2 %copy-start.11 = (f32[2,1,128,128]{2,3,0,1:T(8,128)S(1)}, f32[2,1,128,128]{2,3,0,1:T(8,128)}, u32[]{:S(2)}) copy-start(f32[2,1,128,128]{2,3,0,1:T(8,128)} %pad_maximum_fusion.8) | copy-start | bytes 393220
  121.4 65.3 %copy-start.18 = (f32[1536]{0:T(1024)S(1)}, f32[1536]{0:T(1024)}, u32[]{:S(2)}) copy-start(f32[1536]{0:T(1024)} %copy-done.17) | copy-start | bytes 18436
  121.4 65.3 %copy-start.20 = (f32[1536]{0:T(1024)S(1)}, f32[1536]{0:T(1024)}, u32[]{:S(2)}) copy-start(f32[1536]{0:T(1024)} %copy-done.19) | copy-start | bytes 18436
  121.5 65.3 %copy-start.22 = (f32[1536]{0:T(1024)S(1)}, f32[1536]{0:T(1024)}, u32[]{:S(2)}) copy-start(f32[1536]{0:T(1024)} %copy-done.21) | copy-start | bytes 18436
  121.5 65.3 %copy-start.24 = (f32[1536]{0:T(1024)S(1)}, f32[1536]{0:T(1024)}, u32[]{:S(2)}) copy-start(f32[1536]{0:T(1024)} %copy-done.23) | copy-start | bytes 18436
  121.5 65.3 %copy-start.26 = (f32[1536]{0:T(1024)S(1)}, f32[1536]{0:T(1024)}, u32[]{:S(2)}) copy-start(f32[1536]{0:T(1024)} %copy-done.25) | copy-start | bytes 18436
  121.5 65.3 %copy-start.28 = (f32[1536]{0:T(1024)S(1)}, f32[1536]{0:T(1024)}, u32[]{:S(2)}) copy-start(f32[1536]{0:T(1024)} %copy-done.27) | copy-start | bytes 18436
  121.6 65.1 %collective-permute-start.2 = (f32[2,1,1536]{2,1,0:T(1,128)S(1)}, f32[2,1,1536]{2,1,0:T(1,128)S(1)}, u32[]{:S(2)}, u32[]{:S(2)}) collective-permute-start(f32[2,1,1536]{2,1,0:T(1,128)S(1)} %get-tuple-element.53), channel_id=1, source_target_pairs={{1,0},{2,1},{3,2},{4,3},{5,4},{6,5},{7,6},{9,8},{10,9},{11,10},{12... | collective-permute-start | bytes 36872 | tf_op jit(solution)/shard_map/ppermute | solution.py:20
  123.0 63.7 %collective-permute-start.3 = (f32[2,1,1536]{2,1,0:T(1,128)S(1)}, f32[2,1,1536]{2,1,0:T(1,128)S(1)}, u32[]{:S(2)}, u32[]{:S(2)}) collective-permute-start(f32[2,1,1536]{2,1,0:T(1,128)S(1)} %get-tuple-element.54), channel_id=1, source_target_pairs={{0,1},{1,2},{2,3},{3,4},{4,5},{5,6},{6,7},{8,9},{9,10},{10,11},{11... | collective-permute-start | bytes 36872 | tf_op jit(solution)/shard_map/ppermute | solution.py:18
Sparse Core Ops, SparseCore 0:
  103.5 24.5 reduce-scatter.1
where the time goes:
time: 205 us; the launch traced here: 204 us
  blocking collectives  63.4 us (31%)
  waiting for transfers between devices  56.2 us (27%)
  starting transfers between devices  30.5 us (15%)
  local copies, waits for them, and re-layouts  16.4 us (8%)
  between operations  14.7 us (7%)
  other arithmetic  13.5 us (7%)
  matrix products  9.11 us (4%)
    psum x1, blocking collectives, shards(): lax.psum((conv_grad(value_grad, padded), conv_grad(gate_grad, padded)), (...  39.5 us
    psum x1, blocking collectives, shards(): lax.psum((grad_one, grad_two, grad_three, grad_four), 'dp')  16.6 us
    all_to_all x1, waiting for transfers between devices, shards(): lax.all_to_all(third_grad, 'seq', split_axis=1, concat_axis=2, tiled=True)  16.2 us
    all_to_all x1, waiting for transfers between devices, shards(): lax.all_to_all(first, 'seq', split_axis=2, concat_axis=1, tiled=True)  14.7 us
    all_to_all x1, waiting for transfers between devices, shards(): lax.all_to_all(third, 'seq', split_axis=2, concat_axis=1, tiled=True)  12.8 us
    all_to_all x1, waiting for transfers between devices, shards(): lax.all_to_all(first_grad, 'seq', split_axis=1, concat_axis=2, tiled=True)  10.1 us
    ppermute x2, starting transfers between devices, with_halo(): lax.ppermute(tail, axis, [(i, (i + 1) % count) for i in range(ends)])  9.42 us
    all_gather x1, blocking collectives, shards(): grad_filter = lax.all_gather(finished, 'dp', axis=2, tiled=True)  7.25 us
  transfers between devices with their start and end apart: 9, of which 5 were waited for; matrix products, arithmetic and copies ran while one was open for 16% of the time, Pallas kernels for 0%

commit v1 on v0

v1 whole, which is shorter than its diff:
```python
import functools

import jax
import jax.numpy as jnp
from jax import lax
from jax.experimental import pallas as pl
from jax.experimental.pallas import tpu as pltpu
from jax.sharding import PartitionSpec as P

F32 = jnp.float32
BF16 = jnp.bfloat16
TILE = 16
VMEM = pl.BlockSpec(memory_space=pltpu.VMEM)
SMEM = pl.BlockSpec(memory_space=pltpu.SMEM)
FAR = pl.BlockSpec(memory_space=pl.ANY)


class Plan:
    def __init__(self, dp, seq, tokens, mix_one, mix_two):
        self.dp, self.seq = dp, seq
        self.blk = mix_one.shape[-1]
        self.channels = tokens.shape[-1]
        assert tokens.shape[1] == self.blk and dp % 2 == 0
        self.nblk = seq
        self.kloc = mix_two.shape[1]
        half_dp = dp // 2
        self.fold = max(
            f
            for f in range(1, half_dp + 1)
            if half_dp % f == 0 and self.channels % (seq * f * TILE) == 0
        )
        self.groups = half_dp // self.fold
        self.members = self.fold * seq
        self.width = self.channels // self.members
        assert self.width <= 128
        self.cols = self.fold * self.width
        self.length = self.nblk * self.blk
        self.pairs = self.nblk * self.nblk
        self.yrows = self.kloc * 2 * self.pairs // self.blk
        self.direct = self.yrows == self.kloc
        self.streamed = self.nblk * TILE > self.blk
        self.kgroups = self.blk // TILE
        self.dim = self.nblk * TILE
        unit = TILE * self.fold
        self.half = -(-(2 * self.blk + self.yrows) // unit) * unit
        self.mrows = self.half // self.fold
        self.cores_share = self.width % (2 * TILE) == 0
        self.frows = self.width // 2 if self.cores_share else self.width
        self.full = -(-(self.width + TILE) // (2 * unit)) * 2 * unit
        self.orows = self.full // (2 * self.fold)
        self.share = self.mrows + self.orows
        self.group_lists = [
            [
                ((g * self.fold + h) * 2 + core) * seq + s
                for h in range(self.fold)
                for s in range(seq)
            ]
            for g in range(self.groups)
            for core in range(2)
        ]

    def across_cores(self):
        return [(d, d ^ 1) for d in range(self.dp)]

    def across_fold(self, step):
        moves = []
        for g in range(self.groups):
            for h in range(self.fold):
                for core in range(2):
                    source = (g * self.fold + h) * 2 + core
                    moves.append((source, (g * self.fold + (h + step) % self.fold) * 2 + core))
        return moves

    def across_groups(self, step):
        block = 2 * self.fold
        return [(d, (d + step * block) % self.dp) for d in range(self.dp)]


def each(count, body):
    if count <= 8:
        for i in range(count):
            body(i)
    else:
        lax.fori_loop(0, count, lambda i, c: (body(i), c)[1], 0)


def rows_at(start, size):
    return pl.ds(start if isinstance(start, int) else pl.multiple_of(start, TILE), size)


def dot(a, b, ca, cb):
    return lax.dot_general(a, b, (((ca,), (cb,)), ((), ())), preferred_element_type=F32)


def call(kernel, out_shape, *args, scratch=(), smem=(), far=(), limit=16, name=None):
    single = not isinstance(out_shape, (list, tuple))
    return pl.pallas_call(
        kernel,
        out_shape=out_shape,
        in_specs=[SMEM if i in smem else FAR if i in far else VMEM for i in range(len(args))],
        out_specs=VMEM if single else [VMEM] * len(out_shape),
        scratch_shapes=list(scratch),
        compiler_params=pltpu.CompilerParams(vmem_limit_bytes=limit * 2**20),
        name=name,
    )(*args)


def shape(*dims, dtype=BF16):
    return jax.ShapeDtypeStruct(dims, dtype)


def factor_message_kernel(p, place, *refs):
    count = 5 if p.direct else 4
    far, out, near, rows, turned, done = refs[:count], refs[count], refs[count + 1 : -3], *refs[-3:]
    copies = [pltpu.make_async_copy(f, n, done.at[i]) for i, (f, n) in enumerate(zip(far, near))]
    for copy in copies:
        copy.start()
    h, core = place[0], place[1]
    filt, one, four = near[:3]
    for copy in copies[1:]:
        copy.wait()
    for part in range(2):
        base = part * p.half
        rows[base : base + p.blk] = one[part]
        rows[base + p.blk : base + 2 * p.blk] = four[part]
        if p.direct:
            small = jnp.concatenate([near[3][part], near[4][part]], axis=0).T
        else:
            small = near[3][part]
        rows[base + 2 * p.blk : base + 2 * p.blk + p.yrows] = small
        pad = p.half - 2 * p.blk - p.yrows
        if pad:
            rows[base + p.half - pad : base + p.half] = jnp.zeros((pad, p.blk), BF16)
    mine = rows[rows_at(core * p.half + h * p.mrows, p.mrows)]
    copies[0].wait()
    turned[...] = filt[...].T

    def one_target(s):
        out[s, 0 : p.mrows] = mine
        start = (h * p.seq + s) * p.width
        if p.cores_share:
            start = start + core * p.frows
        out[s, p.mrows :] = turned[rows_at(start, p.frows)]

    each(p.seq, one_target)


def token_message_kernel(p, tokens, upstream, out):
    w = p.width
    token_rows = tokens[...].T
    upstream_rows = upstream[...].T
    for q in range(p.members):
        out[q, 0:w] = token_rows[q * w : (q + 1) * w]
        out[q, w : 2 * w] = upstream_rows[q * w : (q + 1) * w]


def prepare_kernel(p, place, *refs):
    pieces, (one, four, small, filt, rows, turned) = refs[: 2 * p.fold], refs[2 * p.fold :]
    h, core = place[0], place[1]
    for side in range(2):
        c = core if side == 0 else 1 - core
        for step in range(p.fold):
            piece = pieces[side * p.fold + step]
            owner = h - step
            owner = jnp.where(owner < 0, owner + p.fold, owner)
            rows[:, rows_at(c * p.half + owner * p.mrows, p.mrows), :] = piece[:, 0 : p.mrows, :]
            if step == 0 and (p.cores_share or side == 0):
                start = c * p.frows if p.cores_share else 0
                turned[:, rows_at(start, p.frows), :] = piece[:, p.mrows :, :]

    def one_block(i):
        for part in range(2):
            base = part * p.half
            one[i, part * p.blk : (part + 1) * p.blk] = rows[i, base : base + p.blk]
            factor = rows[i, base + p.blk : base + 2 * p.blk]
            four[i, :, part * p.blk : (part + 1) * p.blk] = factor if part == 0 else -factor
            small[part, i] = rows[i, base + 2 * p.blk : base + 2 * p.blk + p.yrows]
        logs = turned[i]
        if p.fold > 1:
            logs = jnp.concatenate([logs] * p.fold, axis=0)
        filt[i] = jnp.exp(logs.T.astype(F32))

    each(p.nblk, one_block)


def iota(dims, axis):
    return lax.broadcasted_iota(jnp.int32, dims, axis)


def block_masks(p):
    d, nb, pairs = p.dim, p.nblk, p.pairs
    same = iota((d, d), 0) % TILE == iota((d, d), 1) // nb
    lane = iota((d, 2 * pairs), 1)
    block = iota((d, 2 * pairs), 0) // TILE
    keep_two = (lane < pairs) & (lane % nb == block)
    keep_three = (lane >= pairs) & ((lane - pairs) // nb == block)
    return same, keep_two, keep_three


def selectors(p, turned):
    d, nb, pairs = p.dim, p.nblk, p.pairs
    dims = (d, 2 * pairs) if turned else (2 * pairs, d)
    lane = iota(dims, 1 if turned else 0)
    block = iota(dims, 0 if turned else 1) % nb
    two = (lane < pairs) & (lane // nb == block)
    three = (lane >= pairs) & ((lane - pairs) % nb == block)
    return two.astype(BF16), three.astype(BF16)


def block_factor_kernel(p, small, two, three):
    same, keep_two, keep_three = block_masks(p)
    pick_two, pick_three = selectors(p, False)
    d = p.dim

    def one_group(g):
        parts = {}
        for part in range(2):
            entries = small[part, rows_at(g * TILE, TILE)]
            tiled = jnp.concatenate([entries] * p.nblk, axis=0)
            zero = jnp.zeros_like(tiled)
            for name, keep, pick in (("two", keep_two, pick_two), ("three", keep_three, pick_three)):
                spread = dot(jnp.where(keep, tiled, zero), pick, 1, 0)
                parts[name, part] = jnp.where(same, spread, 0.0).astype(BF16)
        two[g, :d, :d] = parts["two", 0]
        two[g, d:, d:] = parts["two", 0]
        two[g, :d, d:] = parts["two", 1]
        two[g, d:, :d] = -parts["two", 1]
        three[g, :d, :d] = parts["three", 0]
        three[g, d:, d:] = parts["three", 0]
        three[g, :d, d:] = -parts["three", 1]
        three[g, d:, :d] = parts["three", 1]

    each(p.kgroups, one_group)


def mixer_kernel(
    p, place, tokens_in, taps, one, four, two_far, three_far, filt,
    grad_x, keep, send, small_keep, small_send,
    tok, ups, val, mix, groups_a, groups_b, second, time_a, gate, grad_v, filter_grad, halves, fulls, small, *near,
):
    core = place[1]

    def factor(far, at, g):
        if not p.streamed:
            return far[g]
        pltpu.sync_copy(far.at[g], near[at])
        return near[at][...]

    blk, nb, d, w, cols = p.blk, p.nblk, p.dim, p.width, p.cols
    edge = 8

    def taps_of(branch, offset):
        return taps[3 * branch + offset : 3 * branch + offset + 1, :]

    zero_edge = jnp.zeros((edge, cols), F32)
    for ref in (tok, gate, grad_v):
        ref[0:edge] = zero_edge
        ref[edge + p.length : 2 * edge + p.length] = zero_edge

    def load(i):
        both = [tokens_in[h * nb + i] for h in range(p.fold)]
        t = jnp.concatenate([b[0:w] for b in both], axis=0) if p.fold > 1 else both[0][0:w]
        u = jnp.concatenate([b[w:] for b in both], axis=0) if p.fold > 1 else both[0][w:]
        tok[rows_at(edge + i * blk, blk) if isinstance(i, int) else pl.ds(pl.multiple_of(edge + i * blk, 8), blk)] = t.T.astype(F32)
        ups[rows_at(i * blk, blk)] = u.T

    each(nb, load)

    def window(ref, i, offset):
        return ref[pl.ds(edge + i * blk + offset, blk)]

    def spread(ref, i, value):
        for part in range(2):
            for g in range(p.kgroups):
                row = part * blk + g * TILE
                ref[g, rows_at((part * nb + i) * TILE, TILE)] = value[row : row + TILE]

    def first_stage(i):
        before, here, after = (window(tok, i, o) for o in (-1, 0, 1))
        values = taps_of(0, 0) * before + taps_of(0, 1) * here + taps_of(0, 2) * after
        gating = taps_of(1, 0) * before + taps_of(1, 1) * here + taps_of(1, 2) * after
        values = values.astype(BF16)
        val[rows_at(i * blk, blk)] = values
        up = ups[rows_at(i * blk, blk)].astype(F32)
        mix[rows_at(i * blk, blk)] = (up * gating.astype(BF16).astype(F32)).astype(BF16)
        spread(groups_a, i, dot(one[i], values, 1, 0).astype(BF16))

    each(nb, first_stage)

    def filter_of(g):
        f = filt[rows_at(g * d, d)]
        return f

    def forward_middle(g):
        f = filter_of(g)
        f2 = jnp.concatenate([f, f], axis=0)
        sec = dot(factor(two_far, 0, g), groups_a[g], 0, 0)
        second[g] = sec
        weighted = (f2 * sec).astype(BF16)
        groups_b[g] = weighted
        third = dot(factor(three_far, 1, g), weighted, 1, 0).astype(BF16)
        for part in range(2):
            for n in range(nb):
                row = (part * nb + n) * TILE
                time_a[n, rows_at(part * blk + g * TILE, TILE)] = third[row : row + TILE]

    each(p.kgroups, forward_middle)

    def last_factor(n):
        third = time_a[n]
        last = four[n]
        mixed = dot(last, third, 1, 0)
        at = rows_at(n * blk, blk)
        gate[pl.ds(edge + n * blk, blk)] = ups[at].astype(F32) * mixed
        grads = mix[at]
        back = dot(last, grads, 0, 0).astype(BF16)
        for part in range(2):
            for g in range(p.kgroups):
                row = part * blk + g * TILE
                groups_b[p.kgroups + g, rows_at((part * nb + n) * TILE, TILE)] = back[row : row + TILE]
        products = dot(grads, third, 1, 1)
        halves[0, n, blk : 2 * blk] = products[:, 0:blk].astype(BF16)
        halves[1, n, blk : 2 * blk] = (-products[:, blk:]).astype(BF16)

    each(nb, last_factor)

    same, keep_two, keep_three = block_masks(p)
    pick_two, pick_three = selectors(p, True)

    def folded(real, imag, pick, kept):
        out = []
        for value in (real, imag):
            value = jnp.where(same, value, 0.0).astype(BF16)
            wide = dot(value, pick, 1, 0)
            wide = jnp.where(kept, wide, 0.0)
            out.append(jnp.sum(wide.reshape(nb, TILE, 2 * p.pairs), axis=0))
        return out

    def backward_middle(g):
        f = filter_of(g)
        f2 = jnp.concatenate([f, f], axis=0)
        third_grad = groups_b[p.kgroups + g]
        weighted_grad = dot(factor(three_far, 1, g), third_grad, 0, 0)
        term = weighted_grad * second[g]
        filter_grad[rows_at(g * d, d)] = f * (term[:d] + term[d:])
        products = dot(third_grad, groups_b[g], 1, 1)
        three_real, three_imag = folded(
            products[:d, :d] + products[d:, d:], products[d:, :d] - products[:d, d:], pick_three, keep_three
        )
        second_grad = (f2 * weighted_grad).astype(BF16)
        products = dot(groups_a[g], second_grad, 1, 1)
        two_real, two_imag = folded(
            products[:d, :d] + products[d:, d:], products[:d, d:] - products[d:, :d], pick_two, keep_two
        )
        at = rows_at(g * TILE, TILE)
        small[0, at] = (two_real + three_real).astype(BF16)
        small[1, at] = (two_imag + three_imag).astype(BF16)
        back = dot(factor(two_far, 0, g), second_grad, 1, 0).astype(BF16)
        for part in range(2):
            for i in range(nb):
                row = (part * nb + i) * TILE
                time_a[i, rows_at(part * blk + g * TILE, TILE)] = back[row : row + TILE]

    each(p.kgroups, backward_middle)

    def first_factor(i):
        first_grad = time_a[i]
        grad_v[pl.ds(edge + i * blk, blk)] = dot(one[i], first_grad, 0, 0)
        products = dot(first_grad, val[rows_at(i * blk, blk)], 1, 1)
        for part in range(2):
            halves[part, i, 0:blk] = products[part * blk : (part + 1) * blk].astype(BF16)
        if p.half > 2 * blk:
            rest = jnp.zeros((p.half - 2 * blk, blk), BF16)
            for part in range(2):
                halves[part, i, 2 * blk :] = rest

    each(nb, first_factor)

    sums = [jnp.zeros((8, cols), F32) for _ in range(6)]

    def last_stage(i, sums):
        total = jnp.zeros((blk, cols), F32)
        sums = list(sums)
        for branch, ref in ((0, grad_v), (1, gate)):
            before, here, after = (window(ref, i, o) for o in (-1, 0, 1))
            total += taps_of(branch, 0) * after + taps_of(branch, 1) * here + taps_of(branch, 2) * before
            for offset in range(3):
                product = here * window(tok, i, offset - 1)
                sums[3 * branch + offset] += jnp.sum(product.reshape(blk // 8, 8, cols), axis=0)
        turned = total.astype(BF16).T
        terms = filter_grad[rows_at(i * blk, blk)].T
        term = terms[0:w]
        for h in range(1, p.fold):
            term = term + terms[h * w : (h + 1) * w]
        fulls[i, 0:w] = term.astype(BF16)
        if p.full > w + TILE:
            fulls[i, w + TILE :] = jnp.zeros((p.full - w - TILE, blk), BF16)
        for h in range(p.fold):
            grad_x[h * nb + i] = turned[h * w : (h + 1) * w]
        return tuple(sums)

    if nb <= 8:
        for i in range(nb):
            sums = last_stage(i, sums)
    else:
        sums = lax.fori_loop(0, nb, last_stage, tuple(sums))

    conv = jnp.concatenate([jnp.sum(s, axis=0, keepdims=True) for s in sums] + [jnp.zeros((2, cols), F32)], axis=0)
    term = conv[:, 0:w]
    for h in range(1, p.fold):
        term = term + conv[:, h * w : (h + 1) * w]
    if w < blk:
        term = jnp.concatenate([term, jnp.zeros((8, blk - w), F32)], axis=1)
    high = term.astype(BF16).astype(F32)
    conv_rows = jnp.concatenate([high, term - high], axis=0).astype(BF16)

    def hand_out(s):
        fulls[s, w : w + TILE] = conv_rows
        for ref, c in ((keep, core), (send, 1 - core)):
            for h in range(p.fold):
                ref[h, s, 0 : p.mrows] = halves[c, s, h * p.mrows : (h + 1) * p.mrows]
                ref[h, s, p.mrows :] = fulls[s, rows_at((c * p.fold + h) * p.orows, p.orows)]

    each(nb, hand_out)
    small_keep[...] = small[core]
    small_send[...] = small[1 - core]


def add_kernel(p, grad_x, keep, got, small_keep, small_got, out):
    w = p.width

    def one_target(s):
        extra = (small_keep[s].astype(F32) + small_got[s].astype(F32)).astype(BF16)
        for h in range(p.fold):
            q = h * p.seq + s
            out[q, 0:w] = grad_x[q]
            out[q, w:] = (keep[h, s].astype(F32) + got[h, s].astype(F32)).astype(BF16)
            first, last = 2 * p.blk - h * p.mrows, 2 * p.blk + p.yrows - h * p.mrows
            lo, hi = max(first, 0), min(last, p.mrows)
            if lo < hi:
                out[q, w + lo : w + hi] = extra[lo - first : hi - first]

    each(p.seq, one_target)


def sum_kernel(p, got, out):
    w = p.width
    total = got[0, w : w + p.mrows].astype(F32)
    for q in range(1, p.members):
        total += got[q, w : w + p.mrows].astype(F32)
    out[0 : p.mrows] = total.astype(BF16)
    for q in range(p.members):
        at = p.mrows + q * p.orows
        out[at : at + p.orows] = got[q, w + p.mrows :]


def grad_x_kernel(p, got, out):
    rows = jnp.concatenate([got[q, 0 : p.width] for q in range(p.members)], axis=0)
    out[...] = rows.T


def finish_kernel(p, place, *refs):
    pieces, outs, (rows, fulls) = refs[: 2 * p.fold], refs[2 * p.fold : -2], refs[-2:]
    one, four, filt, conv_value, conv_gate, *small = outs
    h, core = place[0], place[1]
    for side in range(2):
        c = core if side == 0 else 1 - core
        for step in range(p.fold):
            piece = pieces[side * p.fold + step]
            owner = h - step
            owner = jnp.where(owner < 0, owner + p.fold, owner)
            rows[rows_at(c * p.half + owner * p.mrows, p.mrows)] = piece[0 : p.mrows]
            at = rows_at((c * p.fold + owner) * p.orows, p.orows)
            for q in range(p.members):
                fulls[q, at] = piece[p.mrows + q * p.orows : p.mrows + (q + 1) * p.orows]
    for part in range(2):
        base = part * p.half
        one[part] = rows[base : base + p.blk]
        four[part] = rows[base + p.blk : base + 2 * p.blk]
        entries = rows[base + 2 * p.blk : base + 2 * p.blk + p.yrows]
        if p.direct:
            entries = entries.T
            small[0][part] = entries[: p.pairs]
            small[1][part] = entries[p.pairs :]
        else:
            small[0][part] = entries
    turned = jnp.concatenate([fulls[q, 0 : p.width] for q in range(p.members)], axis=0)
    filt[...] = turned.T
    sums = fulls[:, p.width : p.width + TILE].astype(F32)
    sums = sums[:, :8] + sums[:, 8:]
    sums = jnp.concatenate([sums[q].T[: p.width] for q in range(p.members)], axis=0).T
    conv_value[...] = sums[0:3]
    conv_gate[...] = sums[3:6]


def shards(
    tokens, upstream, conv_value, conv_gate, mix_one, mix_two, mix_three, mix_four, filter_log
):
    p = Plan(lax.axis_size("dp"), lax.axis_size("seq"), tokens, mix_one, mix_two)
    dp_at, seq_at = lax.axis_index("dp"), lax.axis_index("seq")
    h_at = (dp_at // 2) % p.fold
    place = jnp.stack([h_at, dp_at % 2]).astype(jnp.int32)
    blk, pairs = p.blk, p.pairs

    def shuffle(array):
        return lax.all_to_all(
            array, ("dp", "seq"), 0, 0, tiled=True, axis_index_groups=p.group_lists
        )

    def swap(array):
        return lax.ppermute(array, "dp", p.across_cores())

    def gathered(array, rows):
        pieces = [array]
        for step in range(1, p.fold):
            pieces.append(lax.ppermute(rows(array), "dp", p.across_fold(step)))
        return pieces + [swap(piece) for piece in pieces]

    if p.direct:
        small = [f.transpose(0, 2, 3, 1).reshape(2, pairs, p.kloc) for f in (mix_two, mix_three)]
    else:
        small = [f.reshape(2, p.kloc, pairs) for f in (mix_two, mix_three)]
        small = [jnp.concatenate(small, axis=2).reshape(2, p.yrows, blk)]
    far = [
        filter_log.reshape(blk, p.channels),
        mix_one.reshape(2, blk, blk),
        mix_four.reshape(2, blk, blk),
        *small,
    ]
    message = call(
        functools.partial(factor_message_kernel, p),
        shape(p.seq, p.mrows + p.frows, blk),
        place,
        *far,
        scratch=[pltpu.VMEM(f.shape, BF16) for f in far]
        + [
            pltpu.VMEM((2 * p.half, blk), BF16),
            pltpu.VMEM((p.channels, blk), BF16),
            pltpu.SemaphoreType.DMA((len(far),)),
        ],
        smem=(0,),
        far=range(1, 1 + len(far)),
        name="factor_message",
    )
    factors = lax.all_to_all(message, "seq", 0, 0, tiled=True)
    pieces = gathered(factors, lambda a: a[:, : p.mrows])
    one, four, small, filt = call(
        functools.partial(prepare_kernel, p),
        [
            shape(p.nblk, 2 * blk, blk),
            shape(p.nblk, blk, 2 * blk),
            shape(2, p.nblk, p.yrows, blk),
            shape(p.nblk, blk, p.cols, dtype=F32),
        ],
        place,
        *pieces,
        scratch=[
            pltpu.VMEM((p.nblk, 2 * p.half, blk), BF16),
            pltpu.VMEM((p.nblk, p.width, blk), BF16),
        ],
        smem=(0,),
        name="prepare",
    )
    two, three = call(
        functools.partial(block_factor_kernel, p),
        [shape(p.kgroups, 2 * p.dim, 2 * p.dim)] * 2,
        small.reshape(2, blk, 2 * pairs),
        limit=48 if p.streamed else 16,
        name="block_factors",
    )

    message = call(
        functools.partial(token_message_kernel, p),
        shape(p.members, 2 * p.width, blk),
        tokens[0],
        upstream[0],
        name="token_message",
    )
    received = shuffle(message)
    start = (h_at * p.seq + seq_at) * p.width
    taps = jnp.concatenate([conv_value, conv_gate], axis=0)
    taps = lax.dynamic_slice_in_dim(taps, start, p.width, 1)
    taps = jnp.concatenate([taps] * p.fold, axis=1)

    padded = p.length + 16
    grad_x, keep, send, small_keep, small_send = call(
        functools.partial(mixer_kernel, p),
        [
            shape(p.members, p.width, blk),
            shape(p.fold, p.seq, p.share, blk),
            shape(p.fold, p.seq, p.share, blk),
            shape(blk, 2 * pairs),
            shape(blk, 2 * pairs),
        ],
        place,
        received,
        taps,
        one,
        four,
        two,
        three,
        filt.reshape(p.length, p.cols),
        scratch=[
            pltpu.VMEM((padded, p.cols), F32),
            pltpu.VMEM((p.length, p.cols), BF16),
            pltpu.VMEM((p.length, p.cols), BF16),
            pltpu.VMEM((p.length, p.cols), BF16),
            pltpu.VMEM((p.kgroups, 2 * p.dim, p.cols), BF16),
            pltpu.VMEM((2 * p.kgroups, 2 * p.dim, p.cols), BF16),
            pltpu.VMEM((p.kgroups, 2 * p.dim, p.cols), F32),
            pltpu.VMEM((p.nblk, 2 * blk, p.cols), BF16),
            pltpu.VMEM((padded, p.cols), F32),
            pltpu.VMEM((padded, p.cols), F32),
            pltpu.VMEM((p.length, p.cols), F32),
            pltpu.VMEM((2, p.nblk, p.half, blk), BF16),
            pltpu.VMEM((p.nblk, p.full, blk), BF16),
            pltpu.VMEM((2, blk, 2 * pairs), BF16),
        ]
        + [pltpu.VMEM((2 * p.dim, 2 * p.dim), BF16)] * (2 if p.streamed else 0),
        smem=(0,),
        far=(5, 6) if p.streamed else (),
        limit=60 if p.streamed else 20,
        name="mixer",
    )

    message = call(
        functools.partial(add_kernel, p),
        shape(p.members, p.width + p.share, blk),
        grad_x,
        keep,
        swap(send),
        small_keep.reshape(p.seq, p.yrows, blk),
        swap(small_send).reshape(p.seq, p.yrows, blk),
        name="add_cores",
    )
    received = shuffle(message)
    sums = call(
        functools.partial(sum_kernel, p),
        shape(p.mrows + p.members * p.orows, blk),
        received,
        name="sum_sources",
    )
    if p.groups > 1:
        total = sums.astype(F32)
        for step in range(1, p.groups):
            total += lax.ppermute(sums, "dp", p.across_groups(step)).astype(F32)
        sums = total.astype(BF16)
    pieces = gathered(sums, lambda a: a)
    token_grad = call(
        functools.partial(grad_x_kernel, p), shape(blk, p.channels), received, name="token_grad"
    )
    grad_one, grad_four, grad_filter, sum_value, sum_gate, *small = call(
        functools.partial(finish_kernel, p),
        [
            shape(2, blk, blk),
            shape(2, blk, blk),
            shape(blk, p.channels),
            shape(3, p.channels, dtype=F32),
            shape(3, p.channels, dtype=F32),
        ]
        + ([shape(2, pairs, p.kloc)] * 2 if p.direct else [shape(2, p.yrows, blk)]),
        place,
        *pieces,
        scratch=[
            pltpu.VMEM((2 * p.half, blk), BF16),
            pltpu.VMEM((p.members, p.full, blk), BF16),
        ],
        smem=(0,),
        name="finish",
    )
    if p.direct:
        small = [f.reshape(2, p.nblk, p.nblk, p.kloc).transpose(0, 3, 1, 2) for f in small]
    else:
        small = small[0].reshape(2, p.kloc, 2, p.nblk, p.nblk)
        small = [small[:, :, 0], small[:, :, 1]]
    return (
        token_grad[None],
        sum_value,
        sum_gate,
        grad_one.reshape(mix_one.shape),
        *small,
        grad_four.reshape(mix_four.shape),
        grad_filter.reshape(filter_log.shape),
    )


def solution(mesh):
    return jax.shard_map(
        shards,
        mesh=mesh,
        in_specs=(
            P("dp", "seq", None),
            P("dp", "seq", None),
            P(),
            P(),
            P(None, "seq", None, None),
            P(None, "seq", None, None),
            P(None, "seq", None, None),
            P(None, "seq", None, None),
            P("seq", None, None),
        ),
        out_specs=(
            P("dp", "seq", None),
            P(),
            P(),
            P(None, "seq", None, None),
            P(None, "seq", None, None),
            P(None, "seq", None, None),
            P(None, "seq", None, None),
            P("seq", None, None),
        ),
        check_vma=False,
    )
```

time: 205 us -> 110 us (0.54)
  blocking collectives: 63.4 us -> 34.6 us
  waiting for transfers between devices: 56.2 us -> 32.4 us
  Pallas kernels: 0 us -> 15.8 us
  starting transfers between devices: 30.5 us -> 15.2 us
  between operations: 14.7 us -> 0.77 us
  other arithmetic: 13.5 us -> 0.23 us
  matrix products: 9.11 us -> 0 us
  local copies, waits for them, and re-layouts: 16.4 us -> 10.1 us
    psum x2 -> x0, blocking collectives: 56.1 us -> none  [the longest x1 39.5 us: shards(): lax.psum((conv_grad(value_grad, padded), conv_grad(gate_grad, padded)), (...]
    all_to_all x4 -> x2, waiting for transfers between devices: 53.8 us -> 10.5 us  [the longest x1 10.5 us: shards(): factors = lax.all_to_all(message, 'seq', 0, 0, tiled=True)]
    all_to_all x0 -> x1, blocking collectives: none -> 34.6 us  [shuffle(): lax.all_to_all(array, ('dp', 'seq'), 0, 0, tiled=True, axis_index_groups=...]
    ppermute x4 -> x8, waiting for transfers between devices: 2.4 us -> 21.9 us  [the longest x2 18.3 us: gathered(): pieces.append(lax.ppermute(rows(array), 'dp', p.across_fold(step)))]
    pallas_call x0 -> x9, Pallas kernels: none -> 15.8 us  [call(): pl.pallas_call(kernel, out_shape=out_shape, in_specs=[SMEM if i in smem e...]
    dot_general x12 -> x0, matrix products: 9.11 us -> none  [the longest x1 1.9 us: shards(): jnp.einsum('qkmc,pikc->qpkmi', second_grad, first_freq, preferred_element...]
    ppermute x4 -> x8, starting transfers between devices: 12.1 us -> 3.29 us  [the longest x2 2.71 us: gathered(): pieces.append(lax.ppermute(rows(array), 'dp', p.across_fold(step)))]
    all_gather x1 -> x0, blocking collectives: 7.25 us -> none  [shards(): grad_filter = lax.all_gather(finished, 'dp', axis=2, tiled=True)]
  transfers between devices with their start and end apart: 9 -> 10, of which waited for: 5 -> 6; matrix products, arithmetic and copies ran while one was open for 16% -> 0% of each run, Pallas kernels for 0% -> 3%
where the time goes in v1:
time: 110 us; the launch traced here: 109 us
  blocking collectives  34.6 us (31%)
  waiting for transfers between devices  32.4 us (29%)
  Pallas kernels  15.8 us (14%)
  starting transfers between devices  15.2 us (14%)
  local copies, waits for them, and re-layouts  10.1 us (9%)
    all_to_all x1, blocking collectives, shuffle(): lax.all_to_all(array, ('dp', 'seq'), 0, 0, tiled=True, axis_index_groups=...  34.6 us
    ppermute x2, waiting for transfers between devices, gathered(): pieces.append(lax.ppermute(rows(array), 'dp', p.across_fold(step)))  18.3 us
    pallas_call x9, Pallas kernels, call(): pl.pallas_call(kernel, out_shape=out_shape, in_specs=[SMEM if i in smem e...  15.8 us
    all_to_all x1, waiting for transfers between devices, shards(): factors = lax.all_to_all(message, 'seq', 0, 0, tiled=True)  10.5 us
    unnamed x30, local copies, waits for them, and re-layouts  10.1 us
    all_to_all x1, starting transfers between devices, shards(): factors = lax.all_to_all(message, 'seq', 0, 0, tiled=True)  7.29 us
    all_to_all x1, starting transfers between devices, shuffle(): lax.all_to_all(array, ('dp', 'seq'), 0, 0, tiled=True, axis_index_groups=...  4.66 us
    ppermute x6, waiting for transfers between devices, swap(): return lax.ppermute(array, 'dp', p.across_cores())  3.64 us
  transfers between devices with their start and end apart: 10, of which 6 were waited for; matrix products, arithmetic and copies ran while one was open for 0% of the time, Pallas kernels for 3%

profile of v1, /device:TPU:0, one launch (start us, length us, event | category | flops | bytes accessed | tf_op | source)
XLA Modules:
  0.0 109.2 jit_solution(9314229026176369401)
XLA Ops:
  0.7 0.1 pad_add_fusion.place
  0.7 0.0 copy-start.6
  0.7 1.0 copy-done.6
  1.7 0.0 copy-start.9
  1.7 0.8 copy-done.9
  2.6 0.0 copy-start.10
  2.6 0.8 copy-done.10
  3.4 0.0 copy-start.11
  3.4 0.8 copy-done.11
  4.2 0.0 copy-start.12
  4.2 0.8 copy-done.12
  4.9 0.0 copy-start.7
  4.9 0.0 copy-start.8
  4.9 2.0 %factor_message.1 = bf16[8,192,128]{2,1,0:T(8,128)(2,1)} custom-call(s32[2]{0:T(128)S(1)} %pad_add_fusion.place, bf16[128,1536]{1,0:T(8,128)(2,1)S(1)} %bitcast.32, bf16[2,128,128]{2,1,0:T(8,128)(2,1)S(1)} %bitcast.35, bf16[2,128,128]{2,1,0:T(8,128)(2,1)S(1)} %bitcast.36, bf16[2,64,16]{2,1,0:T(8,128)(2,1)S(1)} %bitcast.40, bf16[2,64,16]{2,1,0:T(8,128)(2,1)S(1)} %bitcast.41), custom_call_target="tpu_custom_call" | custom-call | tf_op jit(solution)/shard_map/factor_message/pallas_call | solution.py:97
  7.0 7.3 %all-to-all-start.1 = ((bf16[8,192,128]{2,1,0:T(8,128)(2,1)}), bf16[8,192,128]{2,1,0:T(8,128)(2,1)S(1)}, u32[]{:S(2)}, u32[]{:S(2)}) async-start(bf16[8,192,128]{2,1,0:T(8,128)(2,1)} %factor_message.1), calls=%async_computation.1 | async-start | bytes 786432 | tf_op jit(solution)/shard_map/all_to_all | solution.py:545
  14.2 0.0 copy-done.7
  14.3 0.0 copy-done.8
  14.3 1.1 %token_message.1 = bf16[16,192,128]{2,1,0:T(8,128)(2,1)} custom-call(bf16[128,1536]{1,0:T(8,128)(2,1)S(1)} %bitcast.33, bf16[128,1536]{1,0:T(8,128)(2,1)S(1)} %bitcast.34), custom_call_target="tpu_custom_call" | custom-call | tf_op jit(solution)/shard_map/token_message/pallas_call | solution.py:97
  15.4 0.0 copy-start.13
  15.4 0.0 copy-start.14
  15.4 10.5 %all-to-all-done.1.refs_0_ = bf16[8,192,128]{2,1,0:T(8,128)(2,1)S(1)} async-done(((bf16[8,192,128]{2,1,0:T(8,128)(2,1)}), bf16[8,192,128]{2,1,0:T(8,128)(2,1)S(1)}, u32[]{:S(2)}, u32[]{:S(2)}) %all-to-all-start.1) | async-done | bytes 393248 | tf_op jit(solution)/shard_map/all_to_all | solution.py:545
  25.9 4.7 %all-to-all-start = ((bf16[16,192,128]{2,1,0:T(8,128)(2,1)}), bf16[16,192,128]{2,1,0:T(8,128)(2,1)S(1)}, u32[]{:S(2)}, u32[]{:S(2)}) async-start(bf16[16,192,128]{2,1,0:T(8,128)(2,1)} %token_message.1), calls=%async_computation | async-start | bytes 1572864 | tf_op jit(solution)/shard_map/all_to_all | solution.py:506
  30.6 2.0 %collective-permute-start = (bf16[8,144,128]{2,1,0:T(8,128)(2,1)S(1)}, bf16[8,144,128]{2,1,0:T(8,128)(2,1)S(1)}, u32[]{:S(2)}, u32[]{:S(2)}) collective-permute-start(bf16[8,144,128]{2,1,0:T(8,128)(2,1)S(1)} %slice.4), channel_id=1, source_target_pairs={{0,16},{8,24},{16,0},{24,8},{1,17},{9,25},{17,1},{25,9},{2,18},{10... | collective-permute-start | bytes 884744 | tf_op jit(solution)/shard_map/ppermute | solution.py:516
  32.6 0.0 collective-permute-start.1
  32.6 13.6 %collective-permute-done.refs_1_ = bf16[8,144,128]{2,1,0:T(8,128)(2,1)S(1)} collective-permute-done((bf16[8,144,128]{2,1,0:T(8,128)(2,1)S(1)}, bf16[8,144,128]{2,1,0:T(8,128)(2,1)S(1)}, u32[]{:S(2)}, u32[]{:S(2)}) %collective-permute-start) | collective-permute-done | bytes 294944 | tf_op jit(solution)/shard_map/ppermute | solution.py:516
  46.2 0.0 collective-permute-start.2
  46.2 0.0 copy-done.13
  46.2 0.0 copy-done.14
  46.2 0.1 fusion
  46.3 0.1 pad_maximum_fusion.taps
  46.4 0.0 collective-permute-done.1.refs_2_
  46.4 1.4 %collective-permute-done.2.refs_3_ = bf16[8,144,128]{2,1,0:T(8,128)(2,1)S(1)} collective-permute-done((bf16[8,144,128]{2,1,0:T(8,128)(2,1)S(1)}, bf16[8,144,128]{2,1,0:T(8,128)(2,1)S(1)}, u32[]{:S(2)}, u32[]{:S(2)}) %collective-permute-start.2) | collective-permute-done | bytes 294944 | tf_op jit(solution)/shard_map/ppermute | solution.py:511
  47.8 1.0 prepare.1
  48.7 0.0 copy-start.2
  48.7 0.8 copy-done.2
  49.5 0.0 copy-start.4
  49.5 0.8 copy-done.4
  50.3 0.5 block_factors.1
  50.8 0.0 copy-start
  50.8 1.0 copy-done
  51.8 0.0 all-to-all-done.tokens_in
  51.8 0.0 copy-start.1
  51.8 1.2 %copy-done.1 = bf16[8,256,256]{2,1,0:T(8,128)(2,1)S(1)} copy-done((bf16[8,256,256]{2,1,0:T(8,128)(2,1)S(1)}, bf16[8,256,256]{2,1,0:T(8,128)(2,1)}, u32[]{:S(2)}) %copy-start.1) | copy-done | bytes 1048600
  53.0 0.0 copy-start.3
  53.0 1.0 copy-done.3
  54.1 0.0 copy-start.5
  54.1 1.0 copy-done.5
  55.1 8.2 %mixer.1 = (bf16[16,96,128]{2,1,0:T(8,128)(2,1)S(1)}, bf16[2,8,176,128]{3,2,1,0:T(8,128)(2,1)S(1)}, bf16[2,8,176,128]{3,2,1,0:T(8,128)(2,1)S(1)}, bf16[128,128]{1,0:T(8,128)(2,1)S(1)}, bf16[128,128]{1,0:T(8,128)(2,1)S(1)}) custom-call(s32[2]{0:T(128)S(1)} %pad_add_fusion.place, bf16[16,192,128]{2,1,0:T(8,128)(2,1)S(1)} %all-to-all-done.tokens_in, ...), custom_call_target="tpu_custom_call" | custom-call | tf_op jit(solution)/shard_map/mixer/pallas_call | solution.py:97
  63.3 0.2 collective-permute-start.3
  63.5 0.4 collective-permute-start.4
  63.9 1.7 %collective-permute-done.4 = bf16[128,128]{1,0:T(8,128)(2,1)S(1)} collective-permute-done((bf16[128,128]{1,0:T(8,128)(2,1)S(1)}, bf16[128,128]{1,0:T(8,128)(2,1)S(1)}, u32[]{:S(2)}, u32[]{:S(2)}) %collective-permute-start.4) | collective-permute-done | bytes 32800 | tf_op jit(solution)/shard_map/ppermute | solution.py:511
  65.6 0.0 collective-permute-done.3.got
  65.6 0.2 add_cores.1
  65.8 34.6 %all_to_all.15.got = bf16[16,272,128]{2,1,0:T(8,128)(2,1)S(1)} all-to-all(bf16[16,272,128]{2,1,0:T(8,128)(2,1)S(1)} %add_cores.1), channel_id=1, replica_groups={{0,1,2,3,4,5,6,7,16,17,18,19,20,21,22,23},{8,9,10,11,12,13,14,15,24,25,..., dimensions={0} | all-to-all | bytes 2228224 | tf_op jit(solution)/shard_map/all_to_all | solution.py:506
  100.4 0.1 sum_sources.1.refs_0_
  100.5 0.7 collective-permute-start.5
  101.2 0.0 collective-permute-start.6
  101.2 4.7 %collective-permute-done.5.refs_1_ = bf16[656,128]{1,0:T(8,128)(2,1)S(1)} collective-permute-done((bf16[656,128]{1,0:T(8,128)(2,1)S(1)}, bf16[656,128]{1,0:T(8,128)(2,1)S(1)}, u32[]{:S(2)}, u32[]{:S(2)}) %collective-permute-start.5) | collective-permute-done | bytes 167968 | tf_op jit(solution)/shard_map/ppermute | solution.py:516
  105.9 0.0 collective-permute-start.7
  105.9 0.9 token_grad.1
  106.8 0.0 collective-permute-done.6.refs_2_
  106.8 0.5 collective-permute-done.7.refs_3_
  107.3 1.9 %finish.1 = (bf16[2,128,128]{2,1,0:T(8,128)(2,1)}, bf16[2,128,128]{2,1,0:T(8,128)(2,1)}, bf16[128,1536]{1,0:T(8,128)(2,1)}, f32[3,1536]{1,0:T(4,128)}, f32[3,153...) custom-call(s32[2]{0:T(128)S(1)} %pad_add_fusion.place, ...), custom_call_target="tpu_custom_call" | custom-call | tf_op jit(solution)/shard_map/finish/pallas_call | solution.py:97
  (1 shorter events, 0.0 us)
Async XLA Ops:
  0.7 1.0 copy-start.6
  1.7 0.8 copy-start.9
  2.6 0.8 copy-start.10
  3.4 0.8 copy-start.11
  4.2 0.8 copy-start.12
  4.9 9.3 %copy-start.7 = (bf16[1,128,1536]{2,1,0:T(8,128)(2,1)S(1)}, bf16[1,128,1536]{2,1,0:T(8,128)(2,1)}, u32[]{:S(2)}) copy-start(bf16[1,128,1536]{2,1,0:T(8,128)(2,1)} %param.9) | copy-start | bytes 1179652
  4.9 9.3 %copy-start.8 = (bf16[1,128,1536]{2,1,0:T(8,128)(2,1)S(1)}, bf16[1,128,1536]{2,1,0:T(8,128)(2,1)}, u32[]{:S(2)}) copy-start(bf16[1,128,1536]{2,1,0:T(8,128)(2,1)} %param.10) | copy-start | bytes 1179652
  7.0 19.0 %all-to-all-start.1 = ((bf16[8,192,128]{2,1,0:T(8,128)(2,1)}), bf16[8,192,128]{2,1,0:T(8,128)(2,1)S(1)}, u32[]{:S(2)}, u32[]{:S(2)}) async-start(bf16[8,192,128]{2,1,0:T(8,128)(2,1)} %factor_message.1), calls=%async_computation.1 | async-start | bytes 786432 | tf_op jit(solution)/shard_map/all_to_all | solution.py:545
  15.4 30.8 %copy-start.13 = (f32[3,1536]{1,0:T(4,128)S(1)}, f32[3,1536]{1,0:T(4,128)}, u32[]{:S(2)}) copy-start(f32[3,1536]{1,0:T(4,128)} %param.11) | copy-start | bytes 55300
  15.4 30.8 %copy-start.14 = (f32[3,1536]{1,0:T(4,128)S(1)}, f32[3,1536]{1,0:T(4,128)}, u32[]{:S(2)}) copy-start(f32[3,1536]{1,0:T(4,128)} %param.12) | copy-start | bytes 55300
  25.9 25.8 %all-to-all-start = ((bf16[16,192,128]{2,1,0:T(8,128)(2,1)}), bf16[16,192,128]{2,1,0:T(8,128)(2,1)S(1)}, u32[]{:S(2)}, u32[]{:S(2)}) async-start(bf16[16,192,128]{2,1,0:T(8,128)(2,1)} %token_message.1), calls=%async_computation | async-start | bytes 1572864 | tf_op jit(solution)/shard_map/all_to_all | solution.py:506
  30.6 15.6 %collective-permute-start = (bf16[8,144,128]{2,1,0:T(8,128)(2,1)S(1)}, bf16[8,144,128]{2,1,0:T(8,128)(2,1)S(1)}, u32[]{:S(2)}, u32[]{:S(2)}) collective-permute-start(bf16[8,144,128]{2,1,0:T(8,128)(2,1)S(1)} %slice.4), channel_id=1, source_target_pairs={{0,16},{8,24},{16,0},{24,8},{1,17},{9,25},{17,1},{25,9},{2,18},{10... | collective-permute-start | bytes 884744 | tf_op jit(solution)/shard_map/ppermute | solution.py:516
  32.6 13.7 %collective-permute-start.1 = (bf16[8,192,128]{2,1,0:T(8,128)(2,1)S(1)}, bf16[8,192,128]{2,1,0:T(8,128)(2,1)S(1)}, u32[]{:S(2)}, u32[]{:S(2)}) collective-permute-start(bf16[8,192,128]{2,1,0:T(8,128)(2,1)S(1)} %all-to-all-done.1.refs_0_), channel_id=1, source_target_pairs={{0,8},{8,0},{16,24},{24,16},{1,9},{9,1},{17,25},{25,17},{2,10},{10... | collective-permute-start | bytes 1179656 | tf_op jit(solution)/shard_map/ppermute | solution.py:511
  46.2 1.6 %collective-permute-start.2 = (bf16[8,144,128]{2,1,0:T(8,128)(2,1)S(1)}, bf16[8,144,128]{2,1,0:T(8,128)(2,1)S(1)}, u32[]{:S(2)}, u32[]{:S(2)}) collective-permute-start(bf16[8,144,128]{2,1,0:T(8,128)(2,1)S(1)} %collective-permute-done.refs_1_), channel_id=1, source_target_pairs={{0,8},{8,0},{16,24},{24,16},{1,9},{9,1},{17,25},{25,17},{2,10},{10... | collective-permute-start | bytes 884744 | tf_op jit(solution)/shard_map/ppermute | solution.py:511
  48.7 0.8 copy-start.2
  49.5 0.8 copy-start.4
  50.8 1.0 copy-start
  51.8 1.2 %copy-start.1 = (bf16[8,256,256]{2,1,0:T(8,128)(2,1)S(1)}, bf16[8,256,256]{2,1,0:T(8,128)(2,1)}, u32[]{:S(2)}) copy-start(bf16[8,256,256]{2,1,0:T(8,128)(2,1)} %copy-done) | copy-start | bytes 3145732
  53.0 1.0 copy-start.3
  54.1 1.0 copy-start.5
  63.3 2.3 %collective-permute-start.3 = (bf16[2,8,176,128]{3,2,1,0:T(8,128)(2,1)S(1)}, bf16[2,8,176,128]{3,2,1,0:T(8,128)(2,1)S(1)}, u32[]{:S(2)}, u32[]{:S(2)}) collective-permute-start(bf16[2,8,176,128]{3,2,1,0:T(8,128)(2,1)S(1)} %get-tuple-element.34), channel_id=1, source_target_pairs={{0,8},{8,0},{16,24},{24,16},{1,9},{9,1},{17,25},{25,17},{2,10},{10... | collective-permute-start | bytes 2162696 | tf_op jit(solution)/shard_map/ppermute | solution.py:511
  63.5 2.1 %collective-permute-start.4 = (bf16[128,128]{1,0:T(8,128)(2,1)S(1)}, bf16[128,128]{1,0:T(8,128)(2,1)S(1)}, u32[]{:S(2)}, u32[]{:S(2)}) collective-permute-start(bf16[128,128]{1,0:T(8,128)(2,1)S(1)} %get-tuple-element.36), channel_id=1, source_target_pairs={{0,8},{8,0},{16,24},{24,16},{1,9},{9,1},{17,25},{25,17},{2,10},{10... | collective-permute-start | bytes 98312 | tf_op jit(solution)/shard_map/ppermute | solution.py:511
  100.5 5.4 %collective-permute-start.5 = (bf16[656,128]{1,0:T(8,128)(2,1)S(1)}, bf16[656,128]{1,0:T(8,128)(2,1)S(1)}, u32[]{:S(2)}, u32[]{:S(2)}) collective-permute-start(bf16[656,128]{1,0:T(8,128)(2,1)S(1)} %sum_sources.1.refs_0_), channel_id=1, source_target_pairs={{0,16},{8,24},{16,0},{24,8},{1,17},{9,25},{17,1},{25,9},{2,18},{10... | collective-permute-start | bytes 503816 | tf_op jit(solution)/shard_map/ppermute | solution.py:516
  101.2 5.6 %collective-permute-start.6 = (bf16[656,128]{1,0:T(8,128)(2,1)S(1)}, bf16[656,128]{1,0:T(8,128)(2,1)S(1)}, u32[]{:S(2)}, u32[]{:S(2)}) collective-permute-start(bf16[656,128]{1,0:T(8,128)(2,1)S(1)} %sum_sources.1.refs_0_), channel_id=1, source_target_pairs={{0,8},{8,0},{16,24},{24,16},{1,9},{9,1},{17,25},{25,17},{2,10},{10... | collective-permute-start | bytes 503816 | tf_op jit(solution)/shard_map/ppermute | solution.py:511
  105.9 1.4 %collective-permute-start.7 = (bf16[656,128]{1,0:T(8,128)(2,1)S(1)}, bf16[656,128]{1,0:T(8,128)(2,1)S(1)}, u32[]{:S(2)}, u32[]{:S(2)}) collective-permute-start(bf16[656,128]{1,0:T(8,128)(2,1)S(1)} %collective-permute-done.5.refs_1_), channel_id=1, source_target_pairs={{0,8},{8,0},{16,24},{24,16},{1,9},{9,1},{17,25},{25,17},{2,10},{10... | collective-permute-start | bytes 503816 | tf_op jit(solution)/shard_map/ppermute | solution.py:511

commit v2 on v1

--- a/solution.py
+++ b/solution.py
@@ -92,7 +92,7 @@
     return lax.dot_general(a, b, (((ca,), (cb,)), ((), ())), preferred_element_type=F32)
 
 
-def call(kernel, out_shape, *args, scratch=(), smem=(), far=(), limit=16, name=None):
+def call(kernel, out_shape, *args, scratch=(), smem=(), far=(), limit=20, name=None):
     single = not isinstance(out_shape, (list, tuple))
     return pl.pallas_call(
         kernel,
@@ -426,36 +426,32 @@
     small_send[...] = small[1 - core]
 
 
-def add_kernel(p, grad_x, keep, got, small_keep, small_got, out):
-    w = p.width
-
+def add_kernel(p, keep, got, small_keep, small_got, out):
     def one_target(s):
         extra = (small_keep[s].astype(F32) + small_got[s].astype(F32)).astype(BF16)
         for h in range(p.fold):
             q = h * p.seq + s
-            out[q, 0:w] = grad_x[q]
-            out[q, w:] = (keep[h, s].astype(F32) + got[h, s].astype(F32)).astype(BF16)
+            out[q] = (keep[h, s].astype(F32) + got[h, s].astype(F32)).astype(BF16)
             first, last = 2 * p.blk - h * p.mrows, 2 * p.blk + p.yrows - h * p.mrows
             lo, hi = max(first, 0), min(last, p.mrows)
             if lo < hi:
-                out[q, w + lo : w + hi] = extra[lo - first : hi - first]
+                out[q, lo:hi] = extra[lo - first : hi - first]
 
     each(p.seq, one_target)
 
 
 def sum_kernel(p, got, out):
-    w = p.width
-    total = got[0, w : w + p.mrows].astype(F32)
+    total = got[0, 0 : p.mrows].astype(F32)
     for q in range(1, p.members):
-        total += got[q, w : w + p.mrows].astype(F32)
+        total += got[q, 0 : p.mrows].astype(F32)
     out[0 : p.mrows] = total.astype(BF16)
     for q in range(p.members):
         at = p.mrows + q * p.orows
-        out[at : at + p.orows] = got[q, w + p.mrows :]
+        out[at : at + p.orows] = got[q, p.mrows :]
 
 
 def grad_x_kernel(p, got, out):
-    rows = jnp.concatenate([got[q, 0 : p.width] for q in range(p.members)], axis=0)
+    rows = jnp.concatenate([got[q] for q in range(p.members)], axis=0)
     out[...] = rows.T
 
 
@@ -540,10 +536,21 @@
         ],
         smem=(0,),
         far=range(1, 1 + len(far)),
+        limit=60,
         name="factor_message",
     )
     factors = lax.all_to_all(message, "seq", 0, 0, tiled=True)
     pieces = gathered(factors, lambda a: a[:, : p.mrows])
+
+    message = call(
+        functools.partial(token_message_kernel, p),
+        shape(p.members, 2 * p.width, blk),
+        tokens[0],
+        upstream[0],
+        name="token_message",
+    )
+    received = shuffle(message)
+    pieces, received = lax.optimization_barrier((pieces, received))
     one, four, small, filt = call(
         functools.partial(prepare_kernel, p),
         [
@@ -565,18 +572,10 @@
         functools.partial(block_factor_kernel, p),
         [shape(p.kgroups, 2 * p.dim, 2 * p.dim)] * 2,
         small.reshape(2, blk, 2 * pairs),
-        limit=48 if p.streamed else 16,
+        limit=48 if p.streamed else 20,
         name="block_factors",
     )
 
-    message = call(
-        functools.partial(token_message_kernel, p),
-        shape(p.members, 2 * p.width, blk),
-        tokens[0],
-        upstream[0],
-        name="token_message",
-    )
-    received = shuffle(message)
     start = (h_at * p.seq + seq_at) * p.width
     taps = jnp.concatenate([conv_value, conv_gate], axis=0)
     taps = lax.dynamic_slice_in_dim(taps, start, p.width, 1)
@@ -625,8 +624,7 @@
 
     message = call(
         functools.partial(add_kernel, p),
-        shape(p.members, p.width + p.share, blk),
-        grad_x,
+        shape(p.members, p.share, blk),
         keep,
         swap(send),
         small_keep.reshape(p.seq, p.yrows, blk),
@@ -634,6 +632,8 @@
         name="add_cores",
     )
     received = shuffle(message)
+    received, grad_x = lax.optimization_barrier((received, grad_x))
+    grad_x = shuffle(grad_x)
     sums = call(
         functools.partial(sum_kernel, p),
         shape(p.mrows + p.members * p.orows, blk),
@@ -647,7 +647,7 @@
         sums = total.astype(BF16)
     pieces = gathered(sums, lambda a: a)
     token_grad = call(
-        functools.partial(grad_x_kernel, p), shape(blk, p.channels), received, name="token_grad"
+        functools.partial(grad_x_kernel, p), shape(blk, p.channels), grad_x, name="token_grad"
     )
     grad_one, grad_four, grad_filter, sum_value, sum_gate, *small = call(
         functools.partial(finish_kernel, p),

time: 110 us -> 101 us (0.918)
  blocking collectives: 34.6 us -> 23.9 us
  local copies, waits for them, and re-layouts: 10.1 us -> 0.05 us
  waiting for transfers between devices: 32.4 us -> 38.1 us
  starting transfers between devices: 15.2 us -> 20.1 us
  Pallas kernels: 15.8 us -> 17.1 us
    all_to_all x1, blocking collectives: 34.6 us -> 23.9 us  [shuffle(): lax.all_to_all(array, ('dp', 'seq'), 0, 0, tiled=True, axis_index_groups=...]
    unnamed x30 -> x10, local copies, waits for them, and re-layouts: 10.1 us -> 0.03 us
    all_to_all x1 -> x2, starting transfers between devices: 4.66 us -> 8.21 us  [shuffle(): lax.all_to_all(array, ('dp', 'seq'), 0, 0, tiled=True, axis_index_groups=...]
    all_to_all x1 -> x2, waiting for transfers between devices: 0.01 us -> 3.19 us  [shuffle(): lax.all_to_all(array, ('dp', 'seq'), 0, 0, tiled=True, axis_index_groups=...]
    ppermute x2, waiting for transfers between devices: 18.3 us -> 19.9 us  [gathered(): pieces.append(lax.ppermute(rows(array), 'dp', p.across_fold(step)))]
    pallas_call x9, Pallas kernels: 15.8 us -> 17.1 us  [call(): pl.pallas_call(kernel, out_shape=out_shape, in_specs=[SMEM if i in smem e...]
    ppermute x2, starting transfers between devices: 2.71 us -> 3.9 us  [gathered(): pieces.append(lax.ppermute(rows(array), 'dp', p.across_fold(step)))]
  transfers between devices with their start and end apart: 10 -> 11, of which waited for: 6 -> 7; matrix products, arithmetic and copies ran while one was open for 0% -> 0% of each run, Pallas kernels for 3% -> 3%
where the time goes in v2:
time: 101 us
  waiting for transfers between devices  38.1 us (38%)
  blocking collectives  23.9 us (24%)
  starting transfers between devices  20.1 us (20%)
  Pallas kernels  17.1 us (17%)
    all_to_all x1, blocking collectives, shuffle(): lax.all_to_all(array, ('dp', 'seq'), 0, 0, tiled=True, axis_index_groups=...  23.9 us
    ppermute x2, waiting for transfers between devices, gathered(): pieces.append(lax.ppermute(rows(array), 'dp', p.across_fold(step)))  19.9 us
    pallas_call x9, Pallas kernels, call(): pl.pallas_call(kernel, out_shape=out_shape, in_specs=[SMEM if i in smem e...  17.1 us
    all_to_all x1, waiting for transfers between devices, shards(): factors = lax.all_to_all(message, 'seq', 0, 0, tiled=True)  10.5 us
    all_to_all x2, starting transfers between devices, shuffle(): lax.all_to_all(array, ('dp', 'seq'), 0, 0, tiled=True, axis_index_groups=...  8.21 us
    all_to_all x1, starting transfers between devices, shards(): factors = lax.all_to_all(message, 'seq', 0, 0, tiled=True)  7.42 us
    ppermute x6, waiting for transfers between devices, swap(): return lax.ppermute(array, 'dp', p.across_cores())  4.54 us
    ppermute x2, starting transfers between devices, gathered(): pieces.append(lax.ppermute(rows(array), 'dp', p.across_fold(step)))  3.9 us
  transfers between devices with their start and end apart: 11, of which 7 were waited for; matrix products, arithmetic and copies ran while one was open for 0% of the time, Pallas kernels for 3%

profile of v2, /device:TPU:0, one launch (start us, length us, event | category | flops | bytes accessed | tf_op | source)
XLA Modules:
  0.0 100.8 jit_solution(14281269081151431907)
XLA Ops:
  0.7 0.6 pad_add_fusion.place
  1.3 2.7 %factor_message.1 = bf16[8,192,128]{2,1,0:T(8,128)(2,1)} custom-call(s32[2]{0:T(128)} %pad_add_fusion.place, bf16[128,1536]{1,0:T(8,128)(2,1)} %bitcast.37, bf16[2,128,128]{2,1,0:T(8,128)(2,1)} %bitcast.39, bf16[2,128,128]{2,1,0:T(8,128)(2,1)} %bitcast.40, bf16[2,64,16]{2,1,0:T(8,128)(2,1)} %bitcast.41, bf16[2,64,16]{2,1,0:T(8,128)(2,1)} %bitcast.42), custom_call_target="tpu_custom_call" | custom-call | tf_op jit(solution)/shard_map/factor_message/pallas_call | solution.py:97
  3.9 0.0 copy-start
  3.9 0.0 copy-start.1
  4.0 7.4 %all-to-all-start = ((bf16[8,192,128]{2,1,0:T(8,128)(2,1)}), bf16[8,192,128]{2,1,0:T(8,128)(2,1)S(1)}, u32[]{:S(2)}, u32[]{:S(2)}) async-start(bf16[8,192,128]{2,1,0:T(8,128)(2,1)} %factor_message.1), calls=%async_computation | async-start | bytes 786432 | tf_op jit(solution)/shard_map/all_to_all | solution.py:542
  11.4 0.0 copy-done
  11.4 0.0 copy-done.1
  11.4 1.1 %token_message.1 = bf16[16,192,128]{2,1,0:T(8,128)(2,1)} custom-call(bf16[128,1536]{1,0:T(8,128)(2,1)S(1)} %bitcast.32, bf16[128,1536]{1,0:T(8,128)(2,1)S(1)} %bitcast.33), custom_call_target="tpu_custom_call" | custom-call | tf_op jit(solution)/shard_map/token_message/pallas_call | solution.py:97
  12.6 10.5 %all-to-all-done.refs_0_ = bf16[8,192,128]{2,1,0:T(8,128)(2,1)S(1)} async-done(((bf16[8,192,128]{2,1,0:T(8,128)(2,1)}), bf16[8,192,128]{2,1,0:T(8,128)(2,1)S(1)}, u32[]{:S(2)}, u32[]{:S(2)}) %all-to-all-start) | async-done | bytes 393248 | tf_op jit(solution)/shard_map/all_to_all | solution.py:542
  23.1 4.7 %all-to-all-start.1 = ((bf16[16,192,128]{2,1,0:T(8,128)(2,1)}), bf16[16,192,128]{2,1,0:T(8,128)(2,1)S(1)}, u32[]{:S(2)}, u32[]{:S(2)}) async-start(bf16[16,192,128]{2,1,0:T(8,128)(2,1)} %token_message.1), calls=%async_computation.1 | async-start | bytes 1572864 | tf_op jit(solution)/shard_map/all_to_all | solution.py:502
  27.7 0.0 copy-start.3
  27.8 0.0 copy-start.4
  27.8 2.0 %collective-permute-start = (bf16[8,144,128]{2,1,0:T(8,128)(2,1)S(1)}, bf16[8,144,128]{2,1,0:T(8,128)(2,1)S(1)}, u32[]{:S(2)}, u32[]{:S(2)}) collective-permute-start(bf16[8,144,128]{2,1,0:T(8,128)(2,1)S(1)} %slice.4), channel_id=1, source_target_pairs={{0,16},{8,24},{16,0},{24,8},{1,17},{9,25},{17,1},{25,9},{2,18},{10... | collective-permute-start | bytes 884744 | tf_op jit(solution)/shard_map/ppermute | solution.py:512
  29.8 0.0 collective-permute-start.1
  29.8 13.5 %collective-permute-done.refs_1_ = bf16[8,144,128]{2,1,0:T(8,128)(2,1)S(1)} collective-permute-done((bf16[8,144,128]{2,1,0:T(8,128)(2,1)S(1)}, bf16[8,144,128]{2,1,0:T(8,128)(2,1)S(1)}, u32[]{:S(2)}, u32[]{:S(2)}) %collective-permute-start) | collective-permute-done | bytes 294944 | tf_op jit(solution)/shard_map/ppermute | solution.py:512
  43.3 0.0 collective-permute-start.2
  43.3 0.0 copy-done.3
  43.3 0.0 copy-done.4
  43.3 0.1 fusion
  43.4 0.0 copy-start.2
  43.4 0.1 pad_maximum_fusion.taps
  43.5 0.0 collective-permute-done.1.refs_2_
  43.5 1.4 %collective-permute-done.2.refs_3_ = bf16[8,144,128]{2,1,0:T(8,128)(2,1)S(1)} collective-permute-done((bf16[8,144,128]{2,1,0:T(8,128)(2,1)S(1)}, bf16[8,144,128]{2,1,0:T(8,128)(2,1)S(1)}, u32[]{:S(2)}, u32[]{:S(2)}) %collective-permute-start.2) | collective-permute-done | bytes 294944 | tf_op jit(solution)/shard_map/ppermute | solution.py:507
  44.9 3.2 %all-to-all-done.1.tokens_in = bf16[16,192,128]{2,1,0:T(8,128)(2,1)S(1)} async-done(((bf16[16,192,128]{2,1,0:T(8,128)(2,1)}), bf16[16,192,128]{2,1,0:T(8,128)(2,1)S(1)}, u32[]{:S(2)}, u32[]{:S(2)}) %all-to-all-start.1) | async-done | bytes 786464 | tf_op jit(solution)/shard_map/all_to_all | solution.py:502
  48.1 0.0 copy-done.2
  48.1 1.0 prepare.1
  49.0 0.5 block_factors.1
  49.5 8.9 %mixer.1 = (bf16[16,96,128]{2,1,0:T(8,128)(2,1)}, bf16[2,8,176,128]{3,2,1,0:T(8,128)(2,1)S(1)}, bf16[2,8,176,128]{3,2,1,0:T(8,128)(2,1)S(1)}, bf16[128,128]{1,0:T(8,128)(2,1)S(1)}, bf16[128,128]{1,0:T(8,128)(2,1)S(1)}) custom-call(s32[2]{0:T(128)S(1)} %copy-done.2, bf16[16,192,128]{2,1,0:T(8,128)(2,1)S(1)} %all-to-all-done.1.tokens_in, ...), custom_call_target="tpu_custom_call" | custom-call | tf_op jit(solution)/shard_map/mixer/pallas_call | solution.py:97
  58.4 0.0 collective-permute-start.3
  58.4 0.5 collective-permute-start.4
  58.9 1.7 %collective-permute-done.4 = bf16[128,128]{1,0:T(8,128)(2,1)S(1)} collective-permute-done((bf16[128,128]{1,0:T(8,128)(2,1)S(1)}, bf16[128,128]{1,0:T(8,128)(2,1)S(1)}, u32[]{:S(2)}, u32[]{:S(2)}) %collective-permute-start.4) | collective-permute-done | bytes 32800 | tf_op jit(solution)/shard_map/ppermute | solution.py:507
  60.6 0.0 collective-permute-done.3.got
  60.6 0.2 add_cores.1
  60.8 23.9 %all_to_all.20.got = bf16[16,176,128]{2,1,0:T(8,128)(2,1)S(1)} all-to-all(bf16[16,176,128]{2,1,0:T(8,128)(2,1)S(1)} %add_cores.1), channel_id=1, replica_groups={{0,1,2,3,4,5,6,7,16,17,18,19,20,21,22,23},{8,9,10,11,12,13,14,15,24,25,..., dimensions={0} | all-to-all | bytes 1441792 | tf_op jit(solution)/shard_map/all_to_all | solution.py:502
  84.7 3.6 %all-to-all-start.3 = ((bf16[16,96,128]{2,1,0:T(8,128)(2,1)}), bf16[16,96,128]{2,1,0:T(8,128)(2,1)S(1)}, u32[]{:S(2)}, u32[]{:S(2)}) async-start(bf16[16,96,128]{2,1,0:T(8,128)(2,1)} %get-tuple-element.49), calls=%async_computation.3 | async-start | bytes 786432 | tf_op jit(solution)/shard_map/all_to_all | solution.py:502
  88.2 0.1 sum_sources.1.refs_0_
  88.3 1.9 %collective-permute-start.5 = (bf16[656,128]{1,0:T(8,128)(2,1)S(1)}, bf16[656,128]{1,0:T(8,128)(2,1)S(1)}, u32[]{:S(2)}, u32[]{:S(2)}) collective-permute-start(bf16[656,128]{1,0:T(8,128)(2,1)S(1)} %sum_sources.1.refs_0_), channel_id=1, source_target_pairs={{0,16},{8,24},{16,0},{24,8},{1,17},{9,25},{17,1},{25,9},{2,18},{10... | collective-permute-start | bytes 503816 | tf_op jit(solution)/shard_map/ppermute | solution.py:512
  90.2 0.0 collective-permute-start.6
  90.2 6.3 %collective-permute-done.5.refs_1_ = bf16[656,128]{1,0:T(8,128)(2,1)S(1)} collective-permute-done((bf16[656,128]{1,0:T(8,128)(2,1)S(1)}, bf16[656,128]{1,0:T(8,128)(2,1)S(1)}, u32[]{:S(2)}, u32[]{:S(2)}) %collective-permute-start.5) | collective-permute-done | bytes 167968 | tf_op jit(solution)/shard_map/ppermute | solution.py:512
  96.6 0.0 collective-permute-start.7
  96.6 0.0 collective-permute-done.6.refs_2_
  96.6 1.4 %collective-permute-done.7.refs_3_ = bf16[656,128]{1,0:T(8,128)(2,1)S(1)} collective-permute-done((bf16[656,128]{1,0:T(8,128)(2,1)S(1)}, bf16[656,128]{1,0:T(8,128)(2,1)S(1)}, u32[]{:S(2)}, u32[]{:S(2)}) %collective-permute-start.7) | collective-permute-done | bytes 167968 | tf_op jit(solution)/shard_map/ppermute | solution.py:507
  98.0 1.9 %finish.1 = (bf16[2,128,128]{2,1,0:T(8,128)(2,1)}, bf16[2,128,128]{2,1,0:T(8,128)(2,1)}, bf16[128,1536]{1,0:T(8,128)(2,1)}, f32[3,1536]{1,0:T(4,128)}, f32[3,153...) custom-call(s32[2]{0:T(128)S(1)} %copy-done.2, bf16[656,128]{1,0:T(8,128)(2,1)S(1)} %sum_sources.1.refs_0_, ...), custom_call_target="tpu_custom_call" | custom-call | tf_op jit(solution)/shard_map/finish/pallas_call | solution.py:97
  99.8 0.0 all-to-all-done.3.got
  99.9 0.9 token_grad.1
  (1 shorter events, 0.0 us)
Async XLA Ops:
  3.9 7.5 %copy-start = (bf16[1,128,1536]{2,1,0:T(8,128)(2,1)S(1)}, bf16[1,128,1536]{2,1,0:T(8,128)(2,1)}, u32[]{:S(2)}) copy-start(bf16[1,128,1536]{2,1,0:T(8,128)(2,1)} %param.9) | copy-start | bytes 1179652
  3.9 7.4 %copy-start.1 = (bf16[1,128,1536]{2,1,0:T(8,128)(2,1)S(1)}, bf16[1,128,1536]{2,1,0:T(8,128)(2,1)}, u32[]{:S(2)}) copy-start(bf16[1,128,1536]{2,1,0:T(8,128)(2,1)} %param.10) | copy-start | bytes 1179652
  4.0 19.1 %all-to-all-start = ((bf16[8,192,128]{2,1,0:T(8,128)(2,1)}), bf16[8,192,128]{2,1,0:T(8,128)(2,1)S(1)}, u32[]{:S(2)}, u32[]{:S(2)}) async-start(bf16[8,192,128]{2,1,0:T(8,128)(2,1)} %factor_message.1), calls=%async_computation | async-start | bytes 786432 | tf_op jit(solution)/shard_map/all_to_all | solution.py:542
  23.1 25.0 %all-to-all-start.1 = ((bf16[16,192,128]{2,1,0:T(8,128)(2,1)}), bf16[16,192,128]{2,1,0:T(8,128)(2,1)S(1)}, u32[]{:S(2)}, u32[]{:S(2)}) async-start(bf16[16,192,128]{2,1,0:T(8,128)(2,1)} %token_message.1), calls=%async_computation.1 | async-start | bytes 1572864 | tf_op jit(solution)/shard_map/all_to_all | solution.py:502
  27.7 15.6 %copy-start.3 = (f32[3,1536]{1,0:T(4,128)S(1)}, f32[3,1536]{1,0:T(4,128)}, u32[]{:S(2)}) copy-start(f32[3,1536]{1,0:T(4,128)} %param.11) | copy-start | bytes 55300
  27.8 15.6 %copy-start.4 = (f32[3,1536]{1,0:T(4,128)S(1)}, f32[3,1536]{1,0:T(4,128)}, u32[]{:S(2)}) copy-start(f32[3,1536]{1,0:T(4,128)} %param.12) | copy-start | bytes 55300
  27.8 15.5 %collective-permute-start = (bf16[8,144,128]{2,1,0:T(8,128)(2,1)S(1)}, bf16[8,144,128]{2,1,0:T(8,128)(2,1)S(1)}, u32[]{:S(2)}, u32[]{:S(2)}) collective-permute-start(bf16[8,144,128]{2,1,0:T(8,128)(2,1)S(1)} %slice.4), channel_id=1, source_target_pairs={{0,16},{8,24},{16,0},{24,8},{1,17},{9,25},{17,1},{25,9},{2,18},{10... | collective-permute-start | bytes 884744 | tf_op jit(solution)/shard_map/ppermute | solution.py:512
  29.8 13.7 %collective-permute-start.1 = (bf16[8,192,128]{2,1,0:T(8,128)(2,1)S(1)}, bf16[8,192,128]{2,1,0:T(8,128)(2,1)S(1)}, u32[]{:S(2)}, u32[]{:S(2)}) collective-permute-start(bf16[8,192,128]{2,1,0:T(8,128)(2,1)S(1)} %all-to-all-done.refs_0_), channel_id=1, source_target_pairs={{0,8},{8,0},{16,24},{24,16},{1,9},{9,1},{17,25},{25,17},{2,10},{10... | collective-permute-start | bytes 1179656 | tf_op jit(solution)/shard_map/ppermute | solution.py:507
  43.3 1.6 %collective-permute-start.2 = (bf16[8,144,128]{2,1,0:T(8,128)(2,1)S(1)}, bf16[8,144,128]{2,1,0:T(8,128)(2,1)S(1)}, u32[]{:S(2)}, u32[]{:S(2)}) collective-permute-start(bf16[8,144,128]{2,1,0:T(8,128)(2,1)S(1)} %collective-permute-done.refs_1_), channel_id=1, source_target_pairs={{0,8},{8,0},{16,24},{24,16},{1,9},{9,1},{17,25},{25,17},{2,10},{10... | collective-permute-start | bytes 884744 | tf_op jit(solution)/shard_map/ppermute | solution.py:507
  43.4 4.7 %copy-start.2 = (s32[2]{0:T(128)S(1)}, s32[2]{0:T(128)}, u32[]{:S(2)}) copy-start(s32[2]{0:T(128)} %pad_add_fusion.place) | copy-start | bytes 28
  58.4 2.2 %collective-permute-start.3 = (bf16[2,8,176,128]{3,2,1,0:T(8,128)(2,1)S(1)}, bf16[2,8,176,128]{3,2,1,0:T(8,128)(2,1)S(1)}, u32[]{:S(2)}, u32[]{:S(2)}) collective-permute-start(bf16[2,8,176,128]{3,2,1,0:T(8,128)(2,1)S(1)} %get-tuple-element.45), channel_id=1, source_target_pairs={{0,8},{8,0},{16,24},{24,16},{1,9},{9,1},{17,25},{25,17},{2,10},{10... | collective-permute-start | bytes 2162696 | tf_op jit(solution)/shard_map/ppermute | solution.py:507
  58.4 2.2 %collective-permute-start.4 = (bf16[128,128]{1,0:T(8,128)(2,1)S(1)}, bf16[128,128]{1,0:T(8,128)(2,1)S(1)}, u32[]{:S(2)}, u32[]{:S(2)}) collective-permute-start(bf16[128,128]{1,0:T(8,128)(2,1)S(1)} %get-tuple-element.47), channel_id=1, source_target_pairs={{0,8},{8,0},{16,24},{24,16},{1,9},{9,1},{17,25},{25,17},{2,10},{10... | collective-permute-start | bytes 98312 | tf_op jit(solution)/shard_map/ppermute | solution.py:507
  84.7 15.2 %all-to-all-start.3 = ((bf16[16,96,128]{2,1,0:T(8,128)(2,1)}), bf16[16,96,128]{2,1,0:T(8,128)(2,1)S(1)}, u32[]{:S(2)}, u32[]{:S(2)}) async-start(bf16[16,96,128]{2,1,0:T(8,128)(2,1)} %get-tuple-element.49), calls=%async_computation.3 | async-start | bytes 786432 | tf_op jit(solution)/shard_map/all_to_all | solution.py:502
  88.3 8.2 %collective-permute-start.5 = (bf16[656,128]{1,0:T(8,128)(2,1)S(1)}, bf16[656,128]{1,0:T(8,128)(2,1)S(1)}, u32[]{:S(2)}, u32[]{:S(2)}) collective-permute-start(bf16[656,128]{1,0:T(8,128)(2,1)S(1)} %sum_sources.1.refs_0_), channel_id=1, source_target_pairs={{0,16},{8,24},{16,0},{24,8},{1,17},{9,25},{17,1},{25,9},{2,18},{10... | collective-permute-start | bytes 503816 | tf_op jit(solution)/shard_map/ppermute | solution.py:512
  90.2 6.3 %collective-permute-start.6 = (bf16[656,128]{1,0:T(8,128)(2,1)S(1)}, bf16[656,128]{1,0:T(8,128)(2,1)S(1)}, u32[]{:S(2)}, u32[]{:S(2)}) collective-permute-start(bf16[656,128]{1,0:T(8,128)(2,1)S(1)} %sum_sources.1.refs_0_), channel_id=1, source_target_pairs={{0,8},{8,0},{16,24},{24,16},{1,9},{9,1},{17,25},{25,17},{2,10},{10... | collective-permute-start | bytes 503816 | tf_op jit(solution)/shard_map/ppermute | solution.py:507
  96.6 1.4 %collective-permute-start.7 = (bf16[656,128]{1,0:T(8,128)(2,1)S(1)}, bf16[656,128]{1,0:T(8,128)(2,1)S(1)}, u32[]{:S(2)}, u32[]{:S(2)}) collective-permute-start(bf16[656,128]{1,0:T(8,128)(2,1)S(1)} %collective-permute-done.5.refs_1_), channel_id=1, source_target_pairs={{0,8},{8,0},{16,24},{24,16},{1,9},{9,1},{17,25},{25,17},{2,10},{10... | collective-permute-start | bytes 503816 | tf_op jit(solution)/shard_map/ppermute | solution.py:507

commit v3 on v2

--- a/solution.py
+++ b/solution.py
@@ -11,7 +11,6 @@
 BF16 = jnp.bfloat16
 TILE = 16
 VMEM = pl.BlockSpec(memory_space=pltpu.VMEM)
-SMEM = pl.BlockSpec(memory_space=pltpu.SMEM)
 FAR = pl.BlockSpec(memory_space=pl.ANY)
 
 
@@ -76,8 +75,8 @@
         return [(d, (d + step * block) % self.dp) for d in range(self.dp)]
 
 
-def each(count, body):
-    if count <= 8:
+def each(count, body, unrolled=True):
+    if count <= 8 and unrolled:
         for i in range(count):
             body(i)
     else:
@@ -92,12 +91,12 @@
     return lax.dot_general(a, b, (((ca,), (cb,)), ((), ())), preferred_element_type=F32)
 
 
-def call(kernel, out_shape, *args, scratch=(), smem=(), far=(), limit=20, name=None):
+def call(kernel, out_shape, *args, scratch=(), far=(), limit=20, name=None):
     single = not isinstance(out_shape, (list, tuple))
     return pl.pallas_call(
         kernel,
         out_shape=out_shape,
-        in_specs=[SMEM if i in smem else FAR if i in far else VMEM for i in range(len(args))],
+        in_specs=[FAR if i in far else VMEM for i in range(len(args))],
         out_specs=VMEM if single else [VMEM] * len(out_shape),
         scratch_shapes=list(scratch),
         compiler_params=pltpu.CompilerParams(vmem_limit_bytes=limit * 2**20),
@@ -109,38 +108,46 @@
     return jax.ShapeDtypeStruct(dims, dtype)
 
 
-def factor_message_kernel(p, place, *refs):
+def place(p):
+    at = lax.axis_index("dp")
+    return (at // 2) % p.fold, at % 2
+
+
+def factor_message_kernel(p, *refs):
     count = 5 if p.direct else 4
     far, out, near, rows, turned, done = refs[:count], refs[count], refs[count + 1 : -3], *refs[-3:]
-    copies = [pltpu.make_async_copy(f, n, done.at[i]) for i, (f, n) in enumerate(zip(far, near))]
+    h, core = place(p)
+    part_width = p.seq * p.width
+    sources = [far[0].at[:, pl.ds(pl.multiple_of(h * part_width, p.blk), part_width)]]
+    sources += [f.at[core] for f in far[1:]]
+    copies = [pltpu.make_async_copy(f, n, done.at[i]) for i, (f, n) in enumerate(zip(sources, near))]
     for copy in copies:
         copy.start()
-    h, core = place[0], place[1]
     filt, one, four = near[:3]
     for copy in copies[1:]:
         copy.wait()
-    for part in range(2):
-        base = part * p.half
-        rows[base : base + p.blk] = one[part]
-        rows[base + p.blk : base + 2 * p.blk] = four[part]
-        if p.direct:
-            small = jnp.concatenate([near[3][part], near[4][part]], axis=0).T
-        else:
-            small = near[3][part]
-        rows[base + 2 * p.blk : base + 2 * p.blk + p.yrows] = small
-        pad = p.half - 2 * p.blk - p.yrows
-        if pad:
-            rows[base + p.half - pad : base + p.half] = jnp.zeros((pad, p.blk), BF16)
-    mine = rows[rows_at(core * p.half + h * p.mrows, p.mrows)]
+    rows[0 : p.blk] = one[...]
+    rows[p.blk : 2 * p.blk] = four[...]
+    if p.direct:
+        small = jnp.concatenate([near[3][...], near[4][...]], axis=0).T
+    else:
+        small = near[3][...]
+    rows[2 * p.blk : 2 * p.blk + p.yrows] = small
+    pad = p.half - 2 * p.blk - p.yrows
+    if pad:
+        rows[p.half - pad :] = jnp.zeros((pad, p.blk), BF16)
+    mine = rows[0 : p.mrows]
+    for owner in range(1, p.fold):
+        mine = jnp.where(h == owner, rows[owner * p.mrows : (owner + 1) * p.mrows], mine)
     copies[0].wait()
     turned[...] = filt[...].T
 
     def one_target(s):
         out[s, 0 : p.mrows] = mine
-        start = (h * p.seq + s) * p.width
+        logs = turned[rows_at(s * p.width, p.width)]
         if p.cores_share:
-            start = start + core * p.frows
-        out[s, p.mrows :] = turned[rows_at(start, p.frows)]
+            logs = jnp.where(core == 0, logs[: p.frows], logs[p.frows :])
+        out[s, p.mrows :] = logs
 
     each(p.seq, one_target)
 
@@ -154,28 +161,42 @@
         out[q, w : 2 * w] = upstream_rows[q * w : (q + 1) * w]
 
 
-def prepare_kernel(p, place, *refs):
-    pieces, (one, four, small, filt, rows, turned) = refs[: 2 * p.fold], refs[2 * p.fold :]
-    h, core = place[0], place[1]
-    for side in range(2):
-        c = core if side == 0 else 1 - core
-        for step in range(p.fold):
-            piece = pieces[side * p.fold + step]
-            owner = h - step
-            owner = jnp.where(owner < 0, owner + p.fold, owner)
-            rows[:, rows_at(c * p.half + owner * p.mrows, p.mrows), :] = piece[:, 0 : p.mrows, :]
-            if step == 0 and (p.cores_share or side == 0):
-                start = c * p.frows if p.cores_share else 0
-                turned[:, rows_at(start, p.frows), :] = piece[:, p.mrows :, :]
+def shares_in_order(p, pieces):
+    h, core = place(p)
+
+    def share(c, owner, part):
+        value = None
+        for side in range(2):
+            for step in range(p.fold):
+                piece = part(pieces[side * p.fold + step], side, step)
+                if value is None:
+                    value = piece
+                    continue
+                here = core == (c if side == 0 else 1 - c)
+                value = jnp.where(here & (h == (owner + step) % p.fold), piece, value)
+        return value
+
+    return share
+
+
+def prepare_kernel(p, *refs):
+    pieces, (one, four, small, filt) = refs[: 2 * p.fold], refs[2 * p.fold :]
+    share = shares_in_order(p, pieces)
+    _, core = place(p)
 
     def one_block(i):
         for part in range(2):
-            base = part * p.half
-            one[i, part * p.blk : (part + 1) * p.blk] = rows[i, base : base + p.blk]
-            factor = rows[i, base + p.blk : base + 2 * p.blk]
+            rows = [share(part, owner, lambda ref, *_: ref[i, 0 : p.mrows]) for owner in range(p.fold)]
+            rows = jnp.concatenate(rows, axis=0) if p.fold > 1 else rows[0]
+            one[i, part * p.blk : (part + 1) * p.blk] = rows[0 : p.blk]
+            factor = rows[p.blk : 2 * p.blk]
             four[i, :, part * p.blk : (part + 1) * p.blk] = factor if part == 0 else -factor
-            small[part, i] = rows[i, base + 2 * p.blk : base + 2 * p.blk + p.yrows]
-        logs = turned[i]
+            small[part, i] = rows[2 * p.blk : 2 * p.blk + p.yrows]
+        logs = pieces[0][i, p.mrows :]
+        if p.cores_share:
+            other = pieces[p.fold][i, p.mrows :]
+            logs = [jnp.where(core == 0, logs, other), jnp.where(core == 0, other, logs)]
+            logs = jnp.concatenate(logs, axis=0)
         if p.fold > 1:
             logs = jnp.concatenate([logs] * p.fold, axis=0)
         filt[i] = jnp.exp(logs.T.astype(F32))
@@ -234,11 +255,23 @@
 
 
 def mixer_kernel(
-    p, place, tokens_in, taps, one, four, two_far, three_far, filt,
-    grad_x, keep, send, small_keep, small_send,
-    tok, ups, val, mix, groups_a, groups_b, second, time_a, gate, grad_v, filter_grad, halves, fulls, small, *near,
+    p, tokens_in, taps, one, four, two_far, three_far, filt,
+    grad_x, keep, send, *refs,
 ):
-    core = place[1]
+    _, core = place(p)
+    small_out = None if p.direct else refs[:2]
+    (tok, ups, val, mix, groups_a, groups_b, second, time_a, gate, grad_v, filter_grad,
+     gradients, small, groups_d, diagonal, *near) = refs if p.direct else refs[2:]
+
+    def hand_out(i, base, values):
+        mine = jnp.where(core == 0, values[0], values[1])
+        other = jnp.where(core == 0, values[1], values[0])
+        last = base + values[0].shape[0]
+        for h in range(p.fold):
+            lo, hi = max(base, h * p.mrows), min(last, (h + 1) * p.mrows)
+            if lo < hi:
+                keep[h, i, lo - h * p.mrows : hi - h * p.mrows] = mine[lo - base : hi - base]
+                send[h, i, lo - h * p.mrows : hi - h * p.mrows] = other[lo - base : hi - base]
 
     def factor(far, at, g):
         if not p.streamed:
@@ -296,15 +329,25 @@
         f2 = jnp.concatenate([f, f], axis=0)
         sec = dot(factor(two_far, 0, g), groups_a[g], 0, 0)
         second[g] = sec
-        weighted = (f2 * sec).astype(BF16)
-        groups_b[g] = weighted
-        third = dot(factor(three_far, 1, g), weighted, 1, 0).astype(BF16)
+        groups_b[g] = (f2 * sec).astype(BF16)
+
+    def unspread(g, value):
         for part in range(2):
-            for n in range(nb):
-                row = (part * nb + n) * TILE
-                time_a[n, rows_at(part * blk + g * TILE, TILE)] = third[row : row + TILE]
-
-    each(p.kgroups, forward_middle)
+            for i in range(nb):
+                row = (part * nb + i) * TILE
+                time_a[i, rows_at(part * blk + g * TILE, TILE)] = value[row : row + TILE]
+
+    def forward_last(g):
+        unspread(g, dot(factor(three_far, 1, g), groups_b[g], 1, 0).astype(BF16))
+
+    def each_group(*stages):
+        if p.streamed:
+            each(p.kgroups, lambda g: [stage(g) for stage in stages], unrolled=False)
+        else:
+            for stage in stages:
+                each(p.kgroups, stage)
+
+    each_group(forward_middle, forward_last)
 
     def last_factor(n):
         third = time_a[n]
@@ -319,60 +362,57 @@
                 row = part * blk + g * TILE
                 groups_b[p.kgroups + g, rows_at((part * nb + n) * TILE, TILE)] = back[row : row + TILE]
         products = dot(grads, third, 1, 1)
-        halves[0, n, blk : 2 * blk] = products[:, 0:blk].astype(BF16)
-        halves[1, n, blk : 2 * blk] = (-products[:, blk:]).astype(BF16)
+        hand_out(n, blk, (products[:, 0:blk].astype(BF16), (-products[:, blk:]).astype(BF16)))
 
     each(nb, last_factor)
 
     same, keep_two, keep_three = block_masks(p)
     pick_two, pick_three = selectors(p, True)
-
-    def folded(real, imag, pick, kept):
-        out = []
-        for value in (real, imag):
-            value = jnp.where(same, value, 0.0).astype(BF16)
-            wide = dot(value, pick, 1, 0)
-            wide = jnp.where(kept, wide, 0.0)
-            out.append(jnp.sum(wide.reshape(nb, TILE, 2 * p.pairs), axis=0))
-        return out
 
     def backward_middle(g):
         f = filter_of(g)
         f2 = jnp.concatenate([f, f], axis=0)
-        third_grad = groups_b[p.kgroups + g]
-        weighted_grad = dot(factor(three_far, 1, g), third_grad, 0, 0)
+        weighted_grad = dot(factor(three_far, 1, g), groups_b[p.kgroups + g], 0, 0)
         term = weighted_grad * second[g]
         filter_grad[rows_at(g * d, d)] = f * (term[:d] + term[d:])
-        products = dot(third_grad, groups_b[g], 1, 1)
-        three_real, three_imag = folded(
-            products[:d, :d] + products[d:, d:], products[d:, :d] - products[:d, d:], pick_three, keep_three
-        )
-        second_grad = (f2 * weighted_grad).astype(BF16)
-        products = dot(groups_a[g], second_grad, 1, 1)
-        two_real, two_imag = folded(
-            products[:d, :d] + products[d:, d:], products[:d, d:] - products[d:, :d], pick_two, keep_two
-        )
-        at = rows_at(g * TILE, TILE)
-        small[0, at] = (two_real + three_real).astype(BF16)
-        small[1, at] = (two_imag + three_imag).astype(BF16)
-        back = dot(factor(two_far, 0, g), second_grad, 1, 0).astype(BF16)
+        groups_d[g] = (f2 * weighted_grad).astype(BF16)
+
+    def backward_last(g):
+        unspread(g, dot(factor(two_far, 0, g), groups_d[g], 1, 0).astype(BF16))
+
+    def group_products(g):
+        at = rows_at(0 if p.streamed else g * d, d)
+        three = dot(groups_b[p.kgroups + g], groups_b[g], 1, 1)
+        two = dot(groups_a[g], groups_d[g], 1, 1)
+        for kind, real, imag in (
+            (0, two[:d, :d] + two[d:, d:], two[:d, d:] - two[d:, :d]),
+            (1, three[:d, :d] + three[d:, d:], three[d:, :d] - three[:d, d:]),
+        ):
+            diagonal[kind, 0, at] = jnp.where(same, real, 0.0).astype(BF16)
+            diagonal[kind, 1, at] = jnp.where(same, imag, 0.0).astype(BF16)
+
+    def fold_products(g):
+        at = rows_at(0 if p.streamed else g * d, d)
         for part in range(2):
-            for i in range(nb):
-                row = (part * nb + i) * TILE
-                time_a[i, rows_at(part * blk + g * TILE, TILE)] = back[row : row + TILE]
-
-    each(p.kgroups, backward_middle)
+            two = jnp.where(keep_two, dot(diagonal[0, part, at], pick_two, 1, 0), 0.0)
+            three = jnp.where(keep_three, dot(diagonal[1, part, at], pick_three, 1, 0), 0.0)
+            total = jnp.sum((two + three).reshape(nb, TILE, 2 * p.pairs), axis=0)
+            small[part, rows_at(g * TILE, TILE)] = total.astype(BF16)
+        if p.direct:
+            at = rows_at(g * TILE, TILE)
+            hand_out(g, 2 * blk, (small[0, at], small[1, at]))
+
+    each_group(backward_middle, backward_last, group_products, fold_products)
 
     def first_factor(i):
         first_grad = time_a[i]
         grad_v[pl.ds(edge + i * blk, blk)] = dot(one[i], first_grad, 0, 0)
-        products = dot(first_grad, val[rows_at(i * blk, blk)], 1, 1)
-        for part in range(2):
-            halves[part, i, 0:blk] = products[part * blk : (part + 1) * blk].astype(BF16)
-        if p.half > 2 * blk:
-            rest = jnp.zeros((p.half - 2 * blk, blk), BF16)
-            for part in range(2):
-                halves[part, i, 2 * blk :] = rest
+        products = dot(first_grad, val[rows_at(i * blk, blk)], 1, 1).astype(BF16)
+        hand_out(i, 0, (products[:blk], products[blk:]))
+        used = 2 * blk + (p.yrows if p.direct else 0)
+        if p.half > used:
+            rest = jnp.zeros((p.half - used, blk), BF16)
+            hand_out(i, used, (rest, rest))
 
     each(nb, first_factor)
 
@@ -387,16 +427,12 @@
             for offset in range(3):
                 product = here * window(tok, i, offset - 1)
                 sums[3 * branch + offset] += jnp.sum(product.reshape(blk // 8, 8, cols), axis=0)
-        turned = total.astype(BF16).T
+        grad_x[i] = total.astype(BF16)
         terms = filter_grad[rows_at(i * blk, blk)].T
         term = terms[0:w]
         for h in range(1, p.fold):
             term = term + terms[h * w : (h + 1) * w]
-        fulls[i, 0:w] = term.astype(BF16)
-        if p.full > w + TILE:
-            fulls[i, w + TILE :] = jnp.zeros((p.full - w - TILE, blk), BF16)
-        for h in range(p.fold):
-            grad_x[h * nb + i] = turned[h * w : (h + 1) * w]
+        gradients[i] = term.astype(BF16)
         return tuple(sums)
 
     if nb <= 8:
@@ -414,27 +450,46 @@
     high = term.astype(BF16).astype(F32)
     conv_rows = jnp.concatenate([high, term - high], axis=0).astype(BF16)
 
-    def hand_out(s):
-        fulls[s, w : w + TILE] = conv_rows
-        for ref, c in ((keep, core), (send, 1 - core)):
-            for h in range(p.fold):
-                ref[h, s, 0 : p.mrows] = halves[c, s, h * p.mrows : (h + 1) * p.mrows]
-                ref[h, s, p.mrows :] = fulls[s, rows_at((c * p.fold + h) * p.orows, p.orows)]
-
-    each(nb, hand_out)
-    small_keep[...] = small[core]
-    small_send[...] = small[1 - core]
-
-
-def add_kernel(p, keep, got, small_keep, small_got, out):
+    ends = [conv_rows]
+    if p.full > w + TILE:
+        ends.append(jnp.zeros((p.full - w - TILE, blk), BF16))
+
+    def last_rows(i):
+        rows = jnp.concatenate([gradients[i], *ends], axis=0)
+        middle = p.full // 2
+        mine = jnp.where(core == 0, rows[:middle], rows[middle:])
+        other = jnp.where(core == 0, rows[middle:], rows[:middle])
+        for h in range(p.fold):
+            at = slice(h * p.orows, (h + 1) * p.orows)
+            keep[h, i, p.mrows :] = mine[at]
+            send[h, i, p.mrows :] = other[at]
+
+    each(nb, last_rows)
+    if not p.direct:
+        small_out[0][...] = jnp.where(core == 0, small[0], small[1])
+        small_out[1][...] = jnp.where(core == 0, small[1], small[0])
+
+
+def token_grad_message_kernel(p, grads, out):
+    def one_target(i):
+        turned = grads[i].T
+        for h in range(p.fold):
+            out[h * p.nblk + i] = turned[h * p.width : (h + 1) * p.width]
+
+    each(p.nblk, one_target)
+
+
+def add_kernel(p, keep, got, *refs):
+    out = refs[-1]
+
     def one_target(s):
-        extra = (small_keep[s].astype(F32) + small_got[s].astype(F32)).astype(BF16)
         for h in range(p.fold):
             q = h * p.seq + s
             out[q] = (keep[h, s].astype(F32) + got[h, s].astype(F32)).astype(BF16)
             first, last = 2 * p.blk - h * p.mrows, 2 * p.blk + p.yrows - h * p.mrows
             lo, hi = max(first, 0), min(last, p.mrows)
-            if lo < hi:
+            if not p.direct and lo < hi:
+                extra = (refs[0][s].astype(F32) + refs[1][s].astype(F32)).astype(BF16)
                 out[q, lo:hi] = extra[lo - first : hi - first]
 
     each(p.seq, one_target)
@@ -455,36 +510,36 @@
     out[...] = rows.T
 
 
-def finish_kernel(p, place, *refs):
-    pieces, outs, (rows, fulls) = refs[: 2 * p.fold], refs[2 * p.fold : -2], refs[-2:]
+def finish_kernel(p, *refs):
+    pieces, outs = refs[: 2 * p.fold], refs[2 * p.fold :]
     one, four, filt, conv_value, conv_gate, *small = outs
-    h, core = place[0], place[1]
-    for side in range(2):
-        c = core if side == 0 else 1 - core
-        for step in range(p.fold):
-            piece = pieces[side * p.fold + step]
-            owner = h - step
-            owner = jnp.where(owner < 0, owner + p.fold, owner)
-            rows[rows_at(c * p.half + owner * p.mrows, p.mrows)] = piece[0 : p.mrows]
-            at = rows_at((c * p.fold + owner) * p.orows, p.orows)
-            for q in range(p.members):
-                fulls[q, at] = piece[p.mrows + q * p.orows : p.mrows + (q + 1) * p.orows]
+    share = shares_in_order(p, pieces)
     for part in range(2):
-        base = part * p.half
-        one[part] = rows[base : base + p.blk]
-        four[part] = rows[base + p.blk : base + 2 * p.blk]
-        entries = rows[base + 2 * p.blk : base + 2 * p.blk + p.yrows]
+        rows = [share(part, owner, lambda ref, *_: ref[0 : p.mrows]) for owner in range(p.fold)]
+        rows = jnp.concatenate(rows, axis=0) if p.fold > 1 else rows[0]
+        one[part] = rows[0 : p.blk]
+        four[part] = rows[p.blk : 2 * p.blk]
+        entries = rows[2 * p.blk : 2 * p.blk + p.yrows]
         if p.direct:
             entries = entries.T
             small[0][part] = entries[: p.pairs]
             small[1][part] = entries[p.pairs :]
         else:
             small[0][part] = entries
-    turned = jnp.concatenate([fulls[q, 0 : p.width] for q in range(p.members)], axis=0)
-    filt[...] = turned.T
-    sums = fulls[:, p.width : p.width + TILE].astype(F32)
-    sums = sums[:, :8] + sums[:, 8:]
-    sums = jnp.concatenate([sums[q].T[: p.width] for q in range(p.members)], axis=0).T
+    turned, columns = [], []
+    for q in range(p.members):
+        first = p.mrows + q * p.orows
+        rows = [
+            share(c, owner, lambda ref, *_: ref[first : first + p.orows])
+            for c in range(2)
+            for owner in range(p.fold)
+        ]
+        rows = jnp.concatenate(rows, axis=0)
+        turned.append(rows[0 : p.width])
+        both = rows[p.width : p.width + TILE].astype(F32)
+        columns.append((both[:8] + both[8:]).T[: p.width])
+    filt[...] = jnp.concatenate(turned, axis=0).T
+    sums = jnp.concatenate(columns, axis=0).T
     conv_value[...] = sums[0:3]
     conv_gate[...] = sums[3:6]
 
@@ -495,7 +550,6 @@
     p = Plan(lax.axis_size("dp"), lax.axis_size("seq"), tokens, mix_one, mix_two)
     dp_at, seq_at = lax.axis_index("dp"), lax.axis_index("seq")
     h_at = (dp_at // 2) % p.fold
-    place = jnp.stack([h_at, dp_at % 2]).astype(jnp.int32)
     blk, pairs = p.blk, p.pairs
 
     def shuffle(array):
@@ -526,16 +580,15 @@
     message = call(
         functools.partial(factor_message_kernel, p),
         shape(p.seq, p.mrows + p.frows, blk),
-        place,
         *far,
-        scratch=[pltpu.VMEM(f.shape, BF16) for f in far]
+        scratch=[pltpu.VMEM((blk, p.channels // p.fold), BF16)]
+        + [pltpu.VMEM(f.shape[1:], BF16) for f in far[1:]]
         + [
-            pltpu.VMEM((2 * p.half, blk), BF16),
-            pltpu.VMEM((p.channels, blk), BF16),
+            pltpu.VMEM((p.half, blk), BF16),
+            pltpu.VMEM((p.channels // p.fold, blk), BF16),
             pltpu.SemaphoreType.DMA((len(far),)),
         ],
-        smem=(0,),
-        far=range(1, 1 + len(far)),
+        far=range(len(far)),
         limit=60,
         name="factor_message",
     )
@@ -559,13 +612,7 @@
             shape(2, p.nblk, p.yrows, blk),
             shape(p.nblk, blk, p.cols, dtype=F32),
         ],
-        place,
         *pieces,
-        scratch=[
-            pltpu.VMEM((p.nblk, 2 * p.half, blk), BF16),
-            pltpu.VMEM((p.nblk, p.width, blk), BF16),
-        ],
-        smem=(0,),
         name="prepare",
     )
     two, three = call(
@@ -582,16 +629,14 @@
     taps = jnp.concatenate([taps] * p.fold, axis=1)
 
     padded = p.length + 16
-    grad_x, keep, send, small_keep, small_send = call(
+    grad_x, keep, send, *small = call(
         functools.partial(mixer_kernel, p),
         [
-            shape(p.members, p.width, blk),
+            shape(p.nblk, blk, p.cols),
             shape(p.fold, p.seq, p.share, blk),
             shape(p.fold, p.seq, p.share, blk),
-            shape(blk, 2 * pairs),
-            shape(blk, 2 * pairs),
-        ],
-        place,
+        ]
+        + [shape(blk, 2 * pairs)] * (0 if p.direct else 2),
         received,
         taps,
         one,
@@ -611,13 +656,13 @@
             pltpu.VMEM((padded, p.cols), F32),
             pltpu.VMEM((padded, p.cols), F32),
             pltpu.VMEM((p.length, p.cols), F32),
-            pltpu.VMEM((2, p.nblk, p.half, blk), BF16),
-            pltpu.VMEM((p.nblk, p.full, blk), BF16),
+            pltpu.VMEM((p.nblk, p.width, blk), BF16),
             pltpu.VMEM((2, blk, 2 * pairs), BF16),
+            pltpu.VMEM((p.kgroups, 2 * p.dim, p.cols), BF16),
+            pltpu.VMEM((2, 2, (1 if p.streamed else p.kgroups) * p.dim, p.dim), BF16),
         ]
         + [pltpu.VMEM((2 * p.dim, 2 * p.dim), BF16)] * (2 if p.streamed else 0),
-        smem=(0,),
-        far=(5, 6) if p.streamed else (),
+        far=(4, 5) if p.streamed else (),
         limit=60 if p.streamed else 20,
         name="mixer",
     )
@@ -627,11 +672,16 @@
         shape(p.members, p.share, blk),
         keep,
         swap(send),
-        small_keep.reshape(p.seq, p.yrows, blk),
-        swap(small_send).reshape(p.seq, p.yrows, blk),
+        *[f.reshape(p.seq, p.yrows, blk) for f in (small if p.direct else (small[0], swap(small[1])))],
         name="add_cores",
     )
     received = shuffle(message)
+    grad_x = call(
+        functools.partial(token_grad_message_kernel, p),
+        shape(p.members, p.width, blk),
+        grad_x,
+        name="token_grad_message",
+    )
     received, grad_x = lax.optimization_barrier((received, grad_x))
     grad_x = shuffle(grad_x)
     sums = call(
@@ -659,13 +709,7 @@
             shape(3, p.channels, dtype=F32),
         ]
         + ([shape(2, pairs, p.kloc)] * 2 if p.direct else [shape(2, p.yrows, blk)]),
-        place,
         *pieces,
-        scratch=[
-            pltpu.VMEM((2 * p.half, blk), BF16),
-            pltpu.VMEM((p.members, p.full, blk), BF16),
-        ],
-        smem=(0,),
         name="finish",
     )
     if p.direct:

time: 101 us -> 98 us (0.970)
  blocking collectives: 23.9 us -> 0 us
  waiting for transfers between devices: 38.1 us -> 57.7 us
  starting transfers between devices: 20.1 us -> 23.4 us
  Pallas kernels: 17.1 us -> 14.7 us
    all_to_all x1 -> x0, blocking collectives: 23.9 us -> none  [shuffle(): lax.all_to_all(array, ('dp', 'seq'), 0, 0, tiled=True, axis_index_groups=...]
    all_to_all x2 -> x3, waiting for transfers between devices: 3.19 us -> 22.4 us  [shuffle(): lax.all_to_all(array, ('dp', 'seq'), 0, 0, tiled=True, axis_index_groups=...]
    all_to_all x2 -> x3, starting transfers between devices: 8.21 us -> 12 us  [shuffle(): lax.all_to_all(array, ('dp', 'seq'), 0, 0, tiled=True, axis_index_groups=...]
    pallas_call x9 -> x10, Pallas kernels: 17.1 us -> 14.7 us  [call(): pl.pallas_call(kernel, out_shape=out_shape, in_specs=[FAR if i in far els...]
    ppermute x6 -> x5, waiting for transfers between devices: 4.54 us -> 4.24 us  [swap(): return lax.ppermute(array, 'dp', p.across_cores())]
  transfers between devices with their start and end apart: 11 -> 11, of which waited for: 7 -> 9; matrix products, arithmetic and copies ran while one was open for 0% -> 0% of each run, Pallas kernels for 3% -> 4%
where the time goes in v3:
time: 98 us; the launch traced here: 97.4 us
  waiting for transfers between devices  57.7 us (59%)
  starting transfers between devices  23.4 us (24%)
  Pallas kernels  14.7 us (15%)
    all_to_all x3, waiting for transfers between devices, shuffle(): lax.all_to_all(array, ('dp', 'seq'), 0, 0, tiled=True, axis_index_groups=...  22.4 us
    ppermute x2, waiting for transfers between devices, gathered(): pieces.append(lax.ppermute(rows(array), 'dp', p.across_fold(step)))  20.5 us
    pallas_call x10, Pallas kernels, call(): pl.pallas_call(kernel, out_shape=out_shape, in_specs=[FAR if i in far els...  14.7 us
    all_to_all x3, starting transfers between devices, shuffle(): lax.all_to_all(array, ('dp', 'seq'), 0, 0, tiled=True, axis_index_groups=...  12 us
    all_to_all x1, waiting for transfers between devices, shards(): factors = lax.all_to_all(message, 'seq', 0, 0, tiled=True)  10.5 us
    all_to_all x1, starting transfers between devices, shards(): factors = lax.all_to_all(message, 'seq', 0, 0, tiled=True)  7.42 us
    ppermute x5, waiting for transfers between devices, swap(): return lax.ppermute(array, 'dp', p.across_cores())  4.24 us
    ppermute x2, starting transfers between devices, gathered(): pieces.append(lax.ppermute(rows(array), 'dp', p.across_fold(step)))  3.9 us
  transfers between devices with their start and end apart: 11, of which 9 were waited for; matrix products, arithmetic and copies ran while one was open for 0% of the time, Pallas kernels for 4%

profile of v3, /device:TPU:0, one launch (start us, length us, event | category | flops | bytes accessed | tf_op | source)
XLA Modules:
  0.0 97.4 jit_solution(3236549414961783414)
XLA Ops:
  0.6 1.9 %factor_message.1 = bf16[8,192,128]{2,1,0:T(8,128)(2,1)} custom-call(bf16[128,1536]{1,0:T(8,128)(2,1)} %bitcast.32, bf16[2,128,128]{2,1,0:T(8,128)(2,1)} %bitcast.33, bf16[2,128,128]{2,1,0:T(8,128)(2,1)} %bitcast.34, bf16[2,64,16]{2,1,0:T(8,128)(2,1)} %bitcast.35, bf16[2,64,16]{2,1,0:T(8,128)(2,1)} %bitcast.36), custom_call_target="tpu_custom_call" | custom-call | tf_op jit(solution)/shard_map/factor_message/pallas_call | solution.py:96
  2.5 0.0 copy-start
  2.5 0.0 copy-start.1
  2.6 7.4 %all-to-all-start = ((bf16[8,192,128]{2,1,0:T(8,128)(2,1)}), bf16[8,192,128]{2,1,0:T(8,128)(2,1)S(1)}, u32[]{:S(2)}, u32[]{:S(2)}) async-start(bf16[8,192,128]{2,1,0:T(8,128)(2,1)} %factor_message.1), calls=%async_computation | async-start | bytes 786432 | tf_op jit(solution)/shard_map/all_to_all | solution.py:595
  10.0 0.0 copy-done
  10.0 0.0 copy-done.1
  10.0 1.1 %token_message.1 = bf16[16,192,128]{2,1,0:T(8,128)(2,1)} custom-call(bf16[128,1536]{1,0:T(8,128)(2,1)S(1)} %bitcast.28, bf16[128,1536]{1,0:T(8,128)(2,1)S(1)} %bitcast.29), custom_call_target="tpu_custom_call" | custom-call | tf_op jit(solution)/shard_map/token_message/pallas_call | solution.py:96
  11.1 10.5 %all-to-all-done.refs_0_ = bf16[8,192,128]{2,1,0:T(8,128)(2,1)S(1)} async-done(((bf16[8,192,128]{2,1,0:T(8,128)(2,1)}), bf16[8,192,128]{2,1,0:T(8,128)(2,1)S(1)}, u32[]{:S(2)}, u32[]{:S(2)}) %all-to-all-start) | async-done | bytes 393248 | tf_op jit(solution)/shard_map/all_to_all | solution.py:595
  21.7 4.7 %all-to-all-start.1 = ((bf16[16,192,128]{2,1,0:T(8,128)(2,1)}), bf16[16,192,128]{2,1,0:T(8,128)(2,1)S(1)}, u32[]{:S(2)}, u32[]{:S(2)}) async-start(bf16[16,192,128]{2,1,0:T(8,128)(2,1)} %token_message.1), calls=%async_computation.1 | async-start | bytes 1572864 | tf_op jit(solution)/shard_map/all_to_all | solution.py:556
  26.4 2.0 %collective-permute-start = (bf16[8,144,128]{2,1,0:T(8,128)(2,1)S(1)}, bf16[8,144,128]{2,1,0:T(8,128)(2,1)S(1)}, u32[]{:S(2)}, u32[]{:S(2)}) collective-permute-start(bf16[8,144,128]{2,1,0:T(8,128)(2,1)S(1)} %slice.4), channel_id=1, source_target_pairs={{0,16},{8,24},{16,0},{24,8},{1,17},{9,25},{17,1},{25,9},{2,18},{10... | collective-permute-start | bytes 884744 | tf_op jit(solution)/shard_map/ppermute | solution.py:566
  28.4 0.0 collective-permute-start.1
  28.4 13.6 %collective-permute-done.refs_1_ = bf16[8,144,128]{2,1,0:T(8,128)(2,1)S(1)} collective-permute-done((bf16[8,144,128]{2,1,0:T(8,128)(2,1)S(1)}, bf16[8,144,128]{2,1,0:T(8,128)(2,1)S(1)}, u32[]{:S(2)}, u32[]{:S(2)}) %collective-permute-start) | collective-permute-done | bytes 294944 | tf_op jit(solution)/shard_map/ppermute | solution.py:566
  41.9 0.0 collective-permute-start.2
  41.9 0.0 copy-start.3
  41.9 0.0 copy-start.2
  41.9 0.7 copy-done.3
  42.7 0.0 copy-done.2
  42.7 0.1 fusion
  42.8 0.1 pad_maximum_fusion.taps
  42.8 0.0 collective-permute-done.1.refs_2_
  42.8 0.7 collective-permute-done.2.refs_3_
  43.5 3.2 %all-to-all-done.1.tokens_in = bf16[16,192,128]{2,1,0:T(8,128)(2,1)S(1)} async-done(((bf16[16,192,128]{2,1,0:T(8,128)(2,1)}), bf16[16,192,128]{2,1,0:T(8,128)(2,1)S(1)}, u32[]{:S(2)}, u32[]{:S(2)}) %all-to-all-start.1) | async-done | bytes 786464 | tf_op jit(solution)/shard_map/all_to_all | solution.py:556
  46.7 0.7 prepare.1
  47.4 0.5 block_factors.1
  47.8 6.2 %mixer.1 = (bf16[8,128,192]{2,1,0:T(8,128)(2,1)S(1)}, bf16[2,8,176,128]{3,2,1,0:T(8,128)(2,1)S(1)}, bf16[2,8,176,128]{3,2,1,0:T(8,128)(2,1)S(1)}) custom-call(bf16[16,192,128]{2,1,0:T(8,128)(2,1)S(1)} %all-to-all-done.1.tokens_in, f32[6,192]{1,0:T(8,128)S(1)} %pad_maximum_fusion.taps, bf16[8,256,128]{2,1,0:T(8,128)(2,1)S(1)} %get-tuple-element.36.one, ...), custom_call_target="tpu_custom_call" | custom-call | tf_op jit(solution)/shard_map/mixer/pallas_call | solution.py:96
  54.0 0.1 collective-permute-start.3
  54.1 2.2 %collective-permute-done.3.got = bf16[2,8,176,128]{3,2,1,0:T(8,128)(2,1)S(1)} collective-permute-done((bf16[2,8,176,128]{3,2,1,0:T(8,128)(2,1)S(1)}, bf16[2,8,176,128]{3,2,1,0:T(8,128)(2,1)S(1)}, u32[]{:S(2)}, u32[]{:S(2)}) %collective-permute-start.3) | collective-permute-done | bytes 720928 | tf_op jit(solution)/shard_map/ppermute | solution.py:561
  56.3 1.0 %add_cores.1 = bf16[16,176,128]{2,1,0:T(8,128)(2,1)} custom-call(bf16[2,8,176,128]{3,2,1,0:T(8,128)(2,1)S(1)} %get-tuple-element.42.keep, bf16[2,8,176,128]{3,2,1,0:T(8,128)(2,1)S(1)} %collective-permute-done.3.got), custom_call_target="tpu_custom_call" | custom-call | tf_op jit(solution)/shard_map/add_cores/pallas_call | solution.py:96
  57.3 3.8 %all-to-all-start.2 = ((bf16[16,176,128]{2,1,0:T(8,128)(2,1)}), bf16[16,176,128]{2,1,0:T(8,128)(2,1)S(1)}, u32[]{:S(2)}, u32[]{:S(2)}) async-start(bf16[16,176,128]{2,1,0:T(8,128)(2,1)} %add_cores.1), calls=%async_computation.2 | async-start | bytes 1441792 | tf_op jit(solution)/shard_map/all_to_all | solution.py:556
  61.1 0.9 token_grad_message.1
  62.0 18.4 %all-to-all-done.2.got = bf16[16,176,128]{2,1,0:T(8,128)(2,1)S(1)} async-done(((bf16[16,176,128]{2,1,0:T(8,128)(2,1)}), bf16[16,176,128]{2,1,0:T(8,128)(2,1)S(1)}, u32[]{:S(2)}, u32[]{:S(2)}) %all-to-all-start.2) | async-done | bytes 720928 | tf_op jit(solution)/shard_map/all_to_all | solution.py:556
  80.4 3.6 %all-to-all-start.3 = ((bf16[16,96,128]{2,1,0:T(8,128)(2,1)}), bf16[16,96,128]{2,1,0:T(8,128)(2,1)S(1)}, u32[]{:S(2)}, u32[]{:S(2)}) async-start(bf16[16,96,128]{2,1,0:T(8,128)(2,1)} %token_grad_message.1), calls=%async_computation.3 | async-start | bytes 786432 | tf_op jit(solution)/shard_map/all_to_all | solution.py:556
  84.0 0.1 sum_sources.1.refs_0_
  84.1 1.9 %collective-permute-start.4 = (bf16[656,128]{1,0:T(8,128)(2,1)S(1)}, bf16[656,128]{1,0:T(8,128)(2,1)S(1)}, u32[]{:S(2)}, u32[]{:S(2)}) collective-permute-start(bf16[656,128]{1,0:T(8,128)(2,1)S(1)} %sum_sources.1.refs_0_), channel_id=1, source_target_pairs={{0,16},{8,24},{16,0},{24,8},{1,17},{9,25},{17,1},{25,9},{2,18},{10... | collective-permute-start | bytes 503816 | tf_op jit(solution)/shard_map/ppermute | solution.py:566
  86.0 0.0 collective-permute-start.5
  86.0 7.0 %collective-permute-done.4.refs_1_ = bf16[656,128]{1,0:T(8,128)(2,1)S(1)} collective-permute-done((bf16[656,128]{1,0:T(8,128)(2,1)S(1)}, bf16[656,128]{1,0:T(8,128)(2,1)S(1)}, u32[]{:S(2)}, u32[]{:S(2)}) %collective-permute-start.4) | collective-permute-done | bytes 167968 | tf_op jit(solution)/shard_map/ppermute | solution.py:566
  93.0 0.0 collective-permute-start.6
  93.0 0.0 collective-permute-done.5.refs_2_
  93.0 1.4 %collective-permute-done.6.refs_3_ = bf16[656,128]{1,0:T(8,128)(2,1)S(1)} collective-permute-done((bf16[656,128]{1,0:T(8,128)(2,1)S(1)}, bf16[656,128]{1,0:T(8,128)(2,1)S(1)}, u32[]{:S(2)}, u32[]{:S(2)}) %collective-permute-start.6) | collective-permute-done | bytes 167968 | tf_op jit(solution)/shard_map/ppermute | solution.py:561
  94.4 1.4 %finish.1 = (bf16[2,128,128]{2,1,0:T(8,128)(2,1)}, bf16[2,128,128]{2,1,0:T(8,128)(2,1)}, bf16[128,1536]{1,0:T(8,128)(2,1)}, f32[3,1536]{1,0:T(4,128)}, f32[3,153...) custom-call(bf16[656,128]{1,0:T(8,128)(2,1)S(1)} %sum_sources.1.refs_0_, ...), custom_call_target="tpu_custom_call" | custom-call | tf_op jit(solution)/shard_map/finish/pallas_call | solution.py:96
  95.7 0.8 all-to-all-done.3.got
  96.5 0.9 token_grad.1
  (1 shorter events, 0.0 us)
Async XLA Ops:
  2.5 7.5 %copy-start = (bf16[1,128,1536]{2,1,0:T(8,128)(2,1)S(1)}, bf16[1,128,1536]{2,1,0:T(8,128)(2,1)}, u32[]{:S(2)}) copy-start(bf16[1,128,1536]{2,1,0:T(8,128)(2,1)} %param.9) | copy-start | bytes 1179652
  2.5 7.4 %copy-start.1 = (bf16[1,128,1536]{2,1,0:T(8,128)(2,1)S(1)}, bf16[1,128,1536]{2,1,0:T(8,128)(2,1)}, u32[]{:S(2)}) copy-start(bf16[1,128,1536]{2,1,0:T(8,128)(2,1)} %param.10) | copy-start | bytes 1179652
  2.6 19.1 %all-to-all-start = ((bf16[8,192,128]{2,1,0:T(8,128)(2,1)}), bf16[8,192,128]{2,1,0:T(8,128)(2,1)S(1)}, u32[]{:S(2)}, u32[]{:S(2)}) async-start(bf16[8,192,128]{2,1,0:T(8,128)(2,1)} %factor_message.1), calls=%async_computation | async-start | bytes 786432 | tf_op jit(solution)/shard_map/all_to_all | solution.py:595
  21.7 25.0 %all-to-all-start.1 = ((bf16[16,192,128]{2,1,0:T(8,128)(2,1)}), bf16[16,192,128]{2,1,0:T(8,128)(2,1)S(1)}, u32[]{:S(2)}, u32[]{:S(2)}) async-start(bf16[16,192,128]{2,1,0:T(8,128)(2,1)} %token_message.1), calls=%async_computation.1 | async-start | bytes 1572864 | tf_op jit(solution)/shard_map/all_to_all | solution.py:556
  26.4 15.6 %collective-permute-start = (bf16[8,144,128]{2,1,0:T(8,128)(2,1)S(1)}, bf16[8,144,128]{2,1,0:T(8,128)(2,1)S(1)}, u32[]{:S(2)}, u32[]{:S(2)}) collective-permute-start(bf16[8,144,128]{2,1,0:T(8,128)(2,1)S(1)} %slice.4), channel_id=1, source_target_pairs={{0,16},{8,24},{16,0},{24,8},{1,17},{9,25},{17,1},{25,9},{2,18},{10... | collective-permute-start | bytes 884744 | tf_op jit(solution)/shard_map/ppermute | solution.py:566
  28.4 14.5 %collective-permute-start.1 = (bf16[8,192,128]{2,1,0:T(8,128)(2,1)S(1)}, bf16[8,192,128]{2,1,0:T(8,128)(2,1)S(1)}, u32[]{:S(2)}, u32[]{:S(2)}) collective-permute-start(bf16[8,192,128]{2,1,0:T(8,128)(2,1)S(1)} %all-to-all-done.refs_0_), channel_id=1, source_target_pairs={{0,8},{8,0},{16,24},{24,16},{1,9},{9,1},{17,25},{25,17},{2,10},{10... | collective-permute-start | bytes 1179656 | tf_op jit(solution)/shard_map/ppermute | solution.py:561
  41.9 1.6 %collective-permute-start.2 = (bf16[8,144,128]{2,1,0:T(8,128)(2,1)S(1)}, bf16[8,144,128]{2,1,0:T(8,128)(2,1)S(1)}, u32[]{:S(2)}, u32[]{:S(2)}) collective-permute-start(bf16[8,144,128]{2,1,0:T(8,128)(2,1)S(1)} %collective-permute-done.refs_1_), channel_id=1, source_target_pairs={{0,8},{8,0},{16,24},{24,16},{1,9},{9,1},{17,25},{25,17},{2,10},{10... | collective-permute-start | bytes 884744 | tf_op jit(solution)/shard_map/ppermute | solution.py:561
  41.9 0.7 copy-start.3
  41.9 0.8 copy-start.2
  54.0 2.3 %collective-permute-start.3 = (bf16[2,8,176,128]{3,2,1,0:T(8,128)(2,1)S(1)}, bf16[2,8,176,128]{3,2,1,0:T(8,128)(2,1)S(1)}, u32[]{:S(2)}, u32[]{:S(2)}) collective-permute-start(bf16[2,8,176,128]{3,2,1,0:T(8,128)(2,1)S(1)} %get-tuple-element.43), channel_id=1, source_target_pairs={{0,8},{8,0},{16,24},{24,16},{1,9},{9,1},{17,25},{25,17},{2,10},{10... | collective-permute-start | bytes 2162696 | tf_op jit(solution)/shard_map/ppermute | solution.py:561
  57.3 23.1 %all-to-all-start.2 = ((bf16[16,176,128]{2,1,0:T(8,128)(2,1)}), bf16[16,176,128]{2,1,0:T(8,128)(2,1)S(1)}, u32[]{:S(2)}, u32[]{:S(2)}) async-start(bf16[16,176,128]{2,1,0:T(8,128)(2,1)} %add_cores.1), calls=%async_computation.2 | async-start | bytes 1441792 | tf_op jit(solution)/shard_map/all_to_all | solution.py:556
  80.4 16.1 %all-to-all-start.3 = ((bf16[16,96,128]{2,1,0:T(8,128)(2,1)}), bf16[16,96,128]{2,1,0:T(8,128)(2,1)S(1)}, u32[]{:S(2)}, u32[]{:S(2)}) async-start(bf16[16,96,128]{2,1,0:T(8,128)(2,1)} %token_grad_message.1), calls=%async_computation.3 | async-start | bytes 786432 | tf_op jit(solution)/shard_map/all_to_all | solution.py:556
  84.1 8.9 %collective-permute-start.4 = (bf16[656,128]{1,0:T(8,128)(2,1)S(1)}, bf16[656,128]{1,0:T(8,128)(2,1)S(1)}, u32[]{:S(2)}, u32[]{:S(2)}) collective-permute-start(bf16[656,128]{1,0:T(8,128)(2,1)S(1)} %sum_sources.1.refs_0_), channel_id=1, source_target_pairs={{0,16},{8,24},{16,0},{24,8},{1,17},{9,25},{17,1},{25,9},{2,18},{10... | collective-permute-start | bytes 503816 | tf_op jit(solution)/shard_map/ppermute | solution.py:566
  86.0 7.0 %collective-permute-start.5 = (bf16[656,128]{1,0:T(8,128)(2,1)S(1)}, bf16[656,128]{1,0:T(8,128)(2,1)S(1)}, u32[]{:S(2)}, u32[]{:S(2)}) collective-permute-start(bf16[656,128]{1,0:T(8,128)(2,1)S(1)} %sum_sources.1.refs_0_), channel_id=1, source_target_pairs={{0,8},{8,0},{16,24},{24,16},{1,9},{9,1},{17,25},{25,17},{2,10},{10... | collective-permute-start | bytes 503816 | tf_op jit(solution)/shard_map/ppermute | solution.py:561
  93.0 1.4 %collective-permute-start.6 = (bf16[656,128]{1,0:T(8,128)(2,1)S(1)}, bf16[656,128]{1,0:T(8,128)(2,1)S(1)}, u32[]{:S(2)}, u32[]{:S(2)}) collective-permute-start(bf16[656,128]{1,0:T(8,128)(2,1)S(1)} %collective-permute-done.4.refs_1_), channel_id=1, source_target_pairs={{0,8},{8,0},{16,24},{24,16},{1,9},{9,1},{17,25},{25,17},{2,10},{10... | collective-permute-start | bytes 503816 | tf_op jit(solution)/shard_map/ppermute | solution.py:561

commit v4 on v3

--- a/solution.py
+++ b/solution.py
@@ -91,7 +91,7 @@
     return lax.dot_general(a, b, (((ca,), (cb,)), ((), ())), preferred_element_type=F32)
 
 
-def call(kernel, out_shape, *args, scratch=(), far=(), limit=20, name=None):
+def call(kernel, out_shape, *args, scratch=(), far=(), limit=24, name=None):
     single = not isinstance(out_shape, (list, tuple))
     return pl.pallas_call(
         kernel,
@@ -479,43 +479,73 @@
     each(p.nblk, one_target)
 
 
-def add_kernel(p, keep, got, *refs):
-    out = refs[-1]
+def pick(p, values, wanted):
+    value = values[0]
+    for i in range(1, len(values)):
+        value = jnp.where(wanted == i, values[i], value)
+    return value
+
+
+def add_cores_kernel(p, grad_x, keep, got, *refs):
+    count = 0 if p.direct else 2
+    out, shares = refs[count], refs[count + 1 :]
+    h, _ = place(p)
 
     def one_target(s):
-        for h in range(p.fold):
-            q = h * p.seq + s
-            out[q] = (keep[h, s].astype(F32) + got[h, s].astype(F32)).astype(BF16)
-            first, last = 2 * p.blk - h * p.mrows, 2 * p.blk + p.yrows - h * p.mrows
+        rows = []
+        for owner in range(p.fold):
+            q = owner * p.seq + s
+            total = (keep[owner, s].astype(F32) + got[owner, s].astype(F32)).astype(BF16)
+            out[q, 0 : p.width] = grad_x[q]
+            out[q, p.width :] = total[p.mrows :]
+            total = total[: p.mrows]
+            first, last = 2 * p.blk - owner * p.mrows, 2 * p.blk + p.yrows - owner * p.mrows
             lo, hi = max(first, 0), min(last, p.mrows)
             if not p.direct and lo < hi:
                 extra = (refs[0][s].astype(F32) + refs[1][s].astype(F32)).astype(BF16)
-                out[q, lo:hi] = extra[lo - first : hi - first]
+                parts = [total[:lo], extra[lo - first : hi - first], total[hi:]]
+                total = jnp.concatenate([part for part in parts if part.shape[0]], axis=0)
+            rows.append(total)
+        for step in range(p.fold):
+            shares[step][s] = pick(p, [rows[(i + step) % p.fold] for i in range(p.fold)], h)
 
     each(p.seq, one_target)
 
 
+def add_fold_kernel(p, *refs):
+    terms, out = refs[:-1], refs[-1]
+
+    def one_target(s):
+        total = terms[0][s].astype(F32)
+        for term in terms[1:]:
+            total += term[s].astype(F32)
+        out[s] = total.astype(BF16)
+
+    each(p.seq, one_target)
+
+
 def sum_kernel(p, got, out):
-    total = got[0, 0 : p.mrows].astype(F32)
-    for q in range(1, p.members):
-        total += got[q, 0 : p.mrows].astype(F32)
-    out[0 : p.mrows] = total.astype(BF16)
+    total = got[0].astype(F32)
+    for q in range(1, p.seq):
+        total += got[q].astype(F32)
+    out[...] = total.astype(BF16)
+
+
+def filter_rows_kernel(p, got, out):
     for q in range(p.members):
-        at = p.mrows + q * p.orows
-        out[at : at + p.orows] = got[q, p.mrows :]
-
-
-def grad_x_kernel(p, got, out):
-    rows = jnp.concatenate([got[q] for q in range(p.members)], axis=0)
+        out[q] = got[q, p.width :]
+
+
+def token_grad_kernel(p, got, out):
+    rows = jnp.concatenate([got[q, 0 : p.width] for q in range(p.members)], axis=0)
     out[...] = rows.T
 
 
-def finish_kernel(p, *refs):
-    pieces, outs = refs[: 2 * p.fold], refs[2 * p.fold :]
-    one, four, filt, conv_value, conv_gate, *small = outs
+def finish_factors_kernel(p, *refs):
+    pieces, (one, four, *small) = refs[: 2 * p.fold], refs[2 * p.fold :]
     share = shares_in_order(p, pieces)
     for part in range(2):
-        rows = [share(part, owner, lambda ref, *_: ref[0 : p.mrows]) for owner in range(p.fold)]
+        rows = [share(part, owner, lambda ref, *_: ref[...]) for owner in range(p.fold)]
         rows = jnp.concatenate(rows, axis=0) if p.fold > 1 else rows[0]
         one[part] = rows[0 : p.blk]
         four[part] = rows[p.blk : 2 * p.blk]
@@ -526,13 +556,15 @@
             small[1][part] = entries[p.pairs :]
         else:
             small[0][part] = entries
+
+
+def finish_filter_kernel(p, *refs):
+    pieces, (filt, conv_value, conv_gate) = refs[: 2 * p.fold], refs[2 * p.fold :]
+    share = shares_in_order(p, pieces)
     turned, columns = [], []
     for q in range(p.members):
-        first = p.mrows + q * p.orows
         rows = [
-            share(c, owner, lambda ref, *_: ref[first : first + p.orows])
-            for c in range(2)
-            for owner in range(p.fold)
+            share(c, owner, lambda ref, *_: ref[q]) for c in range(2) for owner in range(p.fold)
         ]
         rows = jnp.concatenate(rows, axis=0)
         turned.append(rows[0 : p.width])
@@ -619,7 +651,7 @@
         functools.partial(block_factor_kernel, p),
         [shape(p.kgroups, 2 * p.dim, 2 * p.dim)] * 2,
         small.reshape(2, blk, 2 * pairs),
-        limit=48 if p.streamed else 20,
+        limit=48 if p.streamed else 24,
         name="block_factors",
     )
 
@@ -663,54 +695,80 @@
         ]
         + [pltpu.VMEM((2 * p.dim, 2 * p.dim), BF16)] * (2 if p.streamed else 0),
         far=(4, 5) if p.streamed else (),
-        limit=60 if p.streamed else 20,
+        limit=60 if p.streamed else 24,
         name="mixer",
     )
 
-    message = call(
-        functools.partial(add_kernel, p),
-        shape(p.members, p.share, blk),
-        keep,
-        swap(send),
-        *[f.reshape(p.seq, p.yrows, blk) for f in (small if p.direct else (small[0], swap(small[1])))],
-        name="add_cores",
-    )
-    received = shuffle(message)
+    def summed_over_groups(array):
+        if p.groups == 1:
+            return array
+        total = array.astype(F32)
+        for step in range(1, p.groups):
+            total += lax.ppermute(array, "dp", p.across_groups(step)).astype(F32)
+        return total.astype(BF16)
+
     grad_x = call(
         functools.partial(token_grad_message_kernel, p),
         shape(p.members, p.width, blk),
         grad_x,
         name="token_grad_message",
     )
-    received, grad_x = lax.optimization_barrier((received, grad_x))
-    grad_x = shuffle(grad_x)
-    sums = call(
-        functools.partial(sum_kernel, p),
-        shape(p.mrows + p.members * p.orows, blk),
+    message, *shares = call(
+        functools.partial(add_cores_kernel, p),
+        [shape(p.members, p.width + p.orows, blk)] + [shape(p.seq, p.mrows, blk)] * p.fold,
+        grad_x,
+        keep,
+        swap(send),
+        *[f.reshape(p.seq, p.yrows, blk) for f in (small if p.direct else (small[0], swap(small[1])))],
+        name="add_cores",
+    )
+    received = shuffle(message)
+
+    for step in range(1, p.fold):
+        shares[step] = lax.ppermute(shares[step], "dp", p.across_fold(step))
+    message = shares[0]
+    if p.fold > 1:
+        message = call(
+            functools.partial(add_fold_kernel, p),
+            shape(p.seq, p.mrows, blk),
+            *shares,
+            name="add_fold",
+        )
+    message, received = lax.optimization_barrier((message, received))
+    factor_grads = lax.all_to_all(message, "seq", 0, 0, tiled=True)
+
+    rows = call(
+        functools.partial(filter_rows_kernel, p),
+        shape(p.members, p.orows, blk),
         received,
-        name="sum_sources",
-    )
-    if p.groups > 1:
-        total = sums.astype(F32)
-        for step in range(1, p.groups):
-            total += lax.ppermute(sums, "dp", p.across_groups(step)).astype(F32)
-        sums = total.astype(BF16)
-    pieces = gathered(sums, lambda a: a)
+        name="filter_rows",
+    )
+    rows = gathered(summed_over_groups(rows), lambda a: a)
     token_grad = call(
-        functools.partial(grad_x_kernel, p), shape(blk, p.channels), grad_x, name="token_grad"
-    )
-    grad_one, grad_four, grad_filter, sum_value, sum_gate, *small = call(
-        functools.partial(finish_kernel, p),
+        functools.partial(token_grad_kernel, p), shape(blk, p.channels), received, name="token_grad"
+    )
+    grad_filter, sum_value, sum_gate = call(
+        functools.partial(finish_filter_kernel, p),
         [
-            shape(2, blk, blk),
-            shape(2, blk, blk),
             shape(blk, p.channels),
             shape(3, p.channels, dtype=F32),
             shape(3, p.channels, dtype=F32),
-        ]
+        ],
+        *rows,
+        name="finish_filter",
+    )
+    factor_grads, token_grad, grad_filter, sum_value, sum_gate = lax.optimization_barrier(
+        (factor_grads, token_grad, grad_filter, sum_value, sum_gate)
+    )
+    sums = call(
+        functools.partial(sum_kernel, p), shape(p.mrows, blk), factor_grads, name="sum_sources"
+    )
+    grad_one, grad_four, *small = call(
+        functools.partial(finish_factors_kernel, p),
+        [shape(2, blk, blk)] * 2
         + ([shape(2, pairs, p.kloc)] * 2 if p.direct else [shape(2, p.yrows, blk)]),
-        *pieces,
-        name="finish",
+        *gathered(summed_over_groups(sums), lambda a: a),
+        name="finish_factors",
     )
     if p.direct:
         small = [f.reshape(2, p.nblk, p.nblk, p.kloc).transpose(0, 3, 1, 2) for f in small]

time: 98 us -> 97.4 us (level)
  waiting for transfers between devices: 57.7 us -> 53.8 us
  starting transfers between devices: 23.4 us -> 26.2 us
    all_to_all x3 -> x2, waiting for transfers between devices: 22.4 us -> 3.46 us  [shuffle(): lax.all_to_all(array, ('dp', 'seq'), 0, 0, tiled=True, axis_index_groups=...]
    ppermute x0 -> x1, waiting for transfers between devices: none -> 12.5 us  [shards(): shares[step] = lax.ppermute(shares[step], 'dp', p.across_fold(step))]
    all_to_all x0 -> x1, starting transfers between devices: none -> 5.22 us  [shards(): factor_grads = lax.all_to_all(message, 'seq', 0, 0, tiled=True)]
    all_to_all x3 -> x2, starting transfers between devices: 12 us -> 8.43 us  [shuffle(): lax.all_to_all(array, ('dp', 'seq'), 0, 0, tiled=True, axis_index_groups=...]
    ppermute x0 -> x1, starting transfers between devices: none -> 1.93 us  [shards(): shares[step] = lax.ppermute(shares[step], 'dp', p.across_fold(step))]
    all_to_all x0 -> x1, waiting for transfers between devices: none -> 1.5 us  [shards(): factor_grads = lax.all_to_all(message, 'seq', 0, 0, tiled=True)]
    ppermute x2 -> x3, waiting for transfers between devices: 20.5 us -> 21.5 us  [gathered(): pieces.append(lax.ppermute(rows(array), 'dp', p.across_fold(step)))]
    ppermute x2 -> x3, starting transfers between devices: 3.9 us -> 3.12 us  [gathered(): pieces.append(lax.ppermute(rows(array), 'dp', p.across_fold(step)))]
  transfers between devices with their start and end apart: 11 -> 15, of which waited for: 9 -> 12; matrix products, arithmetic and copies ran while one was open for 0% -> 0% of each run, Pallas kernels for 4% -> 4%
where the time goes in v4:
time: 97.4 us; the launch traced here: 96.8 us
  waiting for transfers between devices  53.8 us (55%)
  starting transfers between devices  26.2 us (27%)
  Pallas kernels  15.1 us (16%)
    ppermute x3, waiting for transfers between devices, gathered(): pieces.append(lax.ppermute(rows(array), 'dp', p.across_fold(step)))  21.5 us
    pallas_call x13, Pallas kernels, call(): pl.pallas_call(kernel, out_shape=out_shape, in_specs=[FAR if i in far els...  15.1 us
    ppermute x1, waiting for transfers between devices, shards(): shares[step] = lax.ppermute(shares[step], 'dp', p.across_fold(step))  12.5 us
    all_to_all x1, waiting for transfers between devices, shards(): factors = lax.all_to_all(message, 'seq', 0, 0, tiled=True)  10.5 us
    all_to_all x2, starting transfers between devices, shuffle(): lax.all_to_all(array, ('dp', 'seq'), 0, 0, tiled=True, axis_index_groups=...  8.43 us
    all_to_all x1, starting transfers between devices, shards(): factors = lax.all_to_all(message, 'seq', 0, 0, tiled=True)  7.42 us
    all_to_all x1, starting transfers between devices, shards(): factor_grads = lax.all_to_all(message, 'seq', 0, 0, tiled=True)  5.22 us
    ppermute x7, waiting for transfers between devices, swap(): return lax.ppermute(array, 'dp', p.across_cores())  4.31 us
  transfers between devices with their start and end apart: 15, of which 12 were waited for; matrix products, arithmetic and copies ran while one was open for 0% of the time, Pallas kernels for 4%

profile of v4, /device:TPU:0, one launch (start us, length us, event | category | flops | bytes accessed | tf_op | source)
XLA Modules:
  0.0 96.8 jit_solution(15824323105430524256)
XLA Ops:
  0.6 1.9 %factor_message.1 = bf16[8,192,128]{2,1,0:T(8,128)(2,1)} custom-call(bf16[128,1536]{1,0:T(8,128)(2,1)} %bitcast.32, bf16[2,128,128]{2,1,0:T(8,128)(2,1)} %bitcast.33, bf16[2,128,128]{2,1,0:T(8,128)(2,1)} %bitcast.34, bf16[2,64,16]{2,1,0:T(8,128)(2,1)} %bitcast.35, bf16[2,64,16]{2,1,0:T(8,128)(2,1)} %bitcast.36), custom_call_target="tpu_custom_call" | custom-call | tf_op jit(solution)/shard_map/factor_message/pallas_call | solution.py:96
  2.5 0.0 copy-start
  2.5 0.0 copy-start.1
  2.6 7.4 %all-to-all-start = ((bf16[8,192,128]{2,1,0:T(8,128)(2,1)}), bf16[8,192,128]{2,1,0:T(8,128)(2,1)S(1)}, u32[]{:S(2)}, u32[]{:S(2)}) async-start(bf16[8,192,128]{2,1,0:T(8,128)(2,1)} %factor_message.1), calls=%async_computation | async-start | bytes 786432 | tf_op jit(solution)/shard_map/all_to_all | solution.py:627
  10.0 0.0 copy-done
  10.0 0.0 copy-done.1
  10.0 1.2 %token_message.1 = bf16[16,192,128]{2,1,0:T(8,128)(2,1)} custom-call(bf16[128,1536]{1,0:T(8,128)(2,1)S(1)} %bitcast.28, bf16[128,1536]{1,0:T(8,128)(2,1)S(1)} %bitcast.29), custom_call_target="tpu_custom_call" | custom-call | tf_op jit(solution)/shard_map/token_message/pallas_call | solution.py:96
  11.1 10.5 %all-to-all-done.refs_0_ = bf16[8,192,128]{2,1,0:T(8,128)(2,1)S(1)} async-done(((bf16[8,192,128]{2,1,0:T(8,128)(2,1)}), bf16[8,192,128]{2,1,0:T(8,128)(2,1)S(1)}, u32[]{:S(2)}, u32[]{:S(2)}) %all-to-all-start) | async-done | bytes 393248 | tf_op jit(solution)/shard_map/all_to_all | solution.py:627
  21.7 4.7 %all-to-all-start.1 = ((bf16[16,192,128]{2,1,0:T(8,128)(2,1)}), bf16[16,192,128]{2,1,0:T(8,128)(2,1)S(1)}, u32[]{:S(2)}, u32[]{:S(2)}) async-start(bf16[16,192,128]{2,1,0:T(8,128)(2,1)} %token_message.1), calls=%async_computation.1 | async-start | bytes 1572864 | tf_op jit(solution)/shard_map/all_to_all | solution.py:588
  26.4 2.0 %collective-permute-start = (bf16[8,144,128]{2,1,0:T(8,128)(2,1)S(1)}, bf16[8,144,128]{2,1,0:T(8,128)(2,1)S(1)}, u32[]{:S(2)}, u32[]{:S(2)}) collective-permute-start(bf16[8,144,128]{2,1,0:T(8,128)(2,1)S(1)} %slice.4), channel_id=1, source_target_pairs={{0,16},{8,24},{16,0},{24,8},{1,17},{9,25},{17,1},{25,9},{2,18},{10... | collective-permute-start | bytes 884744 | tf_op jit(solution)/shard_map/ppermute | solution.py:598
  28.4 0.0 collective-permute-start.1
  28.4 13.6 %collective-permute-done.refs_1_ = bf16[8,144,128]{2,1,0:T(8,128)(2,1)S(1)} collective-permute-done((bf16[8,144,128]{2,1,0:T(8,128)(2,1)S(1)}, bf16[8,144,128]{2,1,0:T(8,128)(2,1)S(1)}, u32[]{:S(2)}, u32[]{:S(2)}) %collective-permute-start) | collective-permute-done | bytes 294944 | tf_op jit(solution)/shard_map/ppermute | solution.py:598
  41.9 0.0 collective-permute-start.2
  41.9 0.0 copy-start.3
  41.9 0.0 copy-start.2
  41.9 0.7 copy-done.3
  42.7 0.0 copy-done.2
  42.7 0.1 fusion
  42.8 0.1 pad_maximum_fusion.taps
  42.8 0.0 collective-permute-done.1.refs_2_
  42.8 0.7 collective-permute-done.2.refs_3_
  43.5 3.2 %all-to-all-done.1.tokens_in = bf16[16,192,128]{2,1,0:T(8,128)(2,1)S(1)} async-done(((bf16[16,192,128]{2,1,0:T(8,128)(2,1)}), bf16[16,192,128]{2,1,0:T(8,128)(2,1)S(1)}, u32[]{:S(2)}, u32[]{:S(2)}) %all-to-all-start.1) | async-done | bytes 786464 | tf_op jit(solution)/shard_map/all_to_all | solution.py:588
  46.7 0.7 prepare.1
  47.4 0.5 block_factors.1
  47.8 6.2 %mixer.1 = (bf16[8,128,192]{2,1,0:T(8,128)(2,1)S(1)}, bf16[2,8,176,128]{3,2,1,0:T(8,128)(2,1)S(1)}, bf16[2,8,176,128]{3,2,1,0:T(8,128)(2,1)S(1)}) custom-call(bf16[16,192,128]{2,1,0:T(8,128)(2,1)S(1)} %all-to-all-done.1.tokens_in, f32[6,192]{1,0:T(8,128)S(1)} %pad_maximum_fusion.taps, bf16[8,256,128]{2,1,0:T(8,128)(2,1)S(1)} %get-tuple-element.44.one, ...), custom_call_target="tpu_custom_call" | custom-call | tf_op jit(solution)/shard_map/mixer/pallas_call | solution.py:96
  54.0 0.1 collective-permute-start.3
  54.1 0.2 token_grad_message.1.grad_x
  54.3 2.0 %collective-permute-done.3.got = bf16[2,8,176,128]{3,2,1,0:T(8,128)(2,1)S(1)} collective-permute-done((bf16[2,8,176,128]{3,2,1,0:T(8,128)(2,1)S(1)}, bf16[2,8,176,128]{3,2,1,0:T(8,128)(2,1)S(1)}, u32[]{:S(2)}, u32[]{:S(2)}) %collective-permute-start.3) | collective-permute-done | bytes 720928 | tf_op jit(solution)/shard_map/ppermute | solution.py:593
  56.3 0.9 add_cores.1
  57.1 3.8 %all-to-all-start.2 = ((bf16[16,128,128]{2,1,0:T(8,128)(2,1)}), bf16[16,128,128]{2,1,0:T(8,128)(2,1)S(1)}, u32[]{:S(2)}, u32[]{:S(2)}) async-start(bf16[16,128,128]{2,1,0:T(8,128)(2,1)} %get-tuple-element.55), calls=%async_computation.2 | async-start | bytes 1048576 | tf_op jit(solution)/shard_map/all_to_all | solution.py:588
  60.9 1.9 %collective-permute-start.4 = (bf16[8,144,128]{2,1,0:T(8,128)(2,1)S(1)}, bf16[8,144,128]{2,1,0:T(8,128)(2,1)S(1)}, u32[]{:S(2)}, u32[]{:S(2)}) collective-permute-start(bf16[8,144,128]{2,1,0:T(8,128)(2,1)S(1)} %get-tuple-element.54), channel_id=1, source_target_pairs={{0,16},{8,24},{16,0},{24,8},{1,17},{9,25},{17,1},{25,9},{2,18},{10... | collective-permute-start | bytes 884744 | tf_op jit(solution)/shard_map/ppermute | solution.py:728
  62.8 12.5 %collective-permute-done.4.refs_1_ = bf16[8,144,128]{2,1,0:T(8,128)(2,1)S(1)} collective-permute-done((bf16[8,144,128]{2,1,0:T(8,128)(2,1)S(1)}, bf16[8,144,128]{2,1,0:T(8,128)(2,1)S(1)}, u32[]{:S(2)}, u32[]{:S(2)}) %collective-permute-start.4) | collective-permute-done | bytes 294944 | tf_op jit(solution)/shard_map/ppermute | solution.py:728
  75.4 0.8 add_fold.1
  76.2 0.3 all-to-all-done.2.got
  76.5 5.2 %all-to-all-start.3 = ((bf16[8,144,128]{2,1,0:T(8,128)(2,1)}), bf16[8,144,128]{2,1,0:T(8,128)(2,1)S(1)}, u32[]{:S(2)}, u32[]{:S(2)}) async-start(bf16[8,144,128]{2,1,0:T(8,128)(2,1)} %add_fold.1), calls=%async_computation.3 | async-start | bytes 589824 | tf_op jit(solution)/shard_map/all_to_all | solution.py:738
  81.7 0.6 collective-permute-start.5
  82.3 0.0 collective-permute-start.6
  82.3 4.4 %collective-permute-done.5.refs_1_ = bf16[16,32,128]{2,1,0:T(8,128)(2,1)S(1)} collective-permute-done((bf16[16,32,128]{2,1,0:T(8,128)(2,1)S(1)}, bf16[16,32,128]{2,1,0:T(8,128)(2,1)S(1)}, u32[]{:S(2)}, u32[]{:S(2)}) %collective-permute-start.5) | collective-permute-done | bytes 131104 | tf_op jit(solution)/shard_map/ppermute | solution.py:598
  86.7 0.0 collective-permute-start.7
  86.7 0.9 token_grad.1
  87.6 0.0 collective-permute-done.6.refs_2_
  87.6 0.4 collective-permute-done.7.refs_3_
  88.1 1.2 %finish_filter.1 = (bf16[128,1536]{1,0:T(8,128)(2,1)}, f32[3,1536]{1,0:T(4,128)}, f32[3,1536]{1,0:T(4,128)}) custom-call(bf16[16,32,128]{2,1,0:T(8,128)(2,1)S(1)} %filter_rows.1.refs_0_, bf16[16,32,128]{2,1,0:T(8,128)(2,1)S(1)} %collective-permute-done.5.refs_1_, bf16[16,32,128]{2,1,0:T(8,128)(2,1)S(1)} %collective-permute-done.6.refs_2_, ...), custom_call_target="tpu_custom_call" | custom-call | tf_op jit(solution)/shard_map/finish_filter/pallas_call | solution.py:96
  89.3 1.5 %all-to-all-done.3.got = bf16[8,144,128]{2,1,0:T(8,128)(2,1)S(1)} async-done(((bf16[8,144,128]{2,1,0:T(8,128)(2,1)}), bf16[8,144,128]{2,1,0:T(8,128)(2,1)S(1)}, u32[]{:S(2)}, u32[]{:S(2)}) %all-to-all-start.3) | async-done | bytes 294944 | tf_op jit(solution)/shard_map/all_to_all | solution.py:738
  90.8 0.5 collective-permute-start.8
  91.4 0.0 collective-permute-start.9
  91.4 3.5 %collective-permute-done.8.refs_1_ = bf16[144,128]{1,0:T(8,128)(2,1)S(1)} collective-permute-done((bf16[144,128]{1,0:T(8,128)(2,1)S(1)}, bf16[144,128]{1,0:T(8,128)(2,1)S(1)}, u32[]{:S(2)}, u32[]{:S(2)}) %collective-permute-start.8) | collective-permute-done | bytes 36896 | tf_op jit(solution)/shard_map/ppermute | solution.py:598
  94.9 0.0 collective-permute-start.10
  94.9 0.0 collective-permute-done.9.refs_2_
  94.9 1.2 %collective-permute-done.10.refs_3_ = bf16[144,128]{1,0:T(8,128)(2,1)S(1)} collective-permute-done((bf16[144,128]{1,0:T(8,128)(2,1)S(1)}, bf16[144,128]{1,0:T(8,128)(2,1)S(1)}, u32[]{:S(2)}, u32[]{:S(2)}) %collective-permute-start.10) | collective-permute-done | bytes 36896 | tf_op jit(solution)/shard_map/ppermute | solution.py:593
  96.1 0.7 finish_factors.1
  (3 shorter events, 0.1 us)
Async XLA Ops:
  2.5 7.5 %copy-start = (bf16[1,128,1536]{2,1,0:T(8,128)(2,1)S(1)}, bf16[1,128,1536]{2,1,0:T(8,128)(2,1)}, u32[]{:S(2)}) copy-start(bf16[1,128,1536]{2,1,0:T(8,128)(2,1)} %param.9) | copy-start | bytes 1179652
  2.5 7.4 %copy-start.1 = (bf16[1,128,1536]{2,1,0:T(8,128)(2,1)S(1)}, bf16[1,128,1536]{2,1,0:T(8,128)(2,1)}, u32[]{:S(2)}) copy-start(bf16[1,128,1536]{2,1,0:T(8,128)(2,1)} %param.10) | copy-start | bytes 1179652
  2.6 19.1 %all-to-all-start = ((bf16[8,192,128]{2,1,0:T(8,128)(2,1)}), bf16[8,192,128]{2,1,0:T(8,128)(2,1)S(1)}, u32[]{:S(2)}, u32[]{:S(2)}) async-start(bf16[8,192,128]{2,1,0:T(8,128)(2,1)} %factor_message.1), calls=%async_computation | async-start | bytes 786432 | tf_op jit(solution)/shard_map/all_to_all | solution.py:627
  21.7 25.0 %all-to-all-start.1 = ((bf16[16,192,128]{2,1,0:T(8,128)(2,1)}), bf16[16,192,128]{2,1,0:T(8,128)(2,1)S(1)}, u32[]{:S(2)}, u32[]{:S(2)}) async-start(bf16[16,192,128]{2,1,0:T(8,128)(2,1)} %token_message.1), calls=%async_computation.1 | async-start | bytes 1572864 | tf_op jit(solution)/shard_map/all_to_all | solution.py:588
  26.4 15.6 %collective-permute-start = (bf16[8,144,128]{2,1,0:T(8,128)(2,1)S(1)}, bf16[8,144,128]{2,1,0:T(8,128)(2,1)S(1)}, u32[]{:S(2)}, u32[]{:S(2)}) collective-permute-start(bf16[8,144,128]{2,1,0:T(8,128)(2,1)S(1)} %slice.4), channel_id=1, source_target_pairs={{0,16},{8,24},{16,0},{24,8},{1,17},{9,25},{17,1},{25,9},{2,18},{10... | collective-permute-start | bytes 884744 | tf_op jit(solution)/shard_map/ppermute | solution.py:598
  28.4 14.5 %collective-permute-start.1 = (bf16[8,192,128]{2,1,0:T(8,128)(2,1)S(1)}, bf16[8,192,128]{2,1,0:T(8,128)(2,1)S(1)}, u32[]{:S(2)}, u32[]{:S(2)}) collective-permute-start(bf16[8,192,128]{2,1,0:T(8,128)(2,1)S(1)} %all-to-all-done.refs_0_), channel_id=1, source_target_pairs={{0,8},{8,0},{16,24},{24,16},{1,9},{9,1},{17,25},{25,17},{2,10},{10... | collective-permute-start | bytes 1179656 | tf_op jit(solution)/shard_map/ppermute | solution.py:593
  41.9 1.6 %collective-permute-start.2 = (bf16[8,144,128]{2,1,0:T(8,128)(2,1)S(1)}, bf16[8,144,128]{2,1,0:T(8,128)(2,1)S(1)}, u32[]{:S(2)}, u32[]{:S(2)}) collective-permute-start(bf16[8,144,128]{2,1,0:T(8,128)(2,1)S(1)} %collective-permute-done.refs_1_), channel_id=1, source_target_pairs={{0,8},{8,0},{16,24},{24,16},{1,9},{9,1},{17,25},{25,17},{2,10},{10... | collective-permute-start | bytes 884744 | tf_op jit(solution)/shard_map/ppermute | solution.py:593
  41.9 0.7 copy-start.3
  41.9 0.8 copy-start.2
  54.0 2.3 %collective-permute-start.3 = (bf16[2,8,176,128]{3,2,1,0:T(8,128)(2,1)S(1)}, bf16[2,8,176,128]{3,2,1,0:T(8,128)(2,1)S(1)}, u32[]{:S(2)}, u32[]{:S(2)}) collective-permute-start(bf16[2,8,176,128]{3,2,1,0:T(8,128)(2,1)S(1)} %get-tuple-element.52), channel_id=1, source_target_pairs={{0,8},{8,0},{16,24},{24,16},{1,9},{9,1},{17,25},{25,17},{2,10},{10... | collective-permute-start | bytes 2162696 | tf_op jit(solution)/shard_map/ppermute | solution.py:593
  57.1 19.3 %all-to-all-start.2 = ((bf16[16,128,128]{2,1,0:T(8,128)(2,1)}), bf16[16,128,128]{2,1,0:T(8,128)(2,1)S(1)}, u32[]{:S(2)}, u32[]{:S(2)}) async-start(bf16[16,128,128]{2,1,0:T(8,128)(2,1)} %get-tuple-element.55), calls=%async_computation.2 | async-start | bytes 1048576 | tf_op jit(solution)/shard_map/all_to_all | solution.py:588
  60.9 14.5 %collective-permute-start.4 = (bf16[8,144,128]{2,1,0:T(8,128)(2,1)S(1)}, bf16[8,144,128]{2,1,0:T(8,128)(2,1)S(1)}, u32[]{:S(2)}, u32[]{:S(2)}) collective-permute-start(bf16[8,144,128]{2,1,0:T(8,128)(2,1)S(1)} %get-tuple-element.54), channel_id=1, source_target_pairs={{0,16},{8,24},{16,0},{24,8},{1,17},{9,25},{17,1},{25,9},{2,18},{10... | collective-permute-start | bytes 884744 | tf_op jit(solution)/shard_map/ppermute | solution.py:728
  76.5 14.3 %all-to-all-start.3 = ((bf16[8,144,128]{2,1,0:T(8,128)(2,1)}), bf16[8,144,128]{2,1,0:T(8,128)(2,1)S(1)}, u32[]{:S(2)}, u32[]{:S(2)}) async-start(bf16[8,144,128]{2,1,0:T(8,128)(2,1)} %add_fold.1), calls=%async_computation.3 | async-start | bytes 589824 | tf_op jit(solution)/shard_map/all_to_all | solution.py:738
  81.7 5.0 %collective-permute-start.5 = (bf16[16,32,128]{2,1,0:T(8,128)(2,1)S(1)}, bf16[16,32,128]{2,1,0:T(8,128)(2,1)S(1)}, u32[]{:S(2)}, u32[]{:S(2)}) collective-permute-start(bf16[16,32,128]{2,1,0:T(8,128)(2,1)S(1)} %filter_rows.1.refs_0_), channel_id=1, source_target_pairs={{0,16},{8,24},{16,0},{24,8},{1,17},{9,25},{17,1},{25,9},{2,18},{10... | collective-permute-start | bytes 393224 | tf_op jit(solution)/shard_map/ppermute | solution.py:598
  82.3 5.4 %collective-permute-start.6 = (bf16[16,32,128]{2,1,0:T(8,128)(2,1)S(1)}, bf16[16,32,128]{2,1,0:T(8,128)(2,1)S(1)}, u32[]{:S(2)}, u32[]{:S(2)}) collective-permute-start(bf16[16,32,128]{2,1,0:T(8,128)(2,1)S(1)} %filter_rows.1.refs_0_), channel_id=1, source_target_pairs={{0,8},{8,0},{16,24},{24,16},{1,9},{9,1},{17,25},{25,17},{2,10},{10... | collective-permute-start | bytes 393224 | tf_op jit(solution)/shard_map/ppermute | solution.py:593
  86.7 1.3 %collective-permute-start.7 = (bf16[16,32,128]{2,1,0:T(8,128)(2,1)S(1)}, bf16[16,32,128]{2,1,0:T(8,128)(2,1)S(1)}, u32[]{:S(2)}, u32[]{:S(2)}) collective-permute-start(bf16[16,32,128]{2,1,0:T(8,128)(2,1)S(1)} %collective-permute-done.5.refs_1_), channel_id=1, source_target_pairs={{0,8},{8,0},{16,24},{24,16},{1,9},{9,1},{17,25},{25,17},{2,10},{10... | collective-permute-start | bytes 393224 | tf_op jit(solution)/shard_map/ppermute | solution.py:593
  90.8 4.0 %collective-permute-start.8 = (bf16[144,128]{1,0:T(8,128)(2,1)S(1)}, bf16[144,128]{1,0:T(8,128)(2,1)S(1)}, u32[]{:S(2)}, u32[]{:S(2)}) collective-permute-start(bf16[144,128]{1,0:T(8,128)(2,1)S(1)} %sum_sources.1.refs_0_), channel_id=1, source_target_pairs={{0,16},{8,24},{16,0},{24,8},{1,17},{9,25},{17,1},{25,9},{2,18},{10... | collective-permute-start | bytes 110600 | tf_op jit(solution)/shard_map/ppermute | solution.py:598
  91.4 3.5 %collective-permute-start.9 = (bf16[144,128]{1,0:T(8,128)(2,1)S(1)}, bf16[144,128]{1,0:T(8,128)(2,1)S(1)}, u32[]{:S(2)}, u32[]{:S(2)}) collective-permute-start(bf16[144,128]{1,0:T(8,128)(2,1)S(1)} %sum_sources.1.refs_0_), channel_id=1, source_target_pairs={{0,8},{8,0},{16,24},{24,16},{1,9},{9,1},{17,25},{25,17},{2,10},{10... | collective-permute-start | bytes 110600 | tf_op jit(solution)/shard_map/ppermute | solution.py:593
  94.9 1.2 %collective-permute-start.10 = (bf16[144,128]{1,0:T(8,128)(2,1)S(1)}, bf16[144,128]{1,0:T(8,128)(2,1)S(1)}, u32[]{:S(2)}, u32[]{:S(2)}) collective-permute-start(bf16[144,128]{1,0:T(8,128)(2,1)S(1)} %collective-permute-done.8.refs_1_), channel_id=1, source_target_pairs={{0,8},{8,0},{16,24},{24,16},{1,9},{9,1},{17,25},{25,17},{2,10},{10... | collective-permute-start | bytes 110600 | tf_op jit(solution)/shard_map/ppermute | solution.py:593

commit v5 on v4

--- a/solution.py
+++ b/solution.py
@@ -21,6 +21,9 @@
         self.channels = tokens.shape[-1]
         assert tokens.shape[1] == self.blk and dp % 2 == 0
         self.nblk = seq
+        self.near = 2 if seq % 2 == 0 else 1
+        self.layers = seq // self.near
+        self.layer_groups = [list(range(y, seq, self.near)) for y in range(self.near)]
         self.kloc = mix_two.shape[1]
         half_dp = dp // 2
         self.fold = max(
@@ -61,14 +64,25 @@
     def across_cores(self):
         return [(d, d ^ 1) for d in range(self.dp)]
 
-    def across_fold(self, step):
+    def across_fold(self, step, side=0):
         moves = []
         for g in range(self.groups):
             for h in range(self.fold):
                 for core in range(2):
                     source = (g * self.fold + h) * 2 + core
-                    moves.append((source, (g * self.fold + (h + step) % self.fold) * 2 + core))
+                    target = (g * self.fold + (h + step) % self.fold) * 2 + (core ^ side)
+                    moves.append((source, target))
         return moves
+
+    def across_plane(self, step, near_step, side=0):
+        return [
+            (source * self.seq + s, target * self.seq + s // self.near * self.near + (s + near_step) % self.near)
+            for source, target in self.across_fold(step, side)
+            for s in range(self.seq)
+        ]
+
+    def plane(self):
+        return [(step, near_step) for step in range(self.fold) for near_step in range(self.near)]
 
     def across_groups(self, step):
         block = 2 * self.fold
@@ -142,14 +156,27 @@
     copies[0].wait()
     turned[...] = filt[...].T
 
-    def one_target(s):
-        out[s, 0 : p.mrows] = mine
-        logs = turned[rows_at(s * p.width, p.width)]
-        if p.cores_share:
-            logs = jnp.where(core == 0, logs[: p.frows], logs[p.frows :])
-        out[s, p.mrows :] = logs
-
-    each(p.seq, one_target)
+    def one_layer(z):
+        out[z, 0 : p.mrows] = mine
+        for near in range(p.near):
+            logs = turned[rows_at((z * p.near + near) * p.width, p.width)]
+            if p.cores_share:
+                logs = jnp.where(core == 0, logs[: p.frows], logs[p.frows :])
+            out[z, p.mrows + near * p.frows : p.mrows + (near + 1) * p.frows] = logs
+
+    each(p.layers, one_layer)
+
+
+def near_message_kernel(p, got, *outs):
+    y = lax.axis_index("seq") % p.near
+
+    def one_layer(z):
+        logs = [got[z, p.mrows + i * p.frows : p.mrows + (i + 1) * p.frows] for i in range(p.near)]
+        for step in range(p.near):
+            outs[step][z, 0 : p.mrows] = got[z, 0 : p.mrows]
+            outs[step][z, p.mrows :] = pick(p, [logs[(i + step) % p.near] for i in range(p.near)], y)
+
+    each(p.layers, one_layer)
 
 
 def token_message_kernel(p, tokens, upstream, out):
@@ -180,28 +207,40 @@
 
 
 def prepare_kernel(p, *refs):
-    pieces, (one, four, small, filt) = refs[: 2 * p.fold], refs[2 * p.fold :]
-    share = shares_in_order(p, pieces)
+    count = 2 * len(p.plane())
+    pieces, (one, four, small, filt) = refs[:count], refs[count:]
     _, core = place(p)
-
-    def one_block(i):
-        for part in range(2):
-            rows = [share(part, owner, lambda ref, *_: ref[i, 0 : p.mrows]) for owner in range(p.fold)]
-            rows = jnp.concatenate(rows, axis=0) if p.fold > 1 else rows[0]
-            one[i, part * p.blk : (part + 1) * p.blk] = rows[0 : p.blk]
-            factor = rows[p.blk : 2 * p.blk]
-            four[i, :, part * p.blk : (part + 1) * p.blk] = factor if part == 0 else -factor
-            small[part, i] = rows[2 * p.blk : 2 * p.blk + p.yrows]
-        logs = pieces[0][i, p.mrows :]
-        if p.cores_share:
-            other = pieces[p.fold][i, p.mrows :]
-            logs = [jnp.where(core == 0, logs, other), jnp.where(core == 0, other, logs)]
-            logs = jnp.concatenate(logs, axis=0)
-        if p.fold > 1:
-            logs = jnp.concatenate([logs] * p.fold, axis=0)
-        filt[i] = jnp.exp(logs.T.astype(F32))
-
-    each(p.nblk, one_block)
+    y = lax.axis_index("seq") % p.near
+
+    def one_layer(z):
+        for near in range(p.near):
+            i = z * p.near + near
+
+            def from_near(part):
+                return pick(p, [part(pieces[(near - at) % p.near :: p.near]) for at in range(p.near)], y)
+
+            for side in range(2):
+                rows = [
+                    from_near(
+                        lambda own: shares_in_order(p, own)(side, owner, lambda ref, *_: ref[z, 0 : p.mrows])
+                    )
+                    for owner in range(p.fold)
+                ]
+                rows = jnp.concatenate(rows, axis=0) if p.fold > 1 else rows[0]
+                one[i, side * p.blk : (side + 1) * p.blk] = rows[0 : p.blk]
+                factor = rows[p.blk : 2 * p.blk]
+                four[i, :, side * p.blk : (side + 1) * p.blk] = factor if side == 0 else -factor
+                small[side, i] = rows[2 * p.blk : 2 * p.blk + p.yrows]
+            logs = from_near(lambda own: own[0][z, p.mrows :])
+            if p.cores_share:
+                other = from_near(lambda own: own[p.fold][z, p.mrows :])
+                logs = [jnp.where(core == 0, logs, other), jnp.where(core == 0, other, logs)]
+                logs = jnp.concatenate(logs, axis=0)
+            if p.fold > 1:
+                logs = jnp.concatenate([logs] * p.fold, axis=0)
+            filt[i] = jnp.exp(logs.T.astype(F32))
+
+    each(p.layers, one_layer)
 
 
 def iota(dims, axis):
@@ -490,43 +529,50 @@
     count = 0 if p.direct else 2
     out, shares = refs[count], refs[count + 1 :]
     h, _ = place(p)
-
-    def one_target(s):
-        rows = []
-        for owner in range(p.fold):
-            q = owner * p.seq + s
-            total = (keep[owner, s].astype(F32) + got[owner, s].astype(F32)).astype(BF16)
-            out[q, 0 : p.width] = grad_x[q]
-            out[q, p.width :] = total[p.mrows :]
-            total = total[: p.mrows]
-            first, last = 2 * p.blk - owner * p.mrows, 2 * p.blk + p.yrows - owner * p.mrows
-            lo, hi = max(first, 0), min(last, p.mrows)
-            if not p.direct and lo < hi:
-                extra = (refs[0][s].astype(F32) + refs[1][s].astype(F32)).astype(BF16)
-                parts = [total[:lo], extra[lo - first : hi - first], total[hi:]]
-                total = jnp.concatenate([part for part in parts if part.shape[0]], axis=0)
-            rows.append(total)
-        for step in range(p.fold):
-            shares[step][s] = pick(p, [rows[(i + step) % p.fold] for i in range(p.fold)], h)
-
-    each(p.seq, one_target)
+    y = lax.axis_index("seq") % p.near
+
+    def one_layer(z):
+        rows = {}
+        for near in range(p.near):
+            s = z * p.near + near
+            for owner in range(p.fold):
+                q = owner * p.seq + s
+                total = (keep[owner, s].astype(F32) + got[owner, s].astype(F32)).astype(BF16)
+                out[q, 0 : p.width] = grad_x[q]
+                out[q, p.width :] = total[p.mrows :]
+                total = total[: p.mrows]
+                first, last = 2 * p.blk - owner * p.mrows, 2 * p.blk + p.yrows - owner * p.mrows
+                lo, hi = max(first, 0), min(last, p.mrows)
+                if not p.direct and lo < hi:
+                    extra = (refs[0][s].astype(F32) + refs[1][s].astype(F32)).astype(BF16)
+                    parts = [total[:lo], extra[lo - first : hi - first], total[hi:]]
+                    total = jnp.concatenate([part for part in parts if part.shape[0]], axis=0)
+                rows[owner, near] = total
+        for share, (step, near_step) in zip(shares, p.plane()):
+            by_near = [
+                pick(p, [rows[(i + step) % p.fold, (near + near_step) % p.near] for i in range(p.fold)], h)
+                for near in range(p.near)
+            ]
+            share[z] = pick(p, by_near, y)
+
+    each(p.layers, one_layer)
 
 
 def add_fold_kernel(p, *refs):
     terms, out = refs[:-1], refs[-1]
 
-    def one_target(s):
-        total = terms[0][s].astype(F32)
+    def one_layer(z):
+        total = terms[0][z].astype(F32)
         for term in terms[1:]:
-            total += term[s].astype(F32)
-        out[s] = total.astype(BF16)
-
-    each(p.seq, one_target)
+            total += term[z].astype(F32)
+        out[z] = total.astype(BF16)
+
+    each(p.layers, one_layer)
 
 
 def sum_kernel(p, got, out):
     total = got[0].astype(F32)
-    for q in range(1, p.seq):
+    for q in range(1, p.layers):
         total += got[q].astype(F32)
     out[...] = total.astype(BF16)
 
@@ -589,6 +635,11 @@
             array, ("dp", "seq"), 0, 0, tiled=True, axis_index_groups=p.group_lists
         )
 
+    def across_layers(array):
+        return lax.all_to_all(
+            array, "seq", 0, 0, tiled=True, axis_index_groups=p.layer_groups
+        )
+
     def swap(array):
         return lax.ppermute(array, "dp", p.across_cores())
 
@@ -597,6 +648,13 @@
         for step in range(1, p.fold):
             pieces.append(lax.ppermute(rows(array), "dp", p.across_fold(step)))
         return pieces + [swap(piece) for piece in pieces]
+
+    def gathered_at_once(array):
+        return [
+            lax.ppermute(array, "dp", p.across_fold(step, side)) if step or side else array
+            for side in range(2)
+            for step in range(p.fold)
+        ]
 
     if p.direct:
         small = [f.transpose(0, 2, 3, 1).reshape(2, pairs, p.kloc) for f in (mix_two, mix_three)]
@@ -611,7 +669,7 @@
     ]
     message = call(
         functools.partial(factor_message_kernel, p),
-        shape(p.seq, p.mrows + p.frows, blk),
+        shape(p.layers, p.mrows + p.near * p.frows, blk),
         *far,
         scratch=[pltpu.VMEM((blk, p.channels // p.fold), BF16)]
         + [pltpu.VMEM(f.shape[1:], BF16) for f in far[1:]]
@@ -624,8 +682,20 @@
         limit=60,
         name="factor_message",
     )
-    factors = lax.all_to_all(message, "seq", 0, 0, tiled=True)
-    pieces = gathered(factors, lambda a: a[:, : p.mrows])
+    factors = across_layers(message)
+    near_messages = [factors]
+    if p.near > 1:
+        near_messages = call(
+            functools.partial(near_message_kernel, p),
+            [shape(p.layers, p.mrows + p.frows, blk)] * p.near,
+            factors,
+            name="near_message",
+        )
+    pieces = [near_messages[0]]
+    for step, near_step in p.plane()[1:]:
+        piece = near_messages[near_step] if step == 0 else factors[:, : p.mrows]
+        pieces.append(lax.ppermute(piece, ("dp", "seq"), p.across_plane(step, near_step)))
+    pieces += [swap(piece) for piece in pieces]
 
     message = call(
         functools.partial(token_message_kernel, p),
@@ -715,7 +785,8 @@
     )
     message, *shares = call(
         functools.partial(add_cores_kernel, p),
-        [shape(p.members, p.width + p.orows, blk)] + [shape(p.seq, p.mrows, blk)] * p.fold,
+        [shape(p.members, p.width + p.orows, blk)]
+        + [shape(p.layers, p.mrows, blk)] * len(p.plane()),
         grad_x,
         keep,
         swap(send),
@@ -724,18 +795,20 @@
     )
     received = shuffle(message)
 
-    for step in range(1, p.fold):
-        shares[step] = lax.ppermute(shares[step], "dp", p.across_fold(step))
     message = shares[0]
-    if p.fold > 1:
+    if len(shares) > 1:
         message = call(
             functools.partial(add_fold_kernel, p),
-            shape(p.seq, p.mrows, blk),
-            *shares,
+            shape(p.layers, p.mrows, blk),
+            message,
+            *[
+                lax.ppermute(share, ("dp", "seq"), p.across_plane(*steps))
+                for share, steps in zip(shares[1:], p.plane()[1:])
+            ],
             name="add_fold",
         )
     message, received = lax.optimization_barrier((message, received))
-    factor_grads = lax.all_to_all(message, "seq", 0, 0, tiled=True)
+    factor_grads = across_layers(message)
 
     rows = call(
         functools.partial(filter_rows_kernel, p),
@@ -767,7 +840,7 @@
         functools.partial(finish_factors_kernel, p),
         [shape(2, blk, blk)] * 2
         + ([shape(2, pairs, p.kloc)] * 2 if p.direct else [shape(2, p.yrows, blk)]),
-        *gathered(summed_over_groups(sums), lambda a: a),
+        *gathered_at_once(summed_over_groups(sums)),
         name="finish_factors",
     )
     if p.direct:

time: 97.4 us -> 91.8 us (0.943)
  waiting for transfers between devices: 53.8 us -> 43.8 us
  starting transfers between devices: 26.2 us -> 31 us
    ppermute x3 -> x1, waiting for transfers between devices: 21.5 us -> 0.01 us  [gathered(): pieces.append(lax.ppermute(rows(array), 'dp', p.across_fold(step)))]
    ppermute x1 -> x9, waiting for transfers between devices: 12.5 us -> 27.2 us  [the longest x3 12.2 us: shards(): lax.ppermute(share, ('dp', 'seq'), p.across_plane(*steps))]
    ppermute x1 -> x9, starting transfers between devices: 1.93 us -> 9.37 us  [the longest x3 3.62 us: shards(): lax.ppermute(piece, ('dp', 'seq'), p.across_plane(step, near_step))]
    ppermute x3 -> x1, starting transfers between devices: 3.12 us -> 0.48 us  [gathered(): pieces.append(lax.ppermute(rows(array), 'dp', p.across_fold(step)))]
    all_to_all x2, waiting for transfers between devices: 12 us -> 10.6 us  [across_layers(): lax.all_to_all(array, 'seq', 0, 0, tiled=True, axis_index_groups=p.layer_...]
    all_to_all x2, starting transfers between devices: 12.6 us -> 11.3 us  [across_layers(): lax.all_to_all(array, 'seq', 0, 0, tiled=True, axis_index_groups=p.layer_...]
    pallas_call x13 -> x14, Pallas kernels: 15.1 us -> 15.5 us  [call(): pl.pallas_call(kernel, out_shape=out_shape, in_specs=[FAR if i in far els...]
  transfers between devices with their start and end apart: 15 -> 21, of which waited for: 12 -> 15; matrix products, arithmetic and copies ran while one was open for 0% -> 0% of each run, Pallas kernels for 4% -> 5%
where the time goes in v5:
time: 91.8 us; the launch traced here: 91.3 us
  waiting for transfers between devices  43.8 us (48%)
  starting transfers between devices  31 us (34%)
  Pallas kernels  15.5 us (17%)
    pallas_call x14, Pallas kernels, call(): pl.pallas_call(kernel, out_shape=out_shape, in_specs=[FAR if i in far els...  15.5 us
    ppermute x3, waiting for transfers between devices, shards(): lax.ppermute(share, ('dp', 'seq'), p.across_plane(*steps))  12.2 us
    ppermute x3, waiting for transfers between devices, shards(): lax.ppermute(piece, ('dp', 'seq'), p.across_plane(step, near_step))  12 us
    all_to_all x2, starting transfers between devices, across_layers(): lax.all_to_all(array, 'seq', 0, 0, tiled=True, axis_index_groups=p.layer_...  11.3 us
    all_to_all x2, waiting for transfers between devices, across_layers(): lax.all_to_all(array, 'seq', 0, 0, tiled=True, axis_index_groups=p.layer_...  10.6 us
    all_to_all x2, starting transfers between devices, shuffle(): lax.all_to_all(array, ('dp', 'seq'), 0, 0, tiled=True, axis_index_groups=...  9.26 us
    ppermute x3, starting transfers between devices, shards(): lax.ppermute(piece, ('dp', 'seq'), p.across_plane(step, near_step))  3.62 us
    ppermute x3, starting transfers between devices, shards(): lax.ppermute(share, ('dp', 'seq'), p.across_plane(*steps))  3.55 us
  transfers between devices with their start and end apart: 21, of which 15 were waited for; matrix products, arithmetic and copies ran while one was open for 0% of the time, Pallas kernels for 5%

profile of v5, /device:TPU:0, one launch (start us, length us, event | category | flops | bytes accessed | tf_op | source)
XLA Modules:
  0.0 91.3 jit_solution(7172787649861367331)
XLA Ops:
  0.6 0.0 copy-start.1
  0.6 1.9 %factor_message.1 = bf16[4,240,128]{2,1,0:T(8,128)(2,1)} custom-call(bf16[128,1536]{1,0:T(8,128)(2,1)} %bitcast.32, bf16[2,128,128]{2,1,0:T(8,128)(2,1)} %bitcast.33, bf16[2,128,128]{2,1,0:T(8,128)(2,1)} %bitcast.34, bf16[2,64,16]{2,1,0:T(8,128)(2,1)} %bitcast.35, bf16[2,64,16]{2,1,0:T(8,128)(2,1)} %bitcast.36), custom_call_target="tpu_custom_call" | custom-call | tf_op jit(solution)/shard_map/factor_message/pallas_call | solution.py:110
  2.5 0.0 copy-start
  2.5 6.5 %all-to-all-start = ((bf16[4,240,128]{2,1,0:T(8,128)(2,1)}), bf16[4,240,128]{2,1,0:T(8,128)(2,1)S(1)}, u32[]{:S(2)}, u32[]{:S(2)}) async-start(bf16[4,240,128]{2,1,0:T(8,128)(2,1)} %factor_message.1), calls=%async_computation | async-start | bytes 491520 | tf_op jit(solution)/shard_map/all_to_all | solution.py:639
  9.0 0.0 copy-done.1
  9.0 0.0 copy-done
  9.0 1.1 %token_message.1 = bf16[16,192,128]{2,1,0:T(8,128)(2,1)} custom-call(bf16[128,1536]{1,0:T(8,128)(2,1)S(1)} %bitcast.28, bf16[128,1536]{1,0:T(8,128)(2,1)S(1)} %bitcast.29), custom_call_target="tpu_custom_call" | custom-call | tf_op jit(solution)/shard_map/token_message/pallas_call | solution.py:110
  10.2 7.4 %all-to-all-done.got = bf16[4,240,128]{2,1,0:T(8,128)(2,1)S(1)} async-done(((bf16[4,240,128]{2,1,0:T(8,128)(2,1)}), bf16[4,240,128]{2,1,0:T(8,128)(2,1)S(1)}, u32[]{:S(2)}, u32[]{:S(2)}) %all-to-all-start) | async-done | bytes 245792 | tf_op jit(solution)/shard_map/all_to_all | solution.py:639
  17.6 4.7 %all-to-all-start.1 = ((bf16[16,192,128]{2,1,0:T(8,128)(2,1)}), bf16[16,192,128]{2,1,0:T(8,128)(2,1)S(1)}, u32[]{:S(2)}, u32[]{:S(2)}) async-start(bf16[16,192,128]{2,1,0:T(8,128)(2,1)} %token_message.1), calls=%async_computation.1 | async-start | bytes 1572864 | tf_op jit(solution)/shard_map/all_to_all | solution.py:634
  22.3 0.1 near_message.1
  22.3 2.0 %collective-permute-start = (bf16[4,192,128]{2,1,0:T(8,128)(2,1)S(1)}, bf16[4,192,128]{2,1,0:T(8,128)(2,1)S(1)}, u32[]{:S(2)}, u32[]{:S(2)}) collective-permute-start(bf16[4,192,128]{2,1,0:T(8,128)(2,1)S(1)} %get-tuple-element.48), channel_id=1, source_target_pairs={{0,1},{1,0},{2,3},{3,2},{4,5},{5,4},{6,7},{7,6},{8,9},{9,8},{10,11... | collective-permute-start | bytes 589832 | tf_op jit(solution)/shard_map/ppermute | solution.py:697
  24.3 1.5 %collective-permute-start.2 = (bf16[4,144,128]{2,1,0:T(8,128)(2,1)S(1)}, bf16[4,144,128]{2,1,0:T(8,128)(2,1)S(1)}, u32[]{:S(2)}, u32[]{:S(2)}) collective-permute-start(bf16[4,144,128]{2,1,0:T(8,128)(2,1)S(1)} %slice.5), channel_id=1, source_target_pairs={{0,17},{1,16},{2,19},{3,18},{4,21},{5,20},{6,23},{7,22},{8,25},{9,... | collective-permute-start | bytes 442376 | tf_op jit(solution)/shard_map/ppermute | solution.py:697
  25.9 0.1 collective-permute-start.1
  26.0 0.0 copy-start.3
  26.0 0.0 copy-start.2
  26.0 0.0 collective-permute-start.3
  26.0 10.1 %collective-permute-done.2.refs_3_ = bf16[4,144,128]{2,1,0:T(8,128)(2,1)S(1)} collective-permute-done((bf16[4,144,128]{2,1,0:T(8,128)(2,1)S(1)}, bf16[4,144,128]{2,1,0:T(8,128)(2,1)S(1)}, u32[]{:S(2)}, u32[]{:S(2)}) %collective-permute-start.2) | collective-permute-done | bytes 147488 | tf_op jit(solution)/shard_map/ppermute | solution.py:697
  36.0 0.0 collective-permute-start.6
  36.0 1.4 %collective-permute-done.1.refs_2_ = bf16[4,144,128]{2,1,0:T(8,128)(2,1)S(1)} collective-permute-done((bf16[4,144,128]{2,1,0:T(8,128)(2,1)S(1)}, bf16[4,144,128]{2,1,0:T(8,128)(2,1)S(1)}, u32[]{:S(2)}, u32[]{:S(2)}) %collective-permute-start.1) | collective-permute-done | bytes 147488 | tf_op jit(solution)/shard_map/ppermute | solution.py:697
  37.5 0.0 collective-permute-start.5
  37.5 0.5 collective-permute-done.refs_1_
  38.0 0.0 collective-permute-start.4
  38.0 0.0 copy-done.3
  38.0 0.0 copy-done.2
  38.0 0.1 fusion
  38.1 0.1 pad_maximum_fusion.taps
  38.2 0.0 collective-permute-done.3.refs_4_
  38.2 0.0 collective-permute-done.6.refs_7_
  38.2 0.7 collective-permute-done.5.refs_6_
  38.9 0.6 collective-permute-done.4.refs_5_
  39.5 2.6 %all-to-all-done.1.tokens_in = bf16[16,192,128]{2,1,0:T(8,128)(2,1)S(1)} async-done(((bf16[16,192,128]{2,1,0:T(8,128)(2,1)}), bf16[16,192,128]{2,1,0:T(8,128)(2,1)S(1)}, u32[]{:S(2)}, u32[]{:S(2)}) %all-to-all-start.1) | async-done | bytes 786464 | tf_op jit(solution)/shard_map/all_to_all | solution.py:634
  42.1 1.2 %prepare.1 = (bf16[8,256,128]{2,1,0:T(8,128)(2,1)S(1)}, bf16[8,128,256]{2,1,0:T(8,128)(2,1)S(1)}, bf16[2,8,16,128]{3,2,1,0:T(8,128)(2,1)S(1)}, f32[8,128,192]{2,1,0:T(8,128)S(1)}) custom-call(bf16[4,192,128]{2,1,0:T(8,128)(2,1)S(1)} %get-tuple-element.50.refs_0_, bf16[4,192,128]{2,1,0:T(8,128)(2,1)S(1)} %collective-permute-done.refs_1_, ...), custom_call_target="tpu_custom_call" | custom-call | tf_op jit(solution)/shard_map/prepare/pallas_call | solution.py:110
  43.2 0.5 block_factors.1
  43.7 6.2 %mixer.1 = (bf16[8,128,192]{2,1,0:T(8,128)(2,1)S(1)}, bf16[2,8,176,128]{3,2,1,0:T(8,128)(2,1)S(1)}, bf16[2,8,176,128]{3,2,1,0:T(8,128)(2,1)S(1)}) custom-call(bf16[16,192,128]{2,1,0:T(8,128)(2,1)S(1)} %all-to-all-done.1.tokens_in, f32[6,192]{1,0:T(8,128)S(1)} %pad_maximum_fusion.taps, bf16[8,256,128]{2,1,0:T(8,128)(2,1)S(1)} %get-tuple-element.58.one, ...), custom_call_target="tpu_custom_call" | custom-call | tf_op jit(solution)/shard_map/mixer/pallas_call | solution.py:110
  49.9 0.1 collective-permute-start.7
  50.0 0.2 token_grad_message.1.grad_x
  50.2 2.0 %collective-permute-done.7.got = bf16[2,8,176,128]{3,2,1,0:T(8,128)(2,1)S(1)} collective-permute-done((bf16[2,8,176,128]{3,2,1,0:T(8,128)(2,1)S(1)}, bf16[2,8,176,128]{3,2,1,0:T(8,128)(2,1)S(1)}, u32[]{:S(2)}, u32[]{:S(2)}) %collective-permute-start.7) | collective-permute-done | bytes 720928 | tf_op jit(solution)/shard_map/ppermute | solution.py:644
  52.1 0.8 add_cores.1
  53.0 4.6 %all-to-all-start.2 = ((bf16[16,128,128]{2,1,0:T(8,128)(2,1)}), bf16[16,128,128]{2,1,0:T(8,128)(2,1)S(1)}, u32[]{:S(2)}, u32[]{:S(2)}) async-start(bf16[16,128,128]{2,1,0:T(8,128)(2,1)} %get-tuple-element.71), calls=%async_computation.2 | async-start | bytes 1048576 | tf_op jit(solution)/shard_map/all_to_all | solution.py:634
  57.6 1.9 %collective-permute-start.8 = (bf16[4,144,128]{2,1,0:T(8,128)(2,1)S(1)}, bf16[4,144,128]{2,1,0:T(8,128)(2,1)S(1)}, u32[]{:S(2)}, u32[]{:S(2)}) collective-permute-start(bf16[4,144,128]{2,1,0:T(8,128)(2,1)S(1)} %get-tuple-element.68), channel_id=1, source_target_pairs={{0,1},{1,0},{2,3},{3,2},{4,5},{5,4},{6,7},{7,6},{8,9},{9,8},{10,11... | collective-permute-start | bytes 442376 | tf_op jit(solution)/shard_map/ppermute | solution.py:805
  59.5 1.5 %collective-permute-start.9 = (bf16[4,144,128]{2,1,0:T(8,128)(2,1)S(1)}, bf16[4,144,128]{2,1,0:T(8,128)(2,1)S(1)}, u32[]{:S(2)}, u32[]{:S(2)}) collective-permute-start(bf16[4,144,128]{2,1,0:T(8,128)(2,1)S(1)} %get-tuple-element.69), channel_id=1, source_target_pairs={{0,16},{1,17},{2,18},{3,19},{4,20},{5,21},{6,22},{7,23},{8,24},{9,... | collective-permute-start | bytes 442376 | tf_op jit(solution)/shard_map/ppermute | solution.py:805
  61.0 0.2 collective-permute-start.10
  61.1 5.0 %collective-permute-done.8.refs_1_ = bf16[4,144,128]{2,1,0:T(8,128)(2,1)S(1)} collective-permute-done((bf16[4,144,128]{2,1,0:T(8,128)(2,1)S(1)}, bf16[4,144,128]{2,1,0:T(8,128)(2,1)S(1)}, u32[]{:S(2)}, u32[]{:S(2)}) %collective-permute-start.8) | collective-permute-done | bytes 147488 | tf_op jit(solution)/shard_map/ppermute | solution.py:805
  66.2 2.6 %collective-permute-done.9.refs_2_ = bf16[4,144,128]{2,1,0:T(8,128)(2,1)S(1)} collective-permute-done((bf16[4,144,128]{2,1,0:T(8,128)(2,1)S(1)}, bf16[4,144,128]{2,1,0:T(8,128)(2,1)S(1)}, u32[]{:S(2)}, u32[]{:S(2)}) %collective-permute-start.9) | collective-permute-done | bytes 147488 | tf_op jit(solution)/shard_map/ppermute | solution.py:805
  68.8 4.6 %collective-permute-done.10.refs_3_ = bf16[4,144,128]{2,1,0:T(8,128)(2,1)S(1)} collective-permute-done((bf16[4,144,128]{2,1,0:T(8,128)(2,1)S(1)}, bf16[4,144,128]{2,1,0:T(8,128)(2,1)S(1)}, u32[]{:S(2)}, u32[]{:S(2)}) %collective-permute-start.10) | collective-permute-done | bytes 147488 | tf_op jit(solution)/shard_map/ppermute | solution.py:805
  73.3 0.7 add_fold.1
  74.1 0.0 all-to-all-done.2.got
  74.1 0.5 collective-permute-start.11
  74.6 4.8 %all-to-all-start.3 = ((bf16[4,144,128]{2,1,0:T(8,128)(2,1)}), bf16[4,144,128]{2,1,0:T(8,128)(2,1)S(1)}, u32[]{:S(2)}, u32[]{:S(2)}) async-start(bf16[4,144,128]{2,1,0:T(8,128)(2,1)} %add_fold.1), calls=%async_computation.3 | async-start | bytes 294912 | tf_op jit(solution)/shard_map/all_to_all | solution.py:639
  79.4 0.0 collective-permute-start.12
  79.4 0.0 collective-permute-done.11.refs_1_
  79.4 0.5 collective-permute-start.13
  79.9 0.9 token_grad.1
  80.8 0.0 collective-permute-done.12.refs_2_
  80.8 0.1 collective-permute-done.13.refs_3_
  80.9 1.2 %finish_filter.1 = (bf16[128,1536]{1,0:T(8,128)(2,1)}, f32[3,1536]{1,0:T(4,128)}, f32[3,1536]{1,0:T(4,128)}) custom-call(bf16[16,32,128]{2,1,0:T(8,128)(2,1)S(1)} %filter_rows.1.refs_0_, bf16[16,32,128]{2,1,0:T(8,128)(2,1)S(1)} %collective-permute-done.11.refs_1_, bf16[16,32,128]{2,1,0:T(8,128)(2,1)S(1)} %collective-permute-done.12.refs_2_, ...), custom_call_target="tpu_custom_call" | custom-call | tf_op jit(solution)/shard_map/finish_filter/pallas_call | solution.py:110
  82.1 3.2 %all-to-all-done.3.got = bf16[4,144,128]{2,1,0:T(8,128)(2,1)S(1)} async-done(((bf16[4,144,128]{2,1,0:T(8,128)(2,1)}), bf16[4,144,128]{2,1,0:T(8,128)(2,1)S(1)}, u32[]{:S(2)}, u32[]{:S(2)}) %all-to-all-start.3) | async-done | bytes 147488 | tf_op jit(solution)/shard_map/all_to_all | solution.py:639
  85.4 0.1 collective-permute-start.16
  85.4 1.1 %collective-permute-start.15 = (bf16[144,128]{1,0:T(8,128)(2,1)S(1)}, bf16[144,128]{1,0:T(8,128)(2,1)S(1)}, u32[]{:S(2)}, u32[]{:S(2)}) collective-permute-start(bf16[144,128]{1,0:T(8,128)(2,1)S(1)} %sum_sources.1.refs_0_), channel_id=1, source_target_pairs={{0,8},{8,0},{16,24},{24,16},{1,9},{9,1},{17,25},{25,17},{2,10},{10... | collective-permute-start | bytes 110600 | tf_op jit(solution)/shard_map/ppermute | solution.py:654
  86.6 1.0 %collective-permute-start.14 = (bf16[144,128]{1,0:T(8,128)(2,1)S(1)}, bf16[144,128]{1,0:T(8,128)(2,1)S(1)}, u32[]{:S(2)}, u32[]{:S(2)}) collective-permute-start(bf16[144,128]{1,0:T(8,128)(2,1)S(1)} %sum_sources.1.refs_0_), channel_id=1, source_target_pairs={{0,16},{8,24},{16,0},{24,8},{1,17},{9,25},{17,1},{25,9},{2,18},{10... | collective-permute-start | bytes 110600 | tf_op jit(solution)/shard_map/ppermute | solution.py:654
  87.6 1.2 %collective-permute-done.16.refs_3_ = bf16[144,128]{1,0:T(8,128)(2,1)S(1)} collective-permute-done((bf16[144,128]{1,0:T(8,128)(2,1)S(1)}, bf16[144,128]{1,0:T(8,128)(2,1)S(1)}, u32[]{:S(2)}, u32[]{:S(2)}) %collective-permute-start.16) | collective-permute-done | bytes 36896 | tf_op jit(solution)/shard_map/ppermute | solution.py:654
  88.8 0.0 collective-permute-done.15.refs_2_
  88.8 1.7 %collective-permute-done.14.refs_1_ = bf16[144,128]{1,0:T(8,128)(2,1)S(1)} collective-permute-done((bf16[144,128]{1,0:T(8,128)(2,1)S(1)}, bf16[144,128]{1,0:T(8,128)(2,1)S(1)}, u32[]{:S(2)}, u32[]{:S(2)}) %collective-permute-start.14) | collective-permute-done | bytes 36896 | tf_op jit(solution)/shard_map/ppermute | solution.py:654
  90.5 0.7 finish_factors.1
  (3 shorter events, 0.0 us)
Async XLA Ops:
  0.6 8.4 %copy-start.1 = (bf16[1,128,1536]{2,1,0:T(8,128)(2,1)S(1)}, bf16[1,128,1536]{2,1,0:T(8,128)(2,1)}, u32[]{:S(2)}) copy-start(bf16[1,128,1536]{2,1,0:T(8,128)(2,1)} %param.10) | copy-start | bytes 1179652
  2.5 6.5 %copy-start = (bf16[1,128,1536]{2,1,0:T(8,128)(2,1)S(1)}, bf16[1,128,1536]{2,1,0:T(8,128)(2,1)}, u32[]{:S(2)}) copy-start(bf16[1,128,1536]{2,1,0:T(8,128)(2,1)} %param.9) | copy-start | bytes 1179652
  2.5 15.0 %all-to-all-start = ((bf16[4,240,128]{2,1,0:T(8,128)(2,1)}), bf16[4,240,128]{2,1,0:T(8,128)(2,1)S(1)}, u32[]{:S(2)}, u32[]{:S(2)}) async-start(bf16[4,240,128]{2,1,0:T(8,128)(2,1)} %factor_message.1), calls=%async_computation | async-start | bytes 491520 | tf_op jit(solution)/shard_map/all_to_all | solution.py:639
  17.6 24.5 %all-to-all-start.1 = ((bf16[16,192,128]{2,1,0:T(8,128)(2,1)}), bf16[16,192,128]{2,1,0:T(8,128)(2,1)S(1)}, u32[]{:S(2)}, u32[]{:S(2)}) async-start(bf16[16,192,128]{2,1,0:T(8,128)(2,1)} %token_message.1), calls=%async_computation.1 | async-start | bytes 1572864 | tf_op jit(solution)/shard_map/all_to_all | solution.py:634
  22.3 15.7 %collective-permute-start = (bf16[4,192,128]{2,1,0:T(8,128)(2,1)S(1)}, bf16[4,192,128]{2,1,0:T(8,128)(2,1)S(1)}, u32[]{:S(2)}, u32[]{:S(2)}) collective-permute-start(bf16[4,192,128]{2,1,0:T(8,128)(2,1)S(1)} %get-tuple-element.48), channel_id=1, source_target_pairs={{0,1},{1,0},{2,3},{3,2},{4,5},{5,4},{6,7},{7,6},{8,9},{9,8},{10,11... | collective-permute-start | bytes 589832 | tf_op jit(solution)/shard_map/ppermute | solution.py:697
  24.3 11.7 %collective-permute-start.2 = (bf16[4,144,128]{2,1,0:T(8,128)(2,1)S(1)}, bf16[4,144,128]{2,1,0:T(8,128)(2,1)S(1)}, u32[]{:S(2)}, u32[]{:S(2)}) collective-permute-start(bf16[4,144,128]{2,1,0:T(8,128)(2,1)S(1)} %slice.5), channel_id=1, source_target_pairs={{0,17},{1,16},{2,19},{3,18},{4,21},{5,20},{6,23},{7,22},{8,25},{9,... | collective-permute-start | bytes 442376 | tf_op jit(solution)/shard_map/ppermute | solution.py:697
  25.9 11.6 %collective-permute-start.1 = (bf16[4,144,128]{2,1,0:T(8,128)(2,1)S(1)}, bf16[4,144,128]{2,1,0:T(8,128)(2,1)S(1)}, u32[]{:S(2)}, u32[]{:S(2)}) collective-permute-start(bf16[4,144,128]{2,1,0:T(8,128)(2,1)S(1)} %slice.5), channel_id=1, source_target_pairs={{0,16},{1,17},{2,18},{3,19},{4,20},{5,21},{6,22},{7,23},{8,24},{9,... | collective-permute-start | bytes 442376 | tf_op jit(solution)/shard_map/ppermute | solution.py:697
  26.0 12.1 %copy-start.3 = (f32[3,1536]{1,0:T(4,128)S(1)}, f32[3,1536]{1,0:T(4,128)}, u32[]{:S(2)}) copy-start(f32[3,1536]{1,0:T(4,128)} %param.12) | copy-start | bytes 55300
  26.0 12.1 %copy-start.2 = (f32[3,1536]{1,0:T(4,128)S(1)}, f32[3,1536]{1,0:T(4,128)}, u32[]{:S(2)}) copy-start(f32[3,1536]{1,0:T(4,128)} %param.11) | copy-start | bytes 55300
  26.0 12.2 %collective-permute-start.3 = (bf16[4,192,128]{2,1,0:T(8,128)(2,1)S(1)}, bf16[4,192,128]{2,1,0:T(8,128)(2,1)S(1)}, u32[]{:S(2)}, u32[]{:S(2)}) collective-permute-start(bf16[4,192,128]{2,1,0:T(8,128)(2,1)S(1)} %get-tuple-element.50.refs_0_), channel_id=1, source_target_pairs={{0,8},{8,0},{16,24},{24,16},{1,9},{9,1},{17,25},{25,17},{2,10},{10... | collective-permute-start | bytes 589832 | tf_op jit(solution)/shard_map/ppermute | solution.py:644
  36.0 2.2 %collective-permute-start.6 = (bf16[4,144,128]{2,1,0:T(8,128)(2,1)S(1)}, bf16[4,144,128]{2,1,0:T(8,128)(2,1)S(1)}, u32[]{:S(2)}, u32[]{:S(2)}) collective-permute-start(bf16[4,144,128]{2,1,0:T(8,128)(2,1)S(1)} %collective-permute-done.2.refs_3_), channel_id=1, source_target_pairs={{0,8},{8,0},{16,24},{24,16},{1,9},{9,1},{17,25},{25,17},{2,10},{10... | collective-permute-start | bytes 442376 | tf_op jit(solution)/shard_map/ppermute | solution.py:644
  37.5 1.4 %collective-permute-start.5 = (bf16[4,144,128]{2,1,0:T(8,128)(2,1)S(1)}, bf16[4,144,128]{2,1,0:T(8,128)(2,1)S(1)}, u32[]{:S(2)}, u32[]{:S(2)}) collective-permute-start(bf16[4,144,128]{2,1,0:T(8,128)(2,1)S(1)} %collective-permute-done.1.refs_2_), channel_id=1, source_target_pairs={{0,8},{8,0},{16,24},{24,16},{1,9},{9,1},{17,25},{25,17},{2,10},{10... | collective-permute-start | bytes 442376 | tf_op jit(solution)/shard_map/ppermute | solution.py:644
  38.0 1.4 %collective-permute-start.4 = (bf16[4,192,128]{2,1,0:T(8,128)(2,1)S(1)}, bf16[4,192,128]{2,1,0:T(8,128)(2,1)S(1)}, u32[]{:S(2)}, u32[]{:S(2)}) collective-permute-start(bf16[4,192,128]{2,1,0:T(8,128)(2,1)S(1)} %collective-permute-done.refs_1_), channel_id=1, source_target_pairs={{0,8},{8,0},{16,24},{24,16},{1,9},{9,1},{17,25},{25,17},{2,10},{10... | collective-permute-start | bytes 589832 | tf_op jit(solution)/shard_map/ppermute | solution.py:644
  49.9 2.3 %collective-permute-start.7 = (bf16[2,8,176,128]{3,2,1,0:T(8,128)(2,1)S(1)}, bf16[2,8,176,128]{3,2,1,0:T(8,128)(2,1)S(1)}, u32[]{:S(2)}, u32[]{:S(2)}) collective-permute-start(bf16[2,8,176,128]{3,2,1,0:T(8,128)(2,1)S(1)} %get-tuple-element.66), channel_id=1, source_target_pairs={{0,8},{8,0},{16,24},{24,16},{1,9},{9,1},{17,25},{25,17},{2,10},{10... | collective-permute-start | bytes 2162696 | tf_op jit(solution)/shard_map/ppermute | solution.py:644
  53.0 21.1 %all-to-all-start.2 = ((bf16[16,128,128]{2,1,0:T(8,128)(2,1)}), bf16[16,128,128]{2,1,0:T(8,128)(2,1)S(1)}, u32[]{:S(2)}, u32[]{:S(2)}) async-start(bf16[16,128,128]{2,1,0:T(8,128)(2,1)} %get-tuple-element.71), calls=%async_computation.2 | async-start | bytes 1048576 | tf_op jit(solution)/shard_map/all_to_all | solution.py:634
  57.6 8.6 %collective-permute-start.8 = (bf16[4,144,128]{2,1,0:T(8,128)(2,1)S(1)}, bf16[4,144,128]{2,1,0:T(8,128)(2,1)S(1)}, u32[]{:S(2)}, u32[]{:S(2)}) collective-permute-start(bf16[4,144,128]{2,1,0:T(8,128)(2,1)S(1)} %get-tuple-element.68), channel_id=1, source_target_pairs={{0,1},{1,0},{2,3},{3,2},{4,5},{5,4},{6,7},{7,6},{8,9},{9,8},{10,11... | collective-permute-start | bytes 442376 | tf_op jit(solution)/shard_map/ppermute | solution.py:805
  59.5 9.2 %collective-permute-start.9 = (bf16[4,144,128]{2,1,0:T(8,128)(2,1)S(1)}, bf16[4,144,128]{2,1,0:T(8,128)(2,1)S(1)}, u32[]{:S(2)}, u32[]{:S(2)}) collective-permute-start(bf16[4,144,128]{2,1,0:T(8,128)(2,1)S(1)} %get-tuple-element.69), channel_id=1, source_target_pairs={{0,16},{1,17},{2,18},{3,19},{4,20},{5,21},{6,22},{7,23},{8,24},{9,... | collective-permute-start | bytes 442376 | tf_op jit(solution)/shard_map/ppermute | solution.py:805
  61.0 12.3 %collective-permute-start.10 = (bf16[4,144,128]{2,1,0:T(8,128)(2,1)S(1)}, bf16[4,144,128]{2,1,0:T(8,128)(2,1)S(1)}, u32[]{:S(2)}, u32[]{:S(2)}) collective-permute-start(bf16[4,144,128]{2,1,0:T(8,128)(2,1)S(1)} %get-tuple-element.70), channel_id=1, source_target_pairs={{0,17},{1,16},{2,19},{3,18},{4,21},{5,20},{6,23},{7,22},{8,25},{9,... | collective-permute-start | bytes 442376 | tf_op jit(solution)/shard_map/ppermute | solution.py:805
  74.1 5.3 %collective-permute-start.11 = (bf16[16,32,128]{2,1,0:T(8,128)(2,1)S(1)}, bf16[16,32,128]{2,1,0:T(8,128)(2,1)S(1)}, u32[]{:S(2)}, u32[]{:S(2)}) collective-permute-start(bf16[16,32,128]{2,1,0:T(8,128)(2,1)S(1)} %filter_rows.1.refs_0_), channel_id=1, source_target_pairs={{0,16},{8,24},{16,0},{24,8},{1,17},{9,25},{17,1},{25,9},{2,18},{10... | collective-permute-start | bytes 393224 | tf_op jit(solution)/shard_map/ppermute | solution.py:649
  74.6 10.8 %all-to-all-start.3 = ((bf16[4,144,128]{2,1,0:T(8,128)(2,1)}), bf16[4,144,128]{2,1,0:T(8,128)(2,1)S(1)}, u32[]{:S(2)}, u32[]{:S(2)}) async-start(bf16[4,144,128]{2,1,0:T(8,128)(2,1)} %add_fold.1), calls=%async_computation.3 | async-start | bytes 294912 | tf_op jit(solution)/shard_map/all_to_all | solution.py:639
  79.4 1.4 %collective-permute-start.12 = (bf16[16,32,128]{2,1,0:T(8,128)(2,1)S(1)}, bf16[16,32,128]{2,1,0:T(8,128)(2,1)S(1)}, u32[]{:S(2)}, u32[]{:S(2)}) collective-permute-start(bf16[16,32,128]{2,1,0:T(8,128)(2,1)S(1)} %filter_rows.1.refs_0_), channel_id=1, source_target_pairs={{0,8},{8,0},{16,24},{24,16},{1,9},{9,1},{17,25},{25,17},{2,10},{10... | collective-permute-start | bytes 393224 | tf_op jit(solution)/shard_map/ppermute | solution.py:644
  79.4 1.5 %collective-permute-start.13 = (bf16[16,32,128]{2,1,0:T(8,128)(2,1)S(1)}, bf16[16,32,128]{2,1,0:T(8,128)(2,1)S(1)}, u32[]{:S(2)}, u32[]{:S(2)}) collective-permute-start(bf16[16,32,128]{2,1,0:T(8,128)(2,1)S(1)} %collective-permute-done.11.refs_1_), channel_id=1, source_target_pairs={{0,8},{8,0},{16,24},{24,16},{1,9},{9,1},{17,25},{25,17},{2,10},{10... | collective-permute-start | bytes 393224 | tf_op jit(solution)/shard_map/ppermute | solution.py:644
  85.4 3.4 %collective-permute-start.16 = (bf16[144,128]{1,0:T(8,128)(2,1)S(1)}, bf16[144,128]{1,0:T(8,128)(2,1)S(1)}, u32[]{:S(2)}, u32[]{:S(2)}) collective-permute-start(bf16[144,128]{1,0:T(8,128)(2,1)S(1)} %sum_sources.1.refs_0_), channel_id=1, source_target_pairs={{0,24},{8,16},{16,8},{24,0},{1,25},{9,17},{17,9},{25,1},{2,26},{10... | collective-permute-start | bytes 110600 | tf_op jit(solution)/shard_map/ppermute | solution.py:654
  85.4 3.4 %collective-permute-start.15 = (bf16[144,128]{1,0:T(8,128)(2,1)S(1)}, bf16[144,128]{1,0:T(8,128)(2,1)S(1)}, u32[]{:S(2)}, u32[]{:S(2)}) collective-permute-start(bf16[144,128]{1,0:T(8,128)(2,1)S(1)} %sum_sources.1.refs_0_), channel_id=1, source_target_pairs={{0,8},{8,0},{16,24},{24,16},{1,9},{9,1},{17,25},{25,17},{2,10},{10... | collective-permute-start | bytes 110600 | tf_op jit(solution)/shard_map/ppermute | solution.py:654
  86.6 4.0 %collective-permute-start.14 = (bf16[144,128]{1,0:T(8,128)(2,1)S(1)}, bf16[144,128]{1,0:T(8,128)(2,1)S(1)}, u32[]{:S(2)}, u32[]{:S(2)}) collective-permute-start(bf16[144,128]{1,0:T(8,128)(2,1)S(1)} %sum_sources.1.refs_0_), channel_id=1, source_target_pairs={{0,16},{8,24},{16,0},{24,8},{1,17},{9,25},{17,1},{25,9},{2,18},{10... | collective-permute-start | bytes 110600 | tf_op jit(solution)/shard_map/ppermute | solution.py:654

commit v6 on v5

--- a/solution.py
+++ b/solution.py
@@ -74,6 +74,11 @@
                     moves.append((source, target))
         return moves
 
+    def layer_partner(self, z, step):
+        if self.layers & (self.layers - 1) == 0:
+            return z ^ step
+        return (step + self.layers - z) % self.layers
+
     def across_plane(self, step, near_step, side=0):
         return [
             (source * self.seq + s, target * self.seq + s // self.near * self.near + (s + near_step) % self.near)
@@ -129,7 +134,8 @@
 
 def factor_message_kernel(p, *refs):
     count = 5 if p.direct else 4
-    far, out, near, rows, turned, done = refs[:count], refs[count], refs[count + 1 : -3], *refs[-3:]
+    far, outs, refs = refs[:count], refs[count : count + p.layers], refs[count + p.layers :]
+    near, rows, turned, done = refs[:-3], *refs[-3:]
     h, core = place(p)
     part_width = p.seq * p.width
     sources = [far[0].at[:, pl.ds(pl.multiple_of(h * part_width, p.blk), part_width)]]
@@ -156,27 +162,30 @@
     copies[0].wait()
     turned[...] = filt[...].T
 
-    def one_layer(z):
-        out[z, 0 : p.mrows] = mine
-        for near in range(p.near):
-            logs = turned[rows_at((z * p.near + near) * p.width, p.width)]
+    z = lax.axis_index("seq") // p.near
+    for near in range(p.near):
+        logs = []
+        for target in range(p.layers):
+            at = (target * p.near + near) * p.width
+            rows_here = turned[at : at + p.width]
             if p.cores_share:
-                logs = jnp.where(core == 0, logs[: p.frows], logs[p.frows :])
-            out[z, p.mrows + near * p.frows : p.mrows + (near + 1) * p.frows] = logs
-
-    each(p.layers, one_layer)
-
-
-def near_message_kernel(p, got, *outs):
+                rows_here = jnp.where(core == 0, rows_here[: p.frows], rows_here[p.frows :])
+            logs.append(rows_here)
+        for step in range(p.layers):
+            chosen = pick(p, [logs[p.layer_partner(at, step)] for at in range(p.layers)], z)
+            outs[step][p.mrows + near * p.frows : p.mrows + (near + 1) * p.frows] = chosen
+    for step in range(p.layers):
+        outs[step][0 : p.mrows] = mine
+
+
+def near_message_kernel(p, *refs):
+    got, outs = refs[: p.layers], refs[p.layers :]
     y = lax.axis_index("seq") % p.near
-
-    def one_layer(z):
-        logs = [got[z, p.mrows + i * p.frows : p.mrows + (i + 1) * p.frows] for i in range(p.near)]
+    for z in range(p.layers):
+        logs = [got[z][p.mrows + i * p.frows : p.mrows + (i + 1) * p.frows] for i in range(p.near)]
         for step in range(p.near):
-            outs[step][z, 0 : p.mrows] = got[z, 0 : p.mrows]
+            outs[step][z, 0 : p.mrows] = got[z][0 : p.mrows]
             outs[step][z, p.mrows :] = pick(p, [logs[(i + step) % p.near] for i in range(p.near)], y)
-
-    each(p.layers, one_layer)
 
 
 def token_message_kernel(p, tokens, upstream, out):
@@ -209,31 +218,35 @@
 def prepare_kernel(p, *refs):
     count = 2 * len(p.plane())
     pieces, (one, four, small, filt) = refs[:count], refs[count:]
-    _, core = place(p)
+    h, core = place(p)
     y = lax.axis_index("seq") % p.near
+
+    def from_near(z, near, side, step, rows):
+        first = (side * p.fold + step) * p.near
+        return pick(p, [pieces[first + (near - at) % p.near][z, rows] for at in range(p.near)], y)
+
+    def half_rows(z, near):
+        sides = []
+        for side in range(2):
+            steps = [from_near(z, near, side, step, slice(0, p.mrows)) for step in range(p.fold)]
+            shares = [
+                pick(p, [steps[(at - owner) % p.fold] for at in range(p.fold)], h)
+                for owner in range(p.fold)
+            ]
+            sides.append(jnp.concatenate(shares, axis=0) if p.fold > 1 else shares[0])
+        return [jnp.where(core == c, sides[0], sides[1]) for c in range(2)]
 
     def one_layer(z):
         for near in range(p.near):
-            i = z * p.near + near
-
-            def from_near(part):
-                return pick(p, [part(pieces[(near - at) % p.near :: p.near]) for at in range(p.near)], y)
-
-            for side in range(2):
-                rows = [
-                    from_near(
-                        lambda own: shares_in_order(p, own)(side, owner, lambda ref, *_: ref[z, 0 : p.mrows])
-                    )
-                    for owner in range(p.fold)
-                ]
-                rows = jnp.concatenate(rows, axis=0) if p.fold > 1 else rows[0]
+            i = p.layer_partner(lax.axis_index("seq") // p.near, z) * p.near + near
+            for side, rows in enumerate(half_rows(z, near)):
                 one[i, side * p.blk : (side + 1) * p.blk] = rows[0 : p.blk]
                 factor = rows[p.blk : 2 * p.blk]
                 four[i, :, side * p.blk : (side + 1) * p.blk] = factor if side == 0 else -factor
                 small[side, i] = rows[2 * p.blk : 2 * p.blk + p.yrows]
-            logs = from_near(lambda own: own[0][z, p.mrows :])
+            logs = from_near(z, near, 0, 0, slice(p.mrows, p.mrows + p.frows))
             if p.cores_share:
-                other = from_near(lambda own: own[p.fold][z, p.mrows :])
+                other = from_near(z, near, 1, 0, slice(p.mrows, p.mrows + p.frows))
                 logs = [jnp.where(core == 0, logs, other), jnp.where(core == 0, other, logs)]
                 logs = jnp.concatenate(logs, axis=0)
             if p.fold > 1:
@@ -669,7 +682,7 @@
     ]
     message = call(
         functools.partial(factor_message_kernel, p),
-        shape(p.layers, p.mrows + p.near * p.frows, blk),
+        [shape(p.mrows + p.near * p.frows, blk)] * p.layers,
         *far,
         scratch=[pltpu.VMEM((blk, p.channels // p.fold), BF16)]
         + [pltpu.VMEM(f.shape[1:], BF16) for f in far[1:]]
@@ -682,18 +695,21 @@
         limit=60,
         name="factor_message",
     )
-    factors = across_layers(message)
-    near_messages = [factors]
-    if p.near > 1:
-        near_messages = call(
-            functools.partial(near_message_kernel, p),
-            [shape(p.layers, p.mrows + p.frows, blk)] * p.near,
-            factors,
-            name="near_message",
-        )
+    factors = [message[0]]
+    for step in range(1, p.layers):
+        moves = [
+            (s, p.layer_partner(s // p.near, step) * p.near + s % p.near) for s in range(p.seq)
+        ]
+        factors.append(lax.ppermute(message[step], "seq", moves))
+    near_messages = call(
+        functools.partial(near_message_kernel, p),
+        [shape(p.layers, p.mrows + p.frows, blk)] * p.near,
+        *factors,
+        name="near_message",
+    )
     pieces = [near_messages[0]]
     for step, near_step in p.plane()[1:]:
-        piece = near_messages[near_step] if step == 0 else factors[:, : p.mrows]
+        piece = near_messages[near_step] if step == 0 else near_messages[0][:, : p.mrows]
         pieces.append(lax.ppermute(piece, ("dp", "seq"), p.across_plane(step, near_step)))
     pieces += [swap(piece) for piece in pieces]
 
@@ -704,6 +720,7 @@
         upstream[0],
         name="token_message",
     )
+    message, factors = lax.optimization_barrier((message, factors))
     received = shuffle(message)
     pieces, received = lax.optimization_barrier((pieces, received))
     one, four, small, filt = call(

time: 91.8 us -> 87.9 us (0.958)
  waiting for transfers between devices: 43.8 us -> 39.8 us
  local copies, waits for them, and re-layouts: 0.03 us -> 1.02 us
    all_to_all x2 -> x1, waiting for transfers between devices: 10.6 us -> 3.21 us  [across_layers(): lax.all_to_all(array, 'seq', 0, 0, tiled=True, axis_index_groups=p.layer_...]
    all_to_all x2 -> x1, starting transfers between devices: 11.3 us -> 4.81 us  [across_layers(): lax.all_to_all(array, 'seq', 0, 0, tiled=True, axis_index_groups=p.layer_...]
    ppermute x0 -> x3, starting transfers between devices: none -> 5.68 us  [shards(): factors.append(lax.ppermute(message[step], 'seq', moves))]
    ppermute x0 -> x3, waiting for transfers between devices: none -> 4.08 us  [shards(): factors.append(lax.ppermute(message[step], 'seq', moves))]
    unnamed x8 -> x10, local copies, waits for them, and re-layouts: 0.02 us -> 1.01 us
  transfers between devices with their start and end apart: 21 -> 23, of which waited for: 15 -> 16; matrix products, arithmetic and copies ran while one was open for 0% -> 0% of each run, Pallas kernels for 5% -> 5%
where the time goes in v6:
time: 87.9 us; the launch traced here: 87.4 us
  waiting for transfers between devices  39.8 us (45%)
  starting transfers between devices  30.3 us (34%)
  Pallas kernels  15.4 us (18%)
  local copies, waits for them, and re-layouts  1.02 us (1%)
    pallas_call x14, Pallas kernels, call(): pl.pallas_call(kernel, out_shape=out_shape, in_specs=[FAR if i in far els...  15.4 us
    ppermute x3, waiting for transfers between devices, shards(): lax.ppermute(share, ('dp', 'seq'), p.across_plane(*steps))  12.2 us
    ppermute x3, waiting for transfers between devices, shards(): lax.ppermute(piece, ('dp', 'seq'), p.across_plane(step, near_step))  11.3 us
    all_to_all x2, starting transfers between devices, shuffle(): lax.all_to_all(array, ('dp', 'seq'), 0, 0, tiled=True, axis_index_groups=...  9.36 us
    ppermute x3, starting transfers between devices, shards(): factors.append(lax.ppermute(message[step], 'seq', moves))  5.68 us
    all_to_all x1, starting transfers between devices, across_layers(): lax.all_to_all(array, 'seq', 0, 0, tiled=True, axis_index_groups=p.layer_...  4.81 us
    ppermute x3, waiting for transfers between devices, shards(): factors.append(lax.ppermute(message[step], 'seq', moves))  4.08 us
    ppermute x3, starting transfers between devices, shards(): lax.ppermute(piece, ('dp', 'seq'), p.across_plane(step, near_step))  3.62 us
  transfers between devices with their start and end apart: 23, of which 16 were waited for; matrix products, arithmetic and copies ran while one was open for 0% of the time, Pallas kernels for 5%

profile of v6, /device:TPU:0, one launch (start us, length us, event | category | flops | bytes accessed | tf_op | source)
XLA Modules:
  0.0 87.4 jit_solution(14490545731022768543)
XLA Ops:
  0.6 0.0 copy-start
  0.6 1.9 %factor_message.1 = (bf16[240,128]{1,0:T(8,128)(2,1)}, bf16[240,128]{1,0:T(8,128)(2,1)}, bf16[240,128]{1,0:T(8,128)(2,1)}, bf16[240,128]{1,0:T(8,128)(2,1)}) custom-call(bf16[128,1536]{1,0:T(8,128)(2,1)} %bitcast.32, bf16[2,128,128]{2,1,0:T(8,128)(2,1)} %bitcast.33, bf16[2,128,128]{2,1,0:T(8,128)(2,1)} %bitcast.34, bf16[2,64,16]{2,1,0:T(8,128)(2,1)} %bitcast.35, ...), custom_call_target="tpu_custom_call" | custom-call | tf_op jit(solution)/shard_map/factor_message/pallas_call | solution.py:115
  2.5 3.1 %collective-permute-start = (bf16[240,128]{1,0:T(8,128)(2,1)}, bf16[240,128]{1,0:T(8,128)(2,1)S(1)}, u32[]{:S(2)}, u32[]{:S(2)}) collective-permute-start(bf16[240,128]{1,0:T(8,128)(2,1)} %get-tuple-element.53), channel_id=1, source_target_pairs={{0,2},{1,3},{2,0},{3,1},{4,6},{5,7},{6,4},{7,5},{8,10},{9,11},{10,... | collective-permute-start | bytes 184328 | tf_op jit(solution)/shard_map/ppermute | solution.py:703
  5.6 2.6 %collective-permute-start.1 = (bf16[240,128]{1,0:T(8,128)(2,1)}, bf16[240,128]{1,0:T(8,128)(2,1)S(1)}, u32[]{:S(2)}, u32[]{:S(2)}) collective-permute-start(bf16[240,128]{1,0:T(8,128)(2,1)} %get-tuple-element.54), channel_id=1, source_target_pairs={{0,4},{1,5},{2,6},{3,7},{4,0},{5,1},{6,2},{7,3},{8,12},{9,13},{10,... | collective-permute-start | bytes 184328 | tf_op jit(solution)/shard_map/ppermute | solution.py:703
  8.2 0.0 collective-permute-start.2
  8.2 0.0 copy-done
  8.2 1.0 %copy-done.1 = bf16[1,128,1536]{2,1,0:T(8,128)(2,1)S(1)} copy-done((bf16[1,128,1536]{2,1,0:T(8,128)(2,1)S(1)}, bf16[1,128,1536]{2,1,0:T(8,128)(2,1)}, u32[]{:S(2)}) %copy-start.1) | copy-done | bytes 393240
  9.2 1.1 %token_message.1 = bf16[16,192,128]{2,1,0:T(8,128)(2,1)} custom-call(bf16[128,1536]{1,0:T(8,128)(2,1)S(1)} %bitcast.28, bf16[128,1536]{1,0:T(8,128)(2,1)S(1)} %bitcast.29), custom_call_target="tpu_custom_call" | custom-call | tf_op jit(solution)/shard_map/token_message/pallas_call | solution.py:115
  10.3 0.0 collective-permute-done.refs_1_
  10.3 1.8 %collective-permute-done.1.refs_2_ = bf16[240,128]{1,0:T(8,128)(2,1)S(1)} collective-permute-done((bf16[240,128]{1,0:T(8,128)(2,1)}, bf16[240,128]{1,0:T(8,128)(2,1)S(1)}, u32[]{:S(2)}, u32[]{:S(2)}) %collective-permute-start.1) | collective-permute-done | bytes 61472 | tf_op jit(solution)/shard_map/ppermute | solution.py:703
  12.2 2.3 %collective-permute-done.2.refs_3_ = bf16[240,128]{1,0:T(8,128)(2,1)S(1)} collective-permute-done((bf16[240,128]{1,0:T(8,128)(2,1)}, bf16[240,128]{1,0:T(8,128)(2,1)S(1)}, u32[]{:S(2)}, u32[]{:S(2)}) %collective-permute-start.2) | collective-permute-done | bytes 61472 | tf_op jit(solution)/shard_map/ppermute | solution.py:703
  14.4 4.9 %all-to-all-start = ((bf16[16,192,128]{2,1,0:T(8,128)(2,1)}), bf16[16,192,128]{2,1,0:T(8,128)(2,1)S(1)}, u32[]{:S(2)}, u32[]{:S(2)}) async-start(bf16[16,192,128]{2,1,0:T(8,128)(2,1)} %token_message.1), calls=%async_computation | async-start | bytes 1572864 | tf_op jit(solution)/shard_map/all_to_all | solution.py:647
  19.4 0.0 copy-done.2
  19.4 0.1 near_message.1
  19.4 2.0 %collective-permute-start.3 = (bf16[4,192,128]{2,1,0:T(8,128)(2,1)S(1)}, bf16[4,192,128]{2,1,0:T(8,128)(2,1)S(1)}, u32[]{:S(2)}, u32[]{:S(2)}) collective-permute-start(bf16[4,192,128]{2,1,0:T(8,128)(2,1)S(1)} %get-tuple-element.57), channel_id=1, source_target_pairs={{0,1},{1,0},{2,3},{3,2},{4,5},{5,4},{6,7},{7,6},{8,9},{9,8},{10,11... | collective-permute-start | bytes 589832 | tf_op jit(solution)/shard_map/ppermute | solution.py:713
  21.4 1.5 %collective-permute-start.5 = (bf16[4,144,128]{2,1,0:T(8,128)(2,1)S(1)}, bf16[4,144,128]{2,1,0:T(8,128)(2,1)S(1)}, u32[]{:S(2)}, u32[]{:S(2)}) collective-permute-start(bf16[4,144,128]{2,1,0:T(8,128)(2,1)S(1)} %slice.4), channel_id=1, source_target_pairs={{0,17},{1,16},{2,19},{3,18},{4,21},{5,20},{6,23},{7,22},{8,25},{9,... | collective-permute-start | bytes 442376 | tf_op jit(solution)/shard_map/ppermute | solution.py:713
  23.0 0.1 collective-permute-start.4
  23.1 0.0 collective-permute-start.6
  23.1 9.0 %collective-permute-done.5.refs_3_ = bf16[4,144,128]{2,1,0:T(8,128)(2,1)S(1)} collective-permute-done((bf16[4,144,128]{2,1,0:T(8,128)(2,1)S(1)}, bf16[4,144,128]{2,1,0:T(8,128)(2,1)S(1)}, u32[]{:S(2)}, u32[]{:S(2)}) %collective-permute-start.5) | collective-permute-done | bytes 147488 | tf_op jit(solution)/shard_map/ppermute | solution.py:713
  32.1 0.0 collective-permute-start.9
  32.1 1.8 %collective-permute-done.4.refs_2_ = bf16[4,144,128]{2,1,0:T(8,128)(2,1)S(1)} collective-permute-done((bf16[4,144,128]{2,1,0:T(8,128)(2,1)S(1)}, bf16[4,144,128]{2,1,0:T(8,128)(2,1)S(1)}, u32[]{:S(2)}, u32[]{:S(2)}) %collective-permute-start.4) | collective-permute-done | bytes 147488 | tf_op jit(solution)/shard_map/ppermute | solution.py:713
  33.9 0.0 collective-permute-start.8
  33.9 0.5 collective-permute-done.3.refs_1_
  34.4 0.0 collective-permute-start.7
  34.4 0.1 fusion
  34.5 0.1 pad_maximum_fusion.taps
  34.6 0.0 collective-permute-done.6.refs_4_
  34.6 0.0 collective-permute-done.9.refs_7_
  34.6 0.7 collective-permute-done.8.refs_6_
  35.2 0.6 collective-permute-done.7.refs_5_
  35.8 2.6 %all-to-all-done.tokens_in = bf16[16,192,128]{2,1,0:T(8,128)(2,1)S(1)} async-done(((bf16[16,192,128]{2,1,0:T(8,128)(2,1)}), bf16[16,192,128]{2,1,0:T(8,128)(2,1)S(1)}, u32[]{:S(2)}, u32[]{:S(2)}) %all-to-all-start) | async-done | bytes 786464 | tf_op jit(solution)/shard_map/all_to_all | solution.py:647
  38.5 0.7 prepare.1
  39.2 0.5 block_factors.1
  39.6 6.5 %mixer.1 = (bf16[8,128,192]{2,1,0:T(8,128)(2,1)S(1)}, bf16[2,8,176,128]{3,2,1,0:T(8,128)(2,1)S(1)}, bf16[2,8,176,128]{3,2,1,0:T(8,128)(2,1)S(1)}) custom-call(bf16[16,192,128]{2,1,0:T(8,128)(2,1)S(1)} %all-to-all-done.tokens_in, f32[6,192]{1,0:T(8,128)S(1)} %pad_maximum_fusion.taps, bf16[8,256,128]{2,1,0:T(8,128)(2,1)S(1)} %get-tuple-element.68.one, ...), custom_call_target="tpu_custom_call" | custom-call | tf_op jit(solution)/shard_map/mixer/pallas_call | solution.py:115
  46.1 0.1 collective-permute-start.10
  46.2 0.2 token_grad_message.1.grad_x
  46.4 2.0 %collective-permute-done.10.got = bf16[2,8,176,128]{3,2,1,0:T(8,128)(2,1)S(1)} collective-permute-done((bf16[2,8,176,128]{3,2,1,0:T(8,128)(2,1)S(1)}, bf16[2,8,176,128]{3,2,1,0:T(8,128)(2,1)S(1)}, u32[]{:S(2)}, u32[]{:S(2)}) %collective-permute-start.10) | collective-permute-done | bytes 720928 | tf_op jit(solution)/shard_map/ppermute | solution.py:657
  48.4 0.9 add_cores.1
  49.3 4.4 %all-to-all-start.1 = ((bf16[16,128,128]{2,1,0:T(8,128)(2,1)}), bf16[16,128,128]{2,1,0:T(8,128)(2,1)S(1)}, u32[]{:S(2)}, u32[]{:S(2)}) async-start(bf16[16,128,128]{2,1,0:T(8,128)(2,1)} %get-tuple-element.81), calls=%async_computation.1 | async-start | bytes 1048576 | tf_op jit(solution)/shard_map/all_to_all | solution.py:647
  53.7 1.9 %collective-permute-start.11 = (bf16[4,144,128]{2,1,0:T(8,128)(2,1)S(1)}, bf16[4,144,128]{2,1,0:T(8,128)(2,1)S(1)}, u32[]{:S(2)}, u32[]{:S(2)}) collective-permute-start(bf16[4,144,128]{2,1,0:T(8,128)(2,1)S(1)} %get-tuple-element.78), channel_id=1, source_target_pairs={{0,1},{1,0},{2,3},{3,2},{4,5},{5,4},{6,7},{7,6},{8,9},{9,8},{10,11... | collective-permute-start | bytes 442376 | tf_op jit(solution)/shard_map/ppermute | solution.py:822
  55.6 1.5 %collective-permute-start.12 = (bf16[4,144,128]{2,1,0:T(8,128)(2,1)S(1)}, bf16[4,144,128]{2,1,0:T(8,128)(2,1)S(1)}, u32[]{:S(2)}, u32[]{:S(2)}) collective-permute-start(bf16[4,144,128]{2,1,0:T(8,128)(2,1)S(1)} %get-tuple-element.79), channel_id=1, source_target_pairs={{0,16},{1,17},{2,18},{3,19},{4,20},{5,21},{6,22},{7,23},{8,24},{9,... | collective-permute-start | bytes 442376 | tf_op jit(solution)/shard_map/ppermute | solution.py:822
  57.1 0.2 collective-permute-start.13
  57.3 5.0 %collective-permute-done.11.refs_1_ = bf16[4,144,128]{2,1,0:T(8,128)(2,1)S(1)} collective-permute-done((bf16[4,144,128]{2,1,0:T(8,128)(2,1)S(1)}, bf16[4,144,128]{2,1,0:T(8,128)(2,1)S(1)}, u32[]{:S(2)}, u32[]{:S(2)}) %collective-permute-start.11) | collective-permute-done | bytes 147488 | tf_op jit(solution)/shard_map/ppermute | solution.py:822
  62.3 2.6 %collective-permute-done.12.refs_2_ = bf16[4,144,128]{2,1,0:T(8,128)(2,1)S(1)} collective-permute-done((bf16[4,144,128]{2,1,0:T(8,128)(2,1)S(1)}, bf16[4,144,128]{2,1,0:T(8,128)(2,1)S(1)}, u32[]{:S(2)}, u32[]{:S(2)}) %collective-permute-start.12) | collective-permute-done | bytes 147488 | tf_op jit(solution)/shard_map/ppermute | solution.py:822
  64.9 4.6 %collective-permute-done.13.refs_3_ = bf16[4,144,128]{2,1,0:T(8,128)(2,1)S(1)} collective-permute-done((bf16[4,144,128]{2,1,0:T(8,128)(2,1)S(1)}, bf16[4,144,128]{2,1,0:T(8,128)(2,1)S(1)}, u32[]{:S(2)}, u32[]{:S(2)}) %collective-permute-start.13) | collective-permute-done | bytes 147488 | tf_op jit(solution)/shard_map/ppermute | solution.py:822
  69.4 0.7 add_fold.1
  70.2 0.0 all-to-all-done.1.got
  70.2 0.5 collective-permute-start.14
  70.7 4.8 %all-to-all-start.2 = ((bf16[4,144,128]{2,1,0:T(8,128)(2,1)}), bf16[4,144,128]{2,1,0:T(8,128)(2,1)S(1)}, u32[]{:S(2)}, u32[]{:S(2)}) async-start(bf16[4,144,128]{2,1,0:T(8,128)(2,1)} %add_fold.1), calls=%async_computation.2 | async-start | bytes 294912 | tf_op jit(solution)/shard_map/all_to_all | solution.py:652
  75.5 0.0 collective-permute-start.15
  75.5 0.0 collective-permute-done.14.refs_1_
  75.5 0.5 collective-permute-start.16
  76.0 0.9 %token_grad.1 = bf16[128,1536]{1,0:T(8,128)(2,1)} custom-call(bf16[16,128,128]{2,1,0:T(8,128)(2,1)S(1)} %all-to-all-done.1.got), custom_call_target="tpu_custom_call" | custom-call | tf_op jit(solution)/shard_map/token_grad/pallas_call | solution.py:115
  76.9 0.0 collective-permute-done.15.refs_2_
  76.9 0.1 collective-permute-done.16.refs_3_
  77.0 1.2 %finish_filter.1 = (bf16[128,1536]{1,0:T(8,128)(2,1)}, f32[3,1536]{1,0:T(4,128)}, f32[3,1536]{1,0:T(4,128)}) custom-call(bf16[16,32,128]{2,1,0:T(8,128)(2,1)S(1)} %filter_rows.1.refs_0_, bf16[16,32,128]{2,1,0:T(8,128)(2,1)S(1)} %collective-permute-done.14.refs_1_, bf16[16,32,128]{2,1,0:T(8,128)(2,1)S(1)} %collective-permute-done.15.refs_2_, ...), custom_call_target="tpu_custom_call" | custom-call | tf_op jit(solution)/shard_map/finish_filter/pallas_call | solution.py:115
  78.2 3.2 %all-to-all-done.2.got = bf16[4,144,128]{2,1,0:T(8,128)(2,1)S(1)} async-done(((bf16[4,144,128]{2,1,0:T(8,128)(2,1)}), bf16[4,144,128]{2,1,0:T(8,128)(2,1)S(1)}, u32[]{:S(2)}, u32[]{:S(2)}) %all-to-all-start.2) | async-done | bytes 147488 | tf_op jit(solution)/shard_map/all_to_all | solution.py:652
  81.5 0.1 collective-permute-start.19
  81.5 1.1 %collective-permute-start.18 = (bf16[144,128]{1,0:T(8,128)(2,1)S(1)}, bf16[144,128]{1,0:T(8,128)(2,1)S(1)}, u32[]{:S(2)}, u32[]{:S(2)}) collective-permute-start(bf16[144,128]{1,0:T(8,128)(2,1)S(1)} %sum_sources.1.refs_0_), channel_id=1, source_target_pairs={{0,8},{8,0},{16,24},{24,16},{1,9},{9,1},{17,25},{25,17},{2,10},{10... | collective-permute-start | bytes 110600 | tf_op jit(solution)/shard_map/ppermute | solution.py:667
  82.7 1.0 %collective-permute-start.17 = (bf16[144,128]{1,0:T(8,128)(2,1)S(1)}, bf16[144,128]{1,0:T(8,128)(2,1)S(1)}, u32[]{:S(2)}, u32[]{:S(2)}) collective-permute-start(bf16[144,128]{1,0:T(8,128)(2,1)S(1)} %sum_sources.1.refs_0_), channel_id=1, source_target_pairs={{0,16},{8,24},{16,0},{24,8},{1,17},{9,25},{17,1},{25,9},{2,18},{10... | collective-permute-start | bytes 110600 | tf_op jit(solution)/shard_map/ppermute | solution.py:667
  83.7 1.2 %collective-permute-done.19.refs_3_ = bf16[144,128]{1,0:T(8,128)(2,1)S(1)} collective-permute-done((bf16[144,128]{1,0:T(8,128)(2,1)S(1)}, bf16[144,128]{1,0:T(8,128)(2,1)S(1)}, u32[]{:S(2)}, u32[]{:S(2)}) %collective-permute-start.19) | collective-permute-done | bytes 36896 | tf_op jit(solution)/shard_map/ppermute | solution.py:667
  84.9 0.0 collective-permute-done.18.refs_2_
  84.9 1.7 %collective-permute-done.17.refs_1_ = bf16[144,128]{1,0:T(8,128)(2,1)S(1)} collective-permute-done((bf16[144,128]{1,0:T(8,128)(2,1)S(1)}, bf16[144,128]{1,0:T(8,128)(2,1)S(1)}, u32[]{:S(2)}, u32[]{:S(2)}) %collective-permute-start.17) | collective-permute-done | bytes 36896 | tf_op jit(solution)/shard_map/ppermute | solution.py:667
  86.6 0.7 finish_factors.1
  (9 shorter events, 0.1 us)
Async XLA Ops:
  0.6 7.6 %copy-start = (bf16[1,128,1536]{2,1,0:T(8,128)(2,1)S(1)}, bf16[1,128,1536]{2,1,0:T(8,128)(2,1)}, u32[]{:S(2)}) copy-start(bf16[1,128,1536]{2,1,0:T(8,128)(2,1)} %param.9) | copy-start | bytes 1179652
  2.5 7.8 %collective-permute-start = (bf16[240,128]{1,0:T(8,128)(2,1)}, bf16[240,128]{1,0:T(8,128)(2,1)S(1)}, u32[]{:S(2)}, u32[]{:S(2)}) collective-permute-start(bf16[240,128]{1,0:T(8,128)(2,1)} %get-tuple-element.53), channel_id=1, source_target_pairs={{0,2},{1,3},{2,0},{3,1},{4,6},{5,7},{6,4},{7,5},{8,10},{9,11},{10,... | collective-permute-start | bytes 184328 | tf_op jit(solution)/shard_map/ppermute | solution.py:703
  5.6 6.6 %collective-permute-start.1 = (bf16[240,128]{1,0:T(8,128)(2,1)}, bf16[240,128]{1,0:T(8,128)(2,1)S(1)}, u32[]{:S(2)}, u32[]{:S(2)}) collective-permute-start(bf16[240,128]{1,0:T(8,128)(2,1)} %get-tuple-element.54), channel_id=1, source_target_pairs={{0,4},{1,5},{2,6},{3,7},{4,0},{5,1},{6,2},{7,3},{8,12},{9,13},{10,... | collective-permute-start | bytes 184328 | tf_op jit(solution)/shard_map/ppermute | solution.py:703
  8.2 6.2 %collective-permute-start.2 = (bf16[240,128]{1,0:T(8,128)(2,1)}, bf16[240,128]{1,0:T(8,128)(2,1)S(1)}, u32[]{:S(2)}, u32[]{:S(2)}) collective-permute-start(bf16[240,128]{1,0:T(8,128)(2,1)} %get-tuple-element.55), channel_id=1, source_target_pairs={{0,6},{1,7},{2,4},{3,5},{4,2},{5,3},{6,0},{7,1},{8,14},{9,15},{10,... | collective-permute-start | bytes 184328 | tf_op jit(solution)/shard_map/ppermute | solution.py:703
  8.2 1.0 %copy-start.1 = (bf16[1,128,1536]{2,1,0:T(8,128)(2,1)S(1)}, bf16[1,128,1536]{2,1,0:T(8,128)(2,1)}, u32[]{:S(2)}) copy-start(bf16[1,128,1536]{2,1,0:T(8,128)(2,1)} %param.10) | copy-start | bytes 1179652
  14.4 4.9 %copy-start.2 = (bf16[240,128]{1,0:T(8,128)(2,1)S(1)}, bf16[240,128]{1,0:T(8,128)(2,1)}, u32[]{:S(2)}) copy-start(bf16[240,128]{1,0:T(8,128)(2,1)} %get-tuple-element.52.refs_0_) | copy-start | bytes 184324
  14.4 24.0 %all-to-all-start = ((bf16[16,192,128]{2,1,0:T(8,128)(2,1)}), bf16[16,192,128]{2,1,0:T(8,128)(2,1)S(1)}, u32[]{:S(2)}, u32[]{:S(2)}) async-start(bf16[16,192,128]{2,1,0:T(8,128)(2,1)} %token_message.1), calls=%async_computation | async-start | bytes 1572864 | tf_op jit(solution)/shard_map/all_to_all | solution.py:647
  19.4 15.0 %collective-permute-start.3 = (bf16[4,192,128]{2,1,0:T(8,128)(2,1)S(1)}, bf16[4,192,128]{2,1,0:T(8,128)(2,1)S(1)}, u32[]{:S(2)}, u32[]{:S(2)}) collective-permute-start(bf16[4,192,128]{2,1,0:T(8,128)(2,1)S(1)} %get-tuple-element.57), channel_id=1, source_target_pairs={{0,1},{1,0},{2,3},{3,2},{4,5},{5,4},{6,7},{7,6},{8,9},{9,8},{10,11... | collective-permute-start | bytes 589832 | tf_op jit(solution)/shard_map/ppermute | solution.py:713
  21.4 10.6 %collective-permute-start.5 = (bf16[4,144,128]{2,1,0:T(8,128)(2,1)S(1)}, bf16[4,144,128]{2,1,0:T(8,128)(2,1)S(1)}, u32[]{:S(2)}, u32[]{:S(2)}) collective-permute-start(bf16[4,144,128]{2,1,0:T(8,128)(2,1)S(1)} %slice.4), channel_id=1, source_target_pairs={{0,17},{1,16},{2,19},{3,18},{4,21},{5,20},{6,23},{7,22},{8,25},{9,... | collective-permute-start | bytes 442376 | tf_op jit(solution)/shard_map/ppermute | solution.py:713
  23.0 10.9 %collective-permute-start.4 = (bf16[4,144,128]{2,1,0:T(8,128)(2,1)S(1)}, bf16[4,144,128]{2,1,0:T(8,128)(2,1)S(1)}, u32[]{:S(2)}, u32[]{:S(2)}) collective-permute-start(bf16[4,144,128]{2,1,0:T(8,128)(2,1)S(1)} %slice.4), channel_id=1, source_target_pairs={{0,16},{1,17},{2,18},{3,19},{4,20},{5,21},{6,22},{7,23},{8,24},{9,... | collective-permute-start | bytes 442376 | tf_op jit(solution)/shard_map/ppermute | solution.py:713
  23.1 11.3 %copy-start.4 = (f32[3,1536]{1,0:T(4,128)S(1)}, f32[3,1536]{1,0:T(4,128)}, u32[]{:S(2)}) copy-start(f32[3,1536]{1,0:T(4,128)} %param.12) | copy-start | bytes 55300
  23.1 11.3 %copy-start.3 = (f32[3,1536]{1,0:T(4,128)S(1)}, f32[3,1536]{1,0:T(4,128)}, u32[]{:S(2)}) copy-start(f32[3,1536]{1,0:T(4,128)} %param.11) | copy-start | bytes 55300
  23.1 11.5 %collective-permute-start.6 = (bf16[4,192,128]{2,1,0:T(8,128)(2,1)S(1)}, bf16[4,192,128]{2,1,0:T(8,128)(2,1)S(1)}, u32[]{:S(2)}, u32[]{:S(2)}) collective-permute-start(bf16[4,192,128]{2,1,0:T(8,128)(2,1)S(1)} %get-tuple-element.60.refs_0_), channel_id=1, source_target_pairs={{0,8},{8,0},{16,24},{24,16},{1,9},{9,1},{17,25},{25,17},{2,10},{10... | collective-permute-start | bytes 589832 | tf_op jit(solution)/shard_map/ppermute | solution.py:657
  32.1 2.5 %collective-permute-start.9 = (bf16[4,144,128]{2,1,0:T(8,128)(2,1)S(1)}, bf16[4,144,128]{2,1,0:T(8,128)(2,1)S(1)}, u32[]{:S(2)}, u32[]{:S(2)}) collective-permute-start(bf16[4,144,128]{2,1,0:T(8,128)(2,1)S(1)} %collective-permute-done.5.refs_3_), channel_id=1, source_target_pairs={{0,8},{8,0},{16,24},{24,16},{1,9},{9,1},{17,25},{25,17},{2,10},{10... | collective-permute-start | bytes 442376 | tf_op jit(solution)/shard_map/ppermute | solution.py:657
  33.9 1.4 %collective-permute-start.8 = (bf16[4,144,128]{2,1,0:T(8,128)(2,1)S(1)}, bf16[4,144,128]{2,1,0:T(8,128)(2,1)S(1)}, u32[]{:S(2)}, u32[]{:S(2)}) collective-permute-start(bf16[4,144,128]{2,1,0:T(8,128)(2,1)S(1)} %collective-permute-done.4.refs_2_), channel_id=1, source_target_pairs={{0,8},{8,0},{16,24},{24,16},{1,9},{9,1},{17,25},{25,17},{2,10},{10... | collective-permute-start | bytes 442376 | tf_op jit(solution)/shard_map/ppermute | solution.py:657
  34.4 1.4 %collective-permute-start.7 = (bf16[4,192,128]{2,1,0:T(8,128)(2,1)S(1)}, bf16[4,192,128]{2,1,0:T(8,128)(2,1)S(1)}, u32[]{:S(2)}, u32[]{:S(2)}) collective-permute-start(bf16[4,192,128]{2,1,0:T(8,128)(2,1)S(1)} %collective-permute-done.3.refs_1_), channel_id=1, source_target_pairs={{0,8},{8,0},{16,24},{24,16},{1,9},{9,1},{17,25},{25,17},{2,10},{10... | collective-permute-start | bytes 589832 | tf_op jit(solution)/shard_map/ppermute | solution.py:657
  46.1 2.3 %collective-permute-start.10 = (bf16[2,8,176,128]{3,2,1,0:T(8,128)(2,1)S(1)}, bf16[2,8,176,128]{3,2,1,0:T(8,128)(2,1)S(1)}, u32[]{:S(2)}, u32[]{:S(2)}) collective-permute-start(bf16[2,8,176,128]{3,2,1,0:T(8,128)(2,1)S(1)} %get-tuple-element.76), channel_id=1, source_target_pairs={{0,8},{8,0},{16,24},{24,16},{1,9},{9,1},{17,25},{25,17},{2,10},{10... | collective-permute-start | bytes 2162696 | tf_op jit(solution)/shard_map/ppermute | solution.py:657
  49.3 20.9 %all-to-all-start.1 = ((bf16[16,128,128]{2,1,0:T(8,128)(2,1)}), bf16[16,128,128]{2,1,0:T(8,128)(2,1)S(1)}, u32[]{:S(2)}, u32[]{:S(2)}) async-start(bf16[16,128,128]{2,1,0:T(8,128)(2,1)} %get-tuple-element.81), calls=%async_computation.1 | async-start | bytes 1048576 | tf_op jit(solution)/shard_map/all_to_all | solution.py:647
  53.7 8.6 %collective-permute-start.11 = (bf16[4,144,128]{2,1,0:T(8,128)(2,1)S(1)}, bf16[4,144,128]{2,1,0:T(8,128)(2,1)S(1)}, u32[]{:S(2)}, u32[]{:S(2)}) collective-permute-start(bf16[4,144,128]{2,1,0:T(8,128)(2,1)S(1)} %get-tuple-element.78), channel_id=1, source_target_pairs={{0,1},{1,0},{2,3},{3,2},{4,5},{5,4},{6,7},{7,6},{8,9},{9,8},{10,11... | collective-permute-start | bytes 442376 | tf_op jit(solution)/shard_map/ppermute | solution.py:822
  55.6 9.2 %collective-permute-start.12 = (bf16[4,144,128]{2,1,0:T(8,128)(2,1)S(1)}, bf16[4,144,128]{2,1,0:T(8,128)(2,1)S(1)}, u32[]{:S(2)}, u32[]{:S(2)}) collective-permute-start(bf16[4,144,128]{2,1,0:T(8,128)(2,1)S(1)} %get-tuple-element.79), channel_id=1, source_target_pairs={{0,16},{1,17},{2,18},{3,19},{4,20},{5,21},{6,22},{7,23},{8,24},{9,... | collective-permute-start | bytes 442376 | tf_op jit(solution)/shard_map/ppermute | solution.py:822
  57.1 12.3 %collective-permute-start.13 = (bf16[4,144,128]{2,1,0:T(8,128)(2,1)S(1)}, bf16[4,144,128]{2,1,0:T(8,128)(2,1)S(1)}, u32[]{:S(2)}, u32[]{:S(2)}) collective-permute-start(bf16[4,144,128]{2,1,0:T(8,128)(2,1)S(1)} %get-tuple-element.80), channel_id=1, source_target_pairs={{0,17},{1,16},{2,19},{3,18},{4,21},{5,20},{6,23},{7,22},{8,25},{9,... | collective-permute-start | bytes 442376 | tf_op jit(solution)/shard_map/ppermute | solution.py:822
  70.2 5.3 %collective-permute-start.14 = (bf16[16,32,128]{2,1,0:T(8,128)(2,1)S(1)}, bf16[16,32,128]{2,1,0:T(8,128)(2,1)S(1)}, u32[]{:S(2)}, u32[]{:S(2)}) collective-permute-start(bf16[16,32,128]{2,1,0:T(8,128)(2,1)S(1)} %filter_rows.1.refs_0_), channel_id=1, source_target_pairs={{0,16},{8,24},{16,0},{24,8},{1,17},{9,25},{17,1},{25,9},{2,18},{10... | collective-permute-start | bytes 393224 | tf_op jit(solution)/shard_map/ppermute | solution.py:662
  70.7 10.8 %all-to-all-start.2 = ((bf16[4,144,128]{2,1,0:T(8,128)(2,1)}), bf16[4,144,128]{2,1,0:T(8,128)(2,1)S(1)}, u32[]{:S(2)}, u32[]{:S(2)}) async-start(bf16[4,144,128]{2,1,0:T(8,128)(2,1)} %add_fold.1), calls=%async_computation.2 | async-start | bytes 294912 | tf_op jit(solution)/shard_map/all_to_all | solution.py:652
  75.5 1.4 %collective-permute-start.15 = (bf16[16,32,128]{2,1,0:T(8,128)(2,1)S(1)}, bf16[16,32,128]{2,1,0:T(8,128)(2,1)S(1)}, u32[]{:S(2)}, u32[]{:S(2)}) collective-permute-start(bf16[16,32,128]{2,1,0:T(8,128)(2,1)S(1)} %filter_rows.1.refs_0_), channel_id=1, source_target_pairs={{0,8},{8,0},{16,24},{24,16},{1,9},{9,1},{17,25},{25,17},{2,10},{10... | collective-permute-start | bytes 393224 | tf_op jit(solution)/shard_map/ppermute | solution.py:657
  75.5 1.5 %collective-permute-start.16 = (bf16[16,32,128]{2,1,0:T(8,128)(2,1)S(1)}, bf16[16,32,128]{2,1,0:T(8,128)(2,1)S(1)}, u32[]{:S(2)}, u32[]{:S(2)}) collective-permute-start(bf16[16,32,128]{2,1,0:T(8,128)(2,1)S(1)} %collective-permute-done.14.refs_1_), channel_id=1, source_target_pairs={{0,8},{8,0},{16,24},{24,16},{1,9},{9,1},{17,25},{25,17},{2,10},{10... | collective-permute-start | bytes 393224 | tf_op jit(solution)/shard_map/ppermute | solution.py:657
  81.5 3.4 %collective-permute-start.19 = (bf16[144,128]{1,0:T(8,128)(2,1)S(1)}, bf16[144,128]{1,0:T(8,128)(2,1)S(1)}, u32[]{:S(2)}, u32[]{:S(2)}) collective-permute-start(bf16[144,128]{1,0:T(8,128)(2,1)S(1)} %sum_sources.1.refs_0_), channel_id=1, source_target_pairs={{0,24},{8,16},{16,8},{24,0},{1,25},{9,17},{17,9},{25,1},{2,26},{10... | collective-permute-start | bytes 110600 | tf_op jit(solution)/shard_map/ppermute | solution.py:667
  81.5 3.4 %collective-permute-start.18 = (bf16[144,128]{1,0:T(8,128)(2,1)S(1)}, bf16[144,128]{1,0:T(8,128)(2,1)S(1)}, u32[]{:S(2)}, u32[]{:S(2)}) collective-permute-start(bf16[144,128]{1,0:T(8,128)(2,1)S(1)} %sum_sources.1.refs_0_), channel_id=1, source_target_pairs={{0,8},{8,0},{16,24},{24,16},{1,9},{9,1},{17,25},{25,17},{2,10},{10... | collective-permute-start | bytes 110600 | tf_op jit(solution)/shard_map/ppermute | solution.py:667
  82.7 4.0 %collective-permute-start.17 = (bf16[144,128]{1,0:T(8,128)(2,1)S(1)}, bf16[144,128]{1,0:T(8,128)(2,1)S(1)}, u32[]{:S(2)}, u32[]{:S(2)}) collective-permute-start(bf16[144,128]{1,0:T(8,128)(2,1)S(1)} %sum_sources.1.refs_0_), channel_id=1, source_target_pairs={{0,16},{8,24},{16,0},{24,8},{1,17},{9,25},{17,1},{25,9},{2,18},{10... | collective-permute-start | bytes 110600 | tf_op jit(solution)/shard_map/ppermute | solution.py:667

commit v7 on v6

--- a/solution.py
+++ b/solution.py
@@ -23,7 +23,6 @@
         self.nblk = seq
         self.near = 2 if seq % 2 == 0 else 1
         self.layers = seq // self.near
-        self.layer_groups = [list(range(y, seq, self.near)) for y in range(self.near)]
         self.kloc = mix_two.shape[1]
         half_dp = dp // 2
         self.fold = max(
@@ -572,21 +571,24 @@
 
 
 def add_fold_kernel(p, *refs):
+    count = len(p.plane())
+    terms, outs = refs[:count], refs[count:]
+    z = lax.axis_index("seq") // p.near
+    totals = []
+    for layer in range(p.layers):
+        total = terms[0][layer].astype(F32)
+        for term in terms[1:]:
+            total += term[layer].astype(F32)
+        totals.append(total.astype(BF16))
+    for step in range(p.layers):
+        outs[step][...] = pick(p, [totals[p.layer_partner(at, step)] for at in range(p.layers)], z)
+
+
+def sum_kernel(p, *refs):
     terms, out = refs[:-1], refs[-1]
-
-    def one_layer(z):
-        total = terms[0][z].astype(F32)
-        for term in terms[1:]:
-            total += term[z].astype(F32)
-        out[z] = total.astype(BF16)
-
-    each(p.layers, one_layer)
-
-
-def sum_kernel(p, got, out):
-    total = got[0].astype(F32)
-    for q in range(1, p.layers):
-        total += got[q].astype(F32)
+    total = terms[0][...].astype(F32)
+    for term in terms[1:]:
+        total += term[...].astype(F32)
     out[...] = total.astype(BF16)
 
 
@@ -648,10 +650,14 @@
             array, ("dp", "seq"), 0, 0, tiled=True, axis_index_groups=p.group_lists
         )
 
-    def across_layers(array):
-        return lax.all_to_all(
-            array, "seq", 0, 0, tiled=True, axis_index_groups=p.layer_groups
-        )
+    def across_layers(pieces):
+        got = [pieces[0]]
+        for step in range(1, p.layers):
+            moves = [
+                (s, p.layer_partner(s // p.near, step) * p.near + s % p.near) for s in range(p.seq)
+            ]
+            got.append(lax.ppermute(pieces[step], "seq", moves))
+        return got
 
     def swap(array):
         return lax.ppermute(array, "dp", p.across_cores())
@@ -695,12 +701,7 @@
         limit=60,
         name="factor_message",
     )
-    factors = [message[0]]
-    for step in range(1, p.layers):
-        moves = [
-            (s, p.layer_partner(s // p.near, step) * p.near + s % p.near) for s in range(p.seq)
-        ]
-        factors.append(lax.ppermute(message[step], "seq", moves))
+    factors = across_layers(message)
     near_messages = call(
         functools.partial(near_message_kernel, p),
         [shape(p.layers, p.mrows + p.frows, blk)] * p.near,
@@ -812,18 +813,16 @@
     )
     received = shuffle(message)
 
-    message = shares[0]
-    if len(shares) > 1:
-        message = call(
-            functools.partial(add_fold_kernel, p),
-            shape(p.layers, p.mrows, blk),
-            message,
-            *[
-                lax.ppermute(share, ("dp", "seq"), p.across_plane(*steps))
-                for share, steps in zip(shares[1:], p.plane()[1:])
-            ],
-            name="add_fold",
-        )
+    message = call(
+        functools.partial(add_fold_kernel, p),
+        [shape(p.mrows, blk)] * p.layers,
+        shares[0],
+        *[
+            lax.ppermute(share, ("dp", "seq"), p.across_plane(*steps))
+            for share, steps in zip(shares[1:], p.plane()[1:])
+        ],
+        name="add_fold",
+    )
     message, received = lax.optimization_barrier((message, received))
     factor_grads = across_layers(message)
 
@@ -833,7 +832,7 @@
         received,
         name="filter_rows",
     )
-    rows = gathered(summed_over_groups(rows), lambda a: a)
+    rows = gathered_at_once(summed_over_groups(rows))
     token_grad = call(
         functools.partial(token_grad_kernel, p), shape(blk, p.channels), received, name="token_grad"
     )
@@ -851,7 +850,7 @@
         (factor_grads, token_grad, grad_filter, sum_value, sum_gate)
     )
     sums = call(
-        functools.partial(sum_kernel, p), shape(p.mrows, blk), factor_grads, name="sum_sources"
+        functools.partial(sum_kernel, p), shape(p.mrows, blk), *factor_grads, name="sum_sources"
     )
     grad_one, grad_four, *small = call(
         functools.partial(finish_factors_kernel, p),

time: 87.9 us -> 87.4 us (level)
  starting transfers between devices: 30.3 us -> 33.2 us
  waiting for transfers between devices: 39.8 us -> 37.1 us
    ppermute x4 -> x6, starting transfers between devices: 6.16 us -> 12.1 us  [across_layers(): got.append(lax.ppermute(pieces[step], 'seq', moves))]
    all_to_all x1 -> x0, starting transfers between devices: 4.81 us -> none  [across_layers(): lax.all_to_all(array, 'seq', 0, 0, tiled=True, axis_index_groups=p.layer_...]
    all_to_all x1 -> x0, waiting for transfers between devices: 3.21 us -> none  [across_layers(): lax.all_to_all(array, 'seq', 0, 0, tiled=True, axis_index_groups=p.layer_...]
    ppermute x3 -> x6, starting transfers between devices: 2.2 us -> 4.4 us  [gathered_at_once(): lax.ppermute(array, 'dp', p.across_fold(step, side))]
    ppermute x4 -> x6, waiting for transfers between devices: 4.08 us -> 4.76 us  [across_layers(): got.append(lax.ppermute(pieces[step], 'seq', moves))]
    ppermute x7 -> x5, waiting for transfers between devices: 3.39 us -> 3.27 us  [swap(): return lax.ppermute(array, 'dp', p.across_cores())]
    ppermute x3 -> x6, waiting for transfers between devices: 2.97 us -> 2.93 us  [gathered_at_once(): lax.ppermute(array, 'dp', p.across_fold(step, side))]
  transfers between devices with their start and end apart: 23 -> 25, of which waited for: 16 -> 16; matrix products, arithmetic and copies ran while one was open for 0% -> 0% of each run, Pallas kernels for 5% -> 4%
where the time goes in v7:
time: 87.4 us; the launch traced here: 87 us
  waiting for transfers between devices  37.1 us (42%)
  starting transfers between devices  33.2 us (38%)
  Pallas kernels  14.7 us (17%)
  local copies, waits for them, and re-layouts  1.02 us (1%)
    pallas_call x14, Pallas kernels, call(): pl.pallas_call(kernel, out_shape=out_shape, in_specs=[FAR if i in far els...  14.7 us
    ppermute x3, waiting for transfers between devices, shards(): lax.ppermute(share, ('dp', 'seq'), p.across_plane(*steps))  12.2 us
    ppermute x6, starting transfers between devices, across_layers(): got.append(lax.ppermute(pieces[step], 'seq', moves))  12.1 us
    ppermute x3, waiting for transfers between devices, shards(): lax.ppermute(piece, ('dp', 'seq'), p.across_plane(step, near_step))  11.3 us
    all_to_all x2, starting transfers between devices, shuffle(): lax.all_to_all(array, ('dp', 'seq'), 0, 0, tiled=True, axis_index_groups=...  9.36 us
    ppermute x6, waiting for transfers between devices, across_layers(): got.append(lax.ppermute(pieces[step], 'seq', moves))  4.76 us
    ppermute x6, starting transfers between devices, gathered_at_once(): lax.ppermute(array, 'dp', p.across_fold(step, side))  4.4 us
    ppermute x3, starting transfers between devices, shards(): lax.ppermute(piece, ('dp', 'seq'), p.across_plane(step, near_step))  3.62 us
  transfers between devices with their start and end apart: 25, of which 16 were waited for; matrix products, arithmetic and copies ran while one was open for 0% of the time, Pallas kernels for 4%

profile of v7, /device:TPU:0, one launch (start us, length us, event | category | flops | bytes accessed | tf_op | source)
XLA Modules:
  0.0 87.0 jit_solution(13628302005987203606)
XLA Ops:
  0.6 1.9 %factor_message.1 = (bf16[240,128]{1,0:T(8,128)(2,1)}, bf16[240,128]{1,0:T(8,128)(2,1)}, bf16[240,128]{1,0:T(8,128)(2,1)}, bf16[240,128]{1,0:T(8,128)(2,1)}) custom-call(bf16[128,1536]{1,0:T(8,128)(2,1)} %bitcast.32, bf16[2,128,128]{2,1,0:T(8,128)(2,1)} %bitcast.33, bf16[2,128,128]{2,1,0:T(8,128)(2,1)} %bitcast.34, bf16[2,64,16]{2,1,0:T(8,128)(2,1)} %bitcast.35, ...), custom_call_target="tpu_custom_call" | custom-call | tf_op jit(solution)/shard_map/factor_message/pallas_call | solution.py:114
  2.5 3.1 %collective-permute-start = (bf16[240,128]{1,0:T(8,128)(2,1)}, bf16[240,128]{1,0:T(8,128)(2,1)S(1)}, u32[]{:S(2)}, u32[]{:S(2)}) collective-permute-start(bf16[240,128]{1,0:T(8,128)(2,1)} %get-tuple-element.63), channel_id=1, source_target_pairs={{0,2},{1,3},{2,0},{3,1},{4,6},{5,7},{6,4},{7,5},{8,10},{9,11},{10,... | collective-permute-start | bytes 184328 | tf_op jit(solution)/shard_map/ppermute | solution.py:659
  5.6 2.6 %collective-permute-start.1 = (bf16[240,128]{1,0:T(8,128)(2,1)}, bf16[240,128]{1,0:T(8,128)(2,1)S(1)}, u32[]{:S(2)}, u32[]{:S(2)}) collective-permute-start(bf16[240,128]{1,0:T(8,128)(2,1)} %get-tuple-element.64), channel_id=1, source_target_pairs={{0,4},{1,5},{2,6},{3,7},{4,0},{5,1},{6,2},{7,3},{8,12},{9,13},{10,... | collective-permute-start | bytes 184328 | tf_op jit(solution)/shard_map/ppermute | solution.py:659
  8.2 0.0 collective-permute-start.2
  8.2 1.0 %copy-done.1 = bf16[1,128,1536]{2,1,0:T(8,128)(2,1)S(1)} copy-done((bf16[1,128,1536]{2,1,0:T(8,128)(2,1)S(1)}, bf16[1,128,1536]{2,1,0:T(8,128)(2,1)}, u32[]{:S(2)}) %copy-start.1) | copy-done | bytes 393240
  9.2 1.1 %token_message.1 = bf16[16,192,128]{2,1,0:T(8,128)(2,1)} custom-call(bf16[128,1536]{1,0:T(8,128)(2,1)S(1)} %bitcast.28, bf16[128,1536]{1,0:T(8,128)(2,1)S(1)} %bitcast.29), custom_call_target="tpu_custom_call" | custom-call | tf_op jit(solution)/shard_map/token_message/pallas_call | solution.py:114
  10.3 0.0 collective-permute-done.refs_1_
  10.3 1.8 %collective-permute-done.1.refs_2_ = bf16[240,128]{1,0:T(8,128)(2,1)S(1)} collective-permute-done((bf16[240,128]{1,0:T(8,128)(2,1)}, bf16[240,128]{1,0:T(8,128)(2,1)S(1)}, u32[]{:S(2)}, u32[]{:S(2)}) %collective-permute-start.1) | collective-permute-done | bytes 61472 | tf_op jit(solution)/shard_map/ppermute | solution.py:659
  12.2 2.3 %collective-permute-done.2.refs_3_ = bf16[240,128]{1,0:T(8,128)(2,1)S(1)} collective-permute-done((bf16[240,128]{1,0:T(8,128)(2,1)}, bf16[240,128]{1,0:T(8,128)(2,1)S(1)}, u32[]{:S(2)}, u32[]{:S(2)}) %collective-permute-start.2) | collective-permute-done | bytes 61472 | tf_op jit(solution)/shard_map/ppermute | solution.py:659
  14.4 4.9 %all-to-all-start = ((bf16[16,192,128]{2,1,0:T(8,128)(2,1)}), bf16[16,192,128]{2,1,0:T(8,128)(2,1)S(1)}, u32[]{:S(2)}, u32[]{:S(2)}) async-start(bf16[16,192,128]{2,1,0:T(8,128)(2,1)} %token_message.1), calls=%async_computation | async-start | bytes 1572864 | tf_op jit(solution)/shard_map/all_to_all | solution.py:649
  19.4 0.1 near_message.1
  19.4 2.0 %collective-permute-start.3 = (bf16[4,192,128]{2,1,0:T(8,128)(2,1)S(1)}, bf16[4,192,128]{2,1,0:T(8,128)(2,1)S(1)}, u32[]{:S(2)}, u32[]{:S(2)}) collective-permute-start(bf16[4,192,128]{2,1,0:T(8,128)(2,1)S(1)} %get-tuple-element.67), channel_id=1, source_target_pairs={{0,1},{1,0},{2,3},{3,2},{4,5},{5,4},{6,7},{7,6},{8,9},{9,8},{10,11... | collective-permute-start | bytes 589832 | tf_op jit(solution)/shard_map/ppermute | solution.py:714
  21.4 1.5 %collective-permute-start.5 = (bf16[4,144,128]{2,1,0:T(8,128)(2,1)S(1)}, bf16[4,144,128]{2,1,0:T(8,128)(2,1)S(1)}, u32[]{:S(2)}, u32[]{:S(2)}) collective-permute-start(bf16[4,144,128]{2,1,0:T(8,128)(2,1)S(1)} %slice.4), channel_id=1, source_target_pairs={{0,17},{1,16},{2,19},{3,18},{4,21},{5,20},{6,23},{7,22},{8,25},{9,... | collective-permute-start | bytes 442376 | tf_op jit(solution)/shard_map/ppermute | solution.py:714
  23.0 0.1 collective-permute-start.4
  23.1 0.0 collective-permute-start.6
  23.1 9.0 %collective-permute-done.5.refs_3_ = bf16[4,144,128]{2,1,0:T(8,128)(2,1)S(1)} collective-permute-done((bf16[4,144,128]{2,1,0:T(8,128)(2,1)S(1)}, bf16[4,144,128]{2,1,0:T(8,128)(2,1)S(1)}, u32[]{:S(2)}, u32[]{:S(2)}) %collective-permute-start.5) | collective-permute-done | bytes 147488 | tf_op jit(solution)/shard_map/ppermute | solution.py:714
  32.1 0.0 collective-permute-start.9
  32.1 1.8 %collective-permute-done.4.refs_2_ = bf16[4,144,128]{2,1,0:T(8,128)(2,1)S(1)} collective-permute-done((bf16[4,144,128]{2,1,0:T(8,128)(2,1)S(1)}, bf16[4,144,128]{2,1,0:T(8,128)(2,1)S(1)}, u32[]{:S(2)}, u32[]{:S(2)}) %collective-permute-start.4) | collective-permute-done | bytes 147488 | tf_op jit(solution)/shard_map/ppermute | solution.py:714
  33.9 0.0 collective-permute-start.8
  33.9 0.5 collective-permute-done.3.refs_1_
  34.4 0.0 collective-permute-start.7
  34.4 0.1 fusion
  34.5 0.1 pad_maximum_fusion.taps
  34.6 0.0 collective-permute-done.6.refs_4_
  34.6 0.0 collective-permute-done.9.refs_7_
  34.6 0.7 collective-permute-done.8.refs_6_
  35.2 0.6 collective-permute-done.7.refs_5_
  35.8 2.6 %all-to-all-done.tokens_in = bf16[16,192,128]{2,1,0:T(8,128)(2,1)S(1)} async-done(((bf16[16,192,128]{2,1,0:T(8,128)(2,1)}), bf16[16,192,128]{2,1,0:T(8,128)(2,1)S(1)}, u32[]{:S(2)}, u32[]{:S(2)}) %all-to-all-start) | async-done | bytes 786464 | tf_op jit(solution)/shard_map/all_to_all | solution.py:649
  38.5 0.7 prepare.1
  39.2 0.5 block_factors.1
  39.6 6.5 %mixer.1 = (bf16[8,128,192]{2,1,0:T(8,128)(2,1)S(1)}, bf16[2,8,176,128]{3,2,1,0:T(8,128)(2,1)S(1)}, bf16[2,8,176,128]{3,2,1,0:T(8,128)(2,1)S(1)}) custom-call(bf16[16,192,128]{2,1,0:T(8,128)(2,1)S(1)} %all-to-all-done.tokens_in, f32[6,192]{1,0:T(8,128)S(1)} %pad_maximum_fusion.taps, bf16[8,256,128]{2,1,0:T(8,128)(2,1)S(1)} %get-tuple-element.78.one, ...), custom_call_target="tpu_custom_call" | custom-call | tf_op jit(solution)/shard_map/mixer/pallas_call | solution.py:114
  46.1 0.1 collective-permute-start.10
  46.2 0.2 token_grad_message.1.grad_x
  46.4 2.0 %collective-permute-done.10.got = bf16[2,8,176,128]{3,2,1,0:T(8,128)(2,1)S(1)} collective-permute-done((bf16[2,8,176,128]{3,2,1,0:T(8,128)(2,1)S(1)}, bf16[2,8,176,128]{3,2,1,0:T(8,128)(2,1)S(1)}, u32[]{:S(2)}, u32[]{:S(2)}) %collective-permute-start.10) | collective-permute-done | bytes 720928 | tf_op jit(solution)/shard_map/ppermute | solution.py:663
  48.4 0.9 add_cores.1
  49.3 4.4 %all-to-all-start.1 = ((bf16[16,128,128]{2,1,0:T(8,128)(2,1)}), bf16[16,128,128]{2,1,0:T(8,128)(2,1)S(1)}, u32[]{:S(2)}, u32[]{:S(2)}) async-start(bf16[16,128,128]{2,1,0:T(8,128)(2,1)} %get-tuple-element.95), calls=%async_computation.1 | async-start | bytes 1048576 | tf_op jit(solution)/shard_map/all_to_all | solution.py:649
  53.7 1.9 %collective-permute-start.11 = (bf16[4,144,128]{2,1,0:T(8,128)(2,1)S(1)}, bf16[4,144,128]{2,1,0:T(8,128)(2,1)S(1)}, u32[]{:S(2)}, u32[]{:S(2)}) collective-permute-start(bf16[4,144,128]{2,1,0:T(8,128)(2,1)S(1)} %get-tuple-element.88), channel_id=1, source_target_pairs={{0,1},{1,0},{2,3},{3,2},{4,5},{5,4},{6,7},{7,6},{8,9},{9,8},{10,11... | collective-permute-start | bytes 442376 | tf_op jit(solution)/shard_map/ppermute | solution.py:821
  55.6 1.5 %collective-permute-start.12 = (bf16[4,144,128]{2,1,0:T(8,128)(2,1)S(1)}, bf16[4,144,128]{2,1,0:T(8,128)(2,1)S(1)}, u32[]{:S(2)}, u32[]{:S(2)}) collective-permute-start(bf16[4,144,128]{2,1,0:T(8,128)(2,1)S(1)} %get-tuple-element.89), channel_id=1, source_target_pairs={{0,16},{1,17},{2,18},{3,19},{4,20},{5,21},{6,22},{7,23},{8,24},{9,... | collective-permute-start | bytes 442376 | tf_op jit(solution)/shard_map/ppermute | solution.py:821
  57.1 0.2 collective-permute-start.13
  57.3 5.0 %collective-permute-done.11.refs_1_ = bf16[4,144,128]{2,1,0:T(8,128)(2,1)S(1)} collective-permute-done((bf16[4,144,128]{2,1,0:T(8,128)(2,1)S(1)}, bf16[4,144,128]{2,1,0:T(8,128)(2,1)S(1)}, u32[]{:S(2)}, u32[]{:S(2)}) %collective-permute-start.11) | collective-permute-done | bytes 147488 | tf_op jit(solution)/shard_map/ppermute | solution.py:821
  62.3 2.6 %collective-permute-done.12.refs_2_ = bf16[4,144,128]{2,1,0:T(8,128)(2,1)S(1)} collective-permute-done((bf16[4,144,128]{2,1,0:T(8,128)(2,1)S(1)}, bf16[4,144,128]{2,1,0:T(8,128)(2,1)S(1)}, u32[]{:S(2)}, u32[]{:S(2)}) %collective-permute-start.12) | collective-permute-done | bytes 147488 | tf_op jit(solution)/shard_map/ppermute | solution.py:821
  64.9 4.6 %collective-permute-done.13.refs_3_ = bf16[4,144,128]{2,1,0:T(8,128)(2,1)S(1)} collective-permute-done((bf16[4,144,128]{2,1,0:T(8,128)(2,1)S(1)}, bf16[4,144,128]{2,1,0:T(8,128)(2,1)S(1)}, u32[]{:S(2)}, u32[]{:S(2)}) %collective-permute-start.13) | collective-permute-done | bytes 147488 | tf_op jit(solution)/shard_map/ppermute | solution.py:821
  69.4 0.1 add_fold.1
  69.6 0.0 all-to-all-done.1.got
  69.6 0.1 collective-permute-start.19
  69.7 0.9 %collective-permute-start.18 = (bf16[16,32,128]{2,1,0:T(8,128)(2,1)S(1)}, bf16[16,32,128]{2,1,0:T(8,128)(2,1)S(1)}, u32[]{:S(2)}, u32[]{:S(2)}) collective-permute-start(bf16[16,32,128]{2,1,0:T(8,128)(2,1)S(1)} %filter_rows.1.refs_0_), channel_id=1, source_target_pairs={{0,8},{8,0},{16,24},{24,16},{1,9},{9,1},{17,25},{25,17},{2,10},{10... | collective-permute-start | bytes 393224 | tf_op jit(solution)/shard_map/ppermute | solution.py:673
  70.6 1.2 %collective-permute-start.17 = (bf16[16,32,128]{2,1,0:T(8,128)(2,1)S(1)}, bf16[16,32,128]{2,1,0:T(8,128)(2,1)S(1)}, u32[]{:S(2)}, u32[]{:S(2)}) collective-permute-start(bf16[16,32,128]{2,1,0:T(8,128)(2,1)S(1)} %filter_rows.1.refs_0_), channel_id=1, source_target_pairs={{0,16},{8,24},{16,0},{24,8},{1,17},{9,25},{17,1},{25,9},{2,18},{10... | collective-permute-start | bytes 393224 | tf_op jit(solution)/shard_map/ppermute | solution.py:673
  71.8 1.8 %collective-permute-start.14 = (bf16[144,128]{1,0:T(8,128)(2,1)S(1)}, bf16[144,128]{1,0:T(8,128)(2,1)S(1)}, u32[]{:S(2)}, u32[]{:S(2)}) collective-permute-start(bf16[144,128]{1,0:T(8,128)(2,1)S(1)} %get-tuple-element.97), channel_id=1, source_target_pairs={{0,2},{1,3},{2,0},{3,1},{4,6},{5,7},{6,4},{7,5},{8,10},{9,11},{10,... | collective-permute-start | bytes 110600 | tf_op jit(solution)/shard_map/ppermute | solution.py:659
  73.6 1.7 %collective-permute-start.15 = (bf16[144,128]{1,0:T(8,128)(2,1)S(1)}, bf16[144,128]{1,0:T(8,128)(2,1)S(1)}, u32[]{:S(2)}, u32[]{:S(2)}) collective-permute-start(bf16[144,128]{1,0:T(8,128)(2,1)S(1)} %get-tuple-element.98), channel_id=1, source_target_pairs={{0,4},{1,5},{2,6},{3,7},{4,0},{5,1},{6,2},{7,3},{8,12},{9,13},{10,... | collective-permute-start | bytes 110600 | tf_op jit(solution)/shard_map/ppermute | solution.py:659
  75.3 0.1 collective-permute-done.19.refs_3_
  75.4 2.9 %collective-permute-start.16 = (bf16[144,128]{1,0:T(8,128)(2,1)S(1)}, bf16[144,128]{1,0:T(8,128)(2,1)S(1)}, u32[]{:S(2)}, u32[]{:S(2)}) collective-permute-start(bf16[144,128]{1,0:T(8,128)(2,1)S(1)} %get-tuple-element.99), channel_id=1, source_target_pairs={{0,6},{1,7},{2,4},{3,5},{4,2},{5,3},{6,0},{7,1},{8,14},{9,15},{10,... | collective-permute-start | bytes 110600 | tf_op jit(solution)/shard_map/ppermute | solution.py:659
  78.3 0.9 %token_grad.1 = bf16[128,1536]{1,0:T(8,128)(2,1)} custom-call(bf16[16,128,128]{2,1,0:T(8,128)(2,1)S(1)} %all-to-all-done.1.got), custom_call_target="tpu_custom_call" | custom-call | tf_op jit(solution)/shard_map/token_grad/pallas_call | solution.py:114
  79.2 0.0 collective-permute-done.18.refs_2_
  79.2 0.0 collective-permute-done.17.refs_1_
  79.2 1.2 %finish_filter.1 = (bf16[128,1536]{1,0:T(8,128)(2,1)}, f32[3,1536]{1,0:T(4,128)}, f32[3,1536]{1,0:T(4,128)}) custom-call(bf16[16,32,128]{2,1,0:T(8,128)(2,1)S(1)} %filter_rows.1.refs_0_, bf16[16,32,128]{2,1,0:T(8,128)(2,1)S(1)} %collective-permute-done.17.refs_1_, bf16[16,32,128]{2,1,0:T(8,128)(2,1)S(1)} %collective-permute-done.18.refs_2_, ...), custom_call_target="tpu_custom_call" | custom-call | tf_op jit(solution)/shard_map/finish_filter/pallas_call | solution.py:114
  80.5 0.0 collective-permute-done.14.refs_1_
  80.5 0.0 collective-permute-done.15.refs_2_
  80.5 0.7 collective-permute-done.16.refs_3_
  81.2 0.1 collective-permute-start.22
  81.2 1.0 %collective-permute-start.21 = (bf16[144,128]{1,0:T(8,128)(2,1)S(1)}, bf16[144,128]{1,0:T(8,128)(2,1)S(1)}, u32[]{:S(2)}, u32[]{:S(2)}) collective-permute-start(bf16[144,128]{1,0:T(8,128)(2,1)S(1)} %sum_sources.1.refs_0_), channel_id=1, source_target_pairs={{0,8},{8,0},{16,24},{24,16},{1,9},{9,1},{17,25},{25,17},{2,10},{10... | collective-permute-start | bytes 110600 | tf_op jit(solution)/shard_map/ppermute | solution.py:673
  82.3 1.1 %collective-permute-start.20 = (bf16[144,128]{1,0:T(8,128)(2,1)S(1)}, bf16[144,128]{1,0:T(8,128)(2,1)S(1)}, u32[]{:S(2)}, u32[]{:S(2)}) collective-permute-start(bf16[144,128]{1,0:T(8,128)(2,1)S(1)} %sum_sources.1.refs_0_), channel_id=1, source_target_pairs={{0,16},{8,24},{16,0},{24,8},{1,17},{9,25},{17,1},{25,9},{2,18},{10... | collective-permute-start | bytes 110600 | tf_op jit(solution)/shard_map/ppermute | solution.py:673
  83.4 1.2 %collective-permute-done.22.refs_3_ = bf16[144,128]{1,0:T(8,128)(2,1)S(1)} collective-permute-done((bf16[144,128]{1,0:T(8,128)(2,1)S(1)}, bf16[144,128]{1,0:T(8,128)(2,1)S(1)}, u32[]{:S(2)}, u32[]{:S(2)}) %collective-permute-start.22) | collective-permute-done | bytes 36896 | tf_op jit(solution)/shard_map/ppermute | solution.py:673
  84.6 1.6 %collective-permute-done.20.refs_1_ = bf16[144,128]{1,0:T(8,128)(2,1)S(1)} collective-permute-done((bf16[144,128]{1,0:T(8,128)(2,1)S(1)}, bf16[144,128]{1,0:T(8,128)(2,1)S(1)}, u32[]{:S(2)}, u32[]{:S(2)}) %collective-permute-start.20) | collective-permute-done | bytes 36896 | tf_op jit(solution)/shard_map/ppermute | solution.py:673
  86.2 0.7 finish_factors.1
  (13 shorter events, 0.1 us)
Async XLA Ops:
  0.6 7.6 %copy-start = (bf16[1,128,1536]{2,1,0:T(8,128)(2,1)S(1)}, bf16[1,128,1536]{2,1,0:T(8,128)(2,1)}, u32[]{:S(2)}) copy-start(bf16[1,128,1536]{2,1,0:T(8,128)(2,1)} %param.9) | copy-start | bytes 1179652
  2.5 7.8 %collective-permute-start = (bf16[240,128]{1,0:T(8,128)(2,1)}, bf16[240,128]{1,0:T(8,128)(2,1)S(1)}, u32[]{:S(2)}, u32[]{:S(2)}) collective-permute-start(bf16[240,128]{1,0:T(8,128)(2,1)} %get-tuple-element.63), channel_id=1, source_target_pairs={{0,2},{1,3},{2,0},{3,1},{4,6},{5,7},{6,4},{7,5},{8,10},{9,11},{10,... | collective-permute-start | bytes 184328 | tf_op jit(solution)/shard_map/ppermute | solution.py:659
  5.6 6.6 %collective-permute-start.1 = (bf16[240,128]{1,0:T(8,128)(2,1)}, bf16[240,128]{1,0:T(8,128)(2,1)S(1)}, u32[]{:S(2)}, u32[]{:S(2)}) collective-permute-start(bf16[240,128]{1,0:T(8,128)(2,1)} %get-tuple-element.64), channel_id=1, source_target_pairs={{0,4},{1,5},{2,6},{3,7},{4,0},{5,1},{6,2},{7,3},{8,12},{9,13},{10,... | collective-permute-start | bytes 184328 | tf_op jit(solution)/shard_map/ppermute | solution.py:659
  8.2 6.2 %collective-permute-start.2 = (bf16[240,128]{1,0:T(8,128)(2,1)}, bf16[240,128]{1,0:T(8,128)(2,1)S(1)}, u32[]{:S(2)}, u32[]{:S(2)}) collective-permute-start(bf16[240,128]{1,0:T(8,128)(2,1)} %get-tuple-element.65), channel_id=1, source_target_pairs={{0,6},{1,7},{2,4},{3,5},{4,2},{5,3},{6,0},{7,1},{8,14},{9,15},{10,... | collective-permute-start | bytes 184328 | tf_op jit(solution)/shard_map/ppermute | solution.py:659
  8.2 1.0 %copy-start.1 = (bf16[1,128,1536]{2,1,0:T(8,128)(2,1)S(1)}, bf16[1,128,1536]{2,1,0:T(8,128)(2,1)}, u32[]{:S(2)}) copy-start(bf16[1,128,1536]{2,1,0:T(8,128)(2,1)} %param.10) | copy-start | bytes 1179652
  14.4 4.9 %copy-start.2 = (bf16[240,128]{1,0:T(8,128)(2,1)S(1)}, bf16[240,128]{1,0:T(8,128)(2,1)}, u32[]{:S(2)}) copy-start(bf16[240,128]{1,0:T(8,128)(2,1)} %get-tuple-element.62.refs_0_) | copy-start | bytes 184324
  14.4 24.0 %all-to-all-start = ((bf16[16,192,128]{2,1,0:T(8,128)(2,1)}), bf16[16,192,128]{2,1,0:T(8,128)(2,1)S(1)}, u32[]{:S(2)}, u32[]{:S(2)}) async-start(bf16[16,192,128]{2,1,0:T(8,128)(2,1)} %token_message.1), calls=%async_computation | async-start | bytes 1572864 | tf_op jit(solution)/shard_map/all_to_all | solution.py:649
  19.4 15.0 %collective-permute-start.3 = (bf16[4,192,128]{2,1,0:T(8,128)(2,1)S(1)}, bf16[4,192,128]{2,1,0:T(8,128)(2,1)S(1)}, u32[]{:S(2)}, u32[]{:S(2)}) collective-permute-start(bf16[4,192,128]{2,1,0:T(8,128)(2,1)S(1)} %get-tuple-element.67), channel_id=1, source_target_pairs={{0,1},{1,0},{2,3},{3,2},{4,5},{5,4},{6,7},{7,6},{8,9},{9,8},{10,11... | collective-permute-start | bytes 589832 | tf_op jit(solution)/shard_map/ppermute | solution.py:714
  21.4 10.6 %collective-permute-start.5 = (bf16[4,144,128]{2,1,0:T(8,128)(2,1)S(1)}, bf16[4,144,128]{2,1,0:T(8,128)(2,1)S(1)}, u32[]{:S(2)}, u32[]{:S(2)}) collective-permute-start(bf16[4,144,128]{2,1,0:T(8,128)(2,1)S(1)} %slice.4), channel_id=1, source_target_pairs={{0,17},{1,16},{2,19},{3,18},{4,21},{5,20},{6,23},{7,22},{8,25},{9,... | collective-permute-start | bytes 442376 | tf_op jit(solution)/shard_map/ppermute | solution.py:714
  23.0 10.9 %collective-permute-start.4 = (bf16[4,144,128]{2,1,0:T(8,128)(2,1)S(1)}, bf16[4,144,128]{2,1,0:T(8,128)(2,1)S(1)}, u32[]{:S(2)}, u32[]{:S(2)}) collective-permute-start(bf16[4,144,128]{2,1,0:T(8,128)(2,1)S(1)} %slice.4), channel_id=1, source_target_pairs={{0,16},{1,17},{2,18},{3,19},{4,20},{5,21},{6,22},{7,23},{8,24},{9,... | collective-permute-start | bytes 442376 | tf_op jit(solution)/shard_map/ppermute | solution.py:714
  23.1 11.3 %copy-start.4 = (f32[3,1536]{1,0:T(4,128)S(1)}, f32[3,1536]{1,0:T(4,128)}, u32[]{:S(2)}) copy-start(f32[3,1536]{1,0:T(4,128)} %param.12) | copy-start | bytes 55300
  23.1 11.3 %copy-start.3 = (f32[3,1536]{1,0:T(4,128)S(1)}, f32[3,1536]{1,0:T(4,128)}, u32[]{:S(2)}) copy-start(f32[3,1536]{1,0:T(4,128)} %param.11) | copy-start | bytes 55300
  23.1 11.5 %collective-permute-start.6 = (bf16[4,192,128]{2,1,0:T(8,128)(2,1)S(1)}, bf16[4,192,128]{2,1,0:T(8,128)(2,1)S(1)}, u32[]{:S(2)}, u32[]{:S(2)}) collective-permute-start(bf16[4,192,128]{2,1,0:T(8,128)(2,1)S(1)} %get-tuple-element.70.refs_0_), channel_id=1, source_target_pairs={{0,8},{8,0},{16,24},{24,16},{1,9},{9,1},{17,25},{25,17},{2,10},{10... | collective-permute-start | bytes 589832 | tf_op jit(solution)/shard_map/ppermute | solution.py:663
  32.1 2.5 %collective-permute-start.9 = (bf16[4,144,128]{2,1,0:T(8,128)(2,1)S(1)}, bf16[4,144,128]{2,1,0:T(8,128)(2,1)S(1)}, u32[]{:S(2)}, u32[]{:S(2)}) collective-permute-start(bf16[4,144,128]{2,1,0:T(8,128)(2,1)S(1)} %collective-permute-done.5.refs_3_), channel_id=1, source_target_pairs={{0,8},{8,0},{16,24},{24,16},{1,9},{9,1},{17,25},{25,17},{2,10},{10... | collective-permute-start | bytes 442376 | tf_op jit(solution)/shard_map/ppermute | solution.py:663
  33.9 1.4 %collective-permute-start.8 = (bf16[4,144,128]{2,1,0:T(8,128)(2,1)S(1)}, bf16[4,144,128]{2,1,0:T(8,128)(2,1)S(1)}, u32[]{:S(2)}, u32[]{:S(2)}) collective-permute-start(bf16[4,144,128]{2,1,0:T(8,128)(2,1)S(1)} %collective-permute-done.4.refs_2_), channel_id=1, source_target_pairs={{0,8},{8,0},{16,24},{24,16},{1,9},{9,1},{17,25},{25,17},{2,10},{10... | collective-permute-start | bytes 442376 | tf_op jit(solution)/shard_map/ppermute | solution.py:663
  34.4 1.4 %collective-permute-start.7 = (bf16[4,192,128]{2,1,0:T(8,128)(2,1)S(1)}, bf16[4,192,128]{2,1,0:T(8,128)(2,1)S(1)}, u32[]{:S(2)}, u32[]{:S(2)}) collective-permute-start(bf16[4,192,128]{2,1,0:T(8,128)(2,1)S(1)} %collective-permute-done.3.refs_1_), channel_id=1, source_target_pairs={{0,8},{8,0},{16,24},{24,16},{1,9},{9,1},{17,25},{25,17},{2,10},{10... | collective-permute-start | bytes 589832 | tf_op jit(solution)/shard_map/ppermute | solution.py:663
  46.1 2.3 %collective-permute-start.10 = (bf16[2,8,176,128]{3,2,1,0:T(8,128)(2,1)S(1)}, bf16[2,8,176,128]{3,2,1,0:T(8,128)(2,1)S(1)}, u32[]{:S(2)}, u32[]{:S(2)}) collective-permute-start(bf16[2,8,176,128]{3,2,1,0:T(8,128)(2,1)S(1)} %get-tuple-element.86), channel_id=1, source_target_pairs={{0,8},{8,0},{16,24},{24,16},{1,9},{9,1},{17,25},{25,17},{2,10},{10... | collective-permute-start | bytes 2162696 | tf_op jit(solution)/shard_map/ppermute | solution.py:663
  49.3 20.3 %all-to-all-start.1 = ((bf16[16,128,128]{2,1,0:T(8,128)(2,1)}), bf16[16,128,128]{2,1,0:T(8,128)(2,1)S(1)}, u32[]{:S(2)}, u32[]{:S(2)}) async-start(bf16[16,128,128]{2,1,0:T(8,128)(2,1)} %get-tuple-element.95), calls=%async_computation.1 | async-start | bytes 1048576 | tf_op jit(solution)/shard_map/all_to_all | solution.py:649
  53.7 8.6 %collective-permute-start.11 = (bf16[4,144,128]{2,1,0:T(8,128)(2,1)S(1)}, bf16[4,144,128]{2,1,0:T(8,128)(2,1)S(1)}, u32[]{:S(2)}, u32[]{:S(2)}) collective-permute-start(bf16[4,144,128]{2,1,0:T(8,128)(2,1)S(1)} %get-tuple-element.88), channel_id=1, source_target_pairs={{0,1},{1,0},{2,3},{3,2},{4,5},{5,4},{6,7},{7,6},{8,9},{9,8},{10,11... | collective-permute-start | bytes 442376 | tf_op jit(solution)/shard_map/ppermute | solution.py:821
  55.6 9.2 %collective-permute-start.12 = (bf16[4,144,128]{2,1,0:T(8,128)(2,1)S(1)}, bf16[4,144,128]{2,1,0:T(8,128)(2,1)S(1)}, u32[]{:S(2)}, u32[]{:S(2)}) collective-permute-start(bf16[4,144,128]{2,1,0:T(8,128)(2,1)S(1)} %get-tuple-element.89), channel_id=1, source_target_pairs={{0,16},{1,17},{2,18},{3,19},{4,20},{5,21},{6,22},{7,23},{8,24},{9,... | collective-permute-start | bytes 442376 | tf_op jit(solution)/shard_map/ppermute | solution.py:821
  57.1 12.3 %collective-permute-start.13 = (bf16[4,144,128]{2,1,0:T(8,128)(2,1)S(1)}, bf16[4,144,128]{2,1,0:T(8,128)(2,1)S(1)}, u32[]{:S(2)}, u32[]{:S(2)}) collective-permute-start(bf16[4,144,128]{2,1,0:T(8,128)(2,1)S(1)} %get-tuple-element.90), channel_id=1, source_target_pairs={{0,17},{1,16},{2,19},{3,18},{4,21},{5,20},{6,23},{7,22},{8,25},{9,... | collective-permute-start | bytes 442376 | tf_op jit(solution)/shard_map/ppermute | solution.py:821
  69.6 5.8 %collective-permute-start.19 = (bf16[16,32,128]{2,1,0:T(8,128)(2,1)S(1)}, bf16[16,32,128]{2,1,0:T(8,128)(2,1)S(1)}, u32[]{:S(2)}, u32[]{:S(2)}) collective-permute-start(bf16[16,32,128]{2,1,0:T(8,128)(2,1)S(1)} %filter_rows.1.refs_0_), channel_id=1, source_target_pairs={{0,24},{8,16},{16,8},{24,0},{1,25},{9,17},{17,9},{25,1},{2,26},{10... | collective-permute-start | bytes 393224 | tf_op jit(solution)/shard_map/ppermute | solution.py:673
  69.7 9.6 %collective-permute-start.18 = (bf16[16,32,128]{2,1,0:T(8,128)(2,1)S(1)}, bf16[16,32,128]{2,1,0:T(8,128)(2,1)S(1)}, u32[]{:S(2)}, u32[]{:S(2)}) collective-permute-start(bf16[16,32,128]{2,1,0:T(8,128)(2,1)S(1)} %filter_rows.1.refs_0_), channel_id=1, source_target_pairs={{0,8},{8,0},{16,24},{24,16},{1,9},{9,1},{17,25},{25,17},{2,10},{10... | collective-permute-start | bytes 393224 | tf_op jit(solution)/shard_map/ppermute | solution.py:673
  70.6 8.6 %collective-permute-start.17 = (bf16[16,32,128]{2,1,0:T(8,128)(2,1)S(1)}, bf16[16,32,128]{2,1,0:T(8,128)(2,1)S(1)}, u32[]{:S(2)}, u32[]{:S(2)}) collective-permute-start(bf16[16,32,128]{2,1,0:T(8,128)(2,1)S(1)} %filter_rows.1.refs_0_), channel_id=1, source_target_pairs={{0,16},{8,24},{16,0},{24,8},{1,17},{9,25},{17,1},{25,9},{2,18},{10... | collective-permute-start | bytes 393224 | tf_op jit(solution)/shard_map/ppermute | solution.py:673
  71.8 8.7 %collective-permute-start.14 = (bf16[144,128]{1,0:T(8,128)(2,1)S(1)}, bf16[144,128]{1,0:T(8,128)(2,1)S(1)}, u32[]{:S(2)}, u32[]{:S(2)}) collective-permute-start(bf16[144,128]{1,0:T(8,128)(2,1)S(1)} %get-tuple-element.97), channel_id=1, source_target_pairs={{0,2},{1,3},{2,0},{3,1},{4,6},{5,7},{6,4},{7,5},{8,10},{9,11},{10,... | collective-permute-start | bytes 110600 | tf_op jit(solution)/shard_map/ppermute | solution.py:659
  73.6 6.8 %collective-permute-start.15 = (bf16[144,128]{1,0:T(8,128)(2,1)S(1)}, bf16[144,128]{1,0:T(8,128)(2,1)S(1)}, u32[]{:S(2)}, u32[]{:S(2)}) collective-permute-start(bf16[144,128]{1,0:T(8,128)(2,1)S(1)} %get-tuple-element.98), channel_id=1, source_target_pairs={{0,4},{1,5},{2,6},{3,7},{4,0},{5,1},{6,2},{7,3},{8,12},{9,13},{10,... | collective-permute-start | bytes 110600 | tf_op jit(solution)/shard_map/ppermute | solution.py:659
  75.4 5.8 %collective-permute-start.16 = (bf16[144,128]{1,0:T(8,128)(2,1)S(1)}, bf16[144,128]{1,0:T(8,128)(2,1)S(1)}, u32[]{:S(2)}, u32[]{:S(2)}) collective-permute-start(bf16[144,128]{1,0:T(8,128)(2,1)S(1)} %get-tuple-element.99), channel_id=1, source_target_pairs={{0,6},{1,7},{2,4},{3,5},{4,2},{5,3},{6,0},{7,1},{8,14},{9,15},{10,... | collective-permute-start | bytes 110600 | tf_op jit(solution)/shard_map/ppermute | solution.py:659
  81.2 3.4 %collective-permute-start.22 = (bf16[144,128]{1,0:T(8,128)(2,1)S(1)}, bf16[144,128]{1,0:T(8,128)(2,1)S(1)}, u32[]{:S(2)}, u32[]{:S(2)}) collective-permute-start(bf16[144,128]{1,0:T(8,128)(2,1)S(1)} %sum_sources.1.refs_0_), channel_id=1, source_target_pairs={{0,24},{8,16},{16,8},{24,0},{1,25},{9,17},{17,9},{25,1},{2,26},{10... | collective-permute-start | bytes 110600 | tf_op jit(solution)/shard_map/ppermute | solution.py:673
  81.2 3.4 %collective-permute-start.21 = (bf16[144,128]{1,0:T(8,128)(2,1)S(1)}, bf16[144,128]{1,0:T(8,128)(2,1)S(1)}, u32[]{:S(2)}, u32[]{:S(2)}) collective-permute-start(bf16[144,128]{1,0:T(8,128)(2,1)S(1)} %sum_sources.1.refs_0_), channel_id=1, source_target_pairs={{0,8},{8,0},{16,24},{24,16},{1,9},{9,1},{17,25},{25,17},{2,10},{10... | collective-permute-start | bytes 110600 | tf_op jit(solution)/shard_map/ppermute | solution.py:673
  82.3 4.0 %collective-permute-start.20 = (bf16[144,128]{1,0:T(8,128)(2,1)S(1)}, bf16[144,128]{1,0:T(8,128)(2,1)S(1)}, u32[]{:S(2)}, u32[]{:S(2)}) collective-permute-start(bf16[144,128]{1,0:T(8,128)(2,1)S(1)} %sum_sources.1.refs_0_), channel_id=1, source_target_pairs={{0,16},{8,24},{16,0},{24,8},{1,17},{9,25},{17,1},{25,9},{2,18},{10... | collective-permute-start | bytes 110600 | tf_op jit(solution)/shard_map/ppermute | solution.py:673
